TPU v7x, 128 devices: a whole 4x4x4 slice. The times are simulated.
128 devices in a mesh: scen: 8 (over x, core), vec: 16 (over z, y).
Axes of the slice: x: 4, y: 4, z: 4, core: 2. Of those that a mesh axis runs over, the one named last changes fastest.
Arguments:
- rhs: float32 [1536, 128], P('vec'), may hold values from -6 to 6
- diag_cost: float32 [1536, 128], P('vec'), may hold values from 1 to 10
- couple: bfloat16 [128, 24, 128, 128], P(('scen', 'vec')), may hold values from -0.5 to 0.5
- couple_idx: int32 [128, 24], P(('scen', 'vec')), may hold values from 0 to 1535
- factor: bfloat16 [128, 24, 3, 128, 128], P(('scen', 'vec')), may hold values from -0.3125 to 0.3125
- pattern: int32 [128, 24, 2], P(('scen', 'vec')), may hold values 0 or 1
Outputs:
- solution: float32 [1536, 128], P('vec')
- residual: float32 [1536, 128], P('vec')
Inputs may be any that keep to these rules, and one draw needn't show every extreme that they name: `couple_idx`: a first-section block index.
All inputs are finite; a program needn't handle non-finite values. No bound on the sum of `pattern` on one device may be relied on, other than what follows from the above.
Results may differ from a plain program's by a relative error of at most 0.017.
Values may be sent and summed in bfloat16 or wider, within the bound.
No kernel may reach another device: no remote copies, remote signals or barrier semaphores. Data moves between devices by JAX's collectives and lax.ppermute only.
A program may use at most 64 MiB of HBM per device.

v0:
```python
import jax
import jax.numpy as jnp
from jax import lax
from jax.sharding import PartitionSpec as P

ITERS = 3


def scenario_lift(full16, couple, couple_idx, factor, pattern):
    row_blocks = couple.shape[1]
    width = couple.shape[2]
    fetched = full16[couple_idx]
    coupled = jnp.einsum(
        "srij,srj->sri", couple, fetched, preferred_element_type=jnp.float32
    ).astype(jnp.bfloat16)
    places = lax.broadcasted_iota(jnp.int32, pattern.shape[:2], 1)
    left_side = pattern[:, :, 0] * (places > 0).astype(jnp.int32)
    right_side = pattern[:, :, 1] * (places < row_blocks - 1).astype(jnp.int32)
    reach = jnp.stack([left_side, jnp.ones_like(left_side), right_side], axis=2).astype(
        jnp.bfloat16
    )
    zero_row = jnp.zeros((couple.shape[0], 1, width), jnp.bfloat16)
    padded = jnp.concatenate([zero_row, coupled, zero_row], axis=1)
    stacked = (
        jnp.stack([padded[:, :-2], padded[:, 1:-1], padded[:, 2:]], axis=2) * reach[:, :, :, None]
    )
    weighted = jnp.einsum(
        "srkij,srkj->sri", factor, stacked, preferred_element_type=jnp.float32
    ).astype(jnp.bfloat16)
    spread_back = jnp.einsum(
        "srkij,sri->srkj", factor, weighted, preferred_element_type=jnp.float32
    ) * reach[:, :, :, None].astype(jnp.float32)
    zero_f = jnp.zeros((couple.shape[0], 1, width), jnp.float32)
    returned = (
        spread_back[:, :, 1]
        + jnp.concatenate([spread_back[:, 1:, 0], zero_f], axis=1)
        + jnp.concatenate([zero_f, spread_back[:, :-1, 2]], axis=1)
    )
    returned = returned.astype(jnp.bfloat16)
    return jnp.einsum("srij,sri->srj", couple, returned, preferred_element_type=jnp.float32)


def inner_sums(values):
    return lax.psum((values[0],), "vec")


def collect_rows(lifted, block_index, row_count):
    targets = lax.iota(jnp.int32, row_count)
    onehot = (block_index[:, :, None] == targets[None, None, :]).astype(jnp.float32)
    return jnp.einsum("srf,srj->fj", onehot, lifted, precision=lax.Precision.HIGHEST)


def shards(rhs, diag_cost, couple, couple_idx, factor, pattern):
    inverse = 1.0 / diag_cost
    solution = jnp.zeros_like(rhs)
    residual = rhs
    precond = inverse * residual
    direction = precond
    rz_now = inner_sums((jnp.sum(residual * precond),))[0]
    for iteration in range(ITERS):
        share16 = direction.astype(jnp.bfloat16)
        full16 = lax.all_gather(share16, "vec", axis=0, tiled=True)
        lifted = scenario_lift(full16, couple, couple_idx, factor, pattern)
        owned = full16.shape[0] // lax.axis_size("vec")
        summed = lax.psum_scatter(
            collect_rows(lifted, couple_idx, lax.axis_size("vec") * owned),
            "vec",
            scatter_dimension=0,
            tiled=True,
        )
        summed = lax.psum(summed, "scen")
        image = diag_cost * direction + summed
        curvature = inner_sums((jnp.sum(direction * image),))[0]
        step_size = rz_now / curvature
        solution = solution + step_size * direction
        residual = residual - step_size * image
        precond = inverse * residual
        rz_next = inner_sums((jnp.sum(residual * precond),))[0]
        direction = precond + rz_next / rz_now * direction
        rz_now = rz_next
    return (solution, residual)


def solution(mesh):
    in_specs = (
        P("vec", None),
        P("vec", None),
        P(("scen", "vec"), None, None, None),
        P(("scen", "vec"), None),
        P(("scen", "vec"), None, None, None, None),
        P(("scen", "vec"), None, None),
    )
    out_specs = (P("vec", None), P("vec", None))
    return jax.shard_map(shards, mesh=mesh, in_specs=in_specs, out_specs=out_specs, check_vma=False)
```

profile of v0, /device:TPU:1, one launch (start us, length us, event | category | flops | bytes accessed | tf_op | source)
XLA Modules:
  0.0 584.5 jit_solution(2080751749812435733)
XLA Ops:
  9.1 0.8 fusion.82
  9.9 21.1 %all_gather.9 = bf16[1536,128]{1,0:T(8,128)(2,1)S(1)} all-gather(bf16[96,128]{1,0:T(8,128)(2,1)S(1)} %fusion.82), channel_id=1, replica_groups=mesh['scen'=8,'vec'=16] {'vec'}, dimensions={0}, use_global_device_ids=true | all-gather | bytes 417792 | tf_op jit(solution)/shard_map/all_gather | solution.py:62
  31.5 1.6 fusion.22
  33.3 0.9 fusion.10
  35.2 1.8 fusion.26
  37.1 75.8 %reduce-scatter.4.cloned.1.call-done = f32[96,128]{1,0:T(8,128)} async-done(((f32[1536,128]{1,0:T(8,128)}), f32[96,128]{1,0:T(8,128)}) %reduce-scatter.4.cloned.1.call-update) | async-done | bytes 49168 | tf_op jit(solution)/shard_map/reduce_scatter | solution.py:65
  112.8 23.7 %psum.64 = f32[96,128]{1,0:T(8,128)S(1)} all-reduce(f32[96,128]{1,0:T(8,128)} %reduce-scatter.4.cloned.1.call-done), channel_id=1, replica_groups=mesh['scen'=8,'vec'=16] {'scen'}, use_global_device_ids=true, to_apply=%region_3.0 | all-reduce | flops 12288 | bytes 98304 | tf_op jit(solution)/shard_map/psum | solution.py:71
  137.1 31.7 %all-reduce.12 = (f32[]{:T(128)}, f32[]{:T(128)}) all-reduce(f32[]{:T(128)} %get-tuple-element.3, f32[]{:T(128)} %get-tuple-element.2), channel_id=1, replica_groups=mesh['scen'=8,'vec'=16] {'vec'}, use_global_device_ids=true, to_apply=%region_1.0 | all-reduce | flops 2 | bytes 16 | tf_op jit(solution)/shard_map/psum | solution.py:44
  170.7 29.3 %psum.66 = f32[]{:T(128)} all-reduce(f32[]{:T(128)} %multiply_reduce_fusion.3), channel_id=1, replica_groups=mesh['scen'=8,'vec'=16] {'vec'}, use_global_device_ids=true, to_apply=%region_7.0 | all-reduce | flops 1 | bytes 8 | tf_op jit(solution)/shard_map/psum | solution.py:44
  201.4 19.6 %all_gather.10 = bf16[1536,128]{1,0:T(8,128)(2,1)} all-gather(bf16[96,128]{1,0:T(8,128)(2,1)S(1)} %fusion.81), channel_id=1, replica_groups=mesh['scen'=8,'vec'=16] {'vec'}, dimensions={0}, use_global_device_ids=true | all-gather | bytes 417792 | tf_op jit(solution)/shard_map/all_gather | solution.py:62
  221.0 1.6 gather_fusion.1
  223.2 0.9 fusion.6
  225.1 1.8 fusion.25
  227.0 89.4 %reduce-scatter.6.cloned.1.call-done = f32[96,128]{1,0:T(8,128)} async-done(((f32[1536,128]{1,0:T(8,128)}), f32[96,128]{1,0:T(8,128)}) %reduce-scatter.6.cloned.1.call-update) | async-done | bytes 49168 | tf_op jit(solution)/shard_map/reduce_scatter | solution.py:65
  316.4 23.7 %psum.67 = f32[96,128]{1,0:T(8,128)S(1)} all-reduce(f32[96,128]{1,0:T(8,128)} %reduce-scatter.6.cloned.1.call-done), channel_id=1, replica_groups=mesh['scen'=8,'vec'=16] {'scen'}, use_global_device_ids=true, to_apply=%region_9.0 | all-reduce | flops 12288 | bytes 98304 | tf_op jit(solution)/shard_map/psum | solution.py:71
  340.7 31.7 %psum.68 = f32[]{:T(128)} all-reduce(f32[]{:T(128)} %multiply_reduce_fusion.2), channel_id=1, replica_groups=mesh['scen'=8,'vec'=16] {'vec'}, use_global_device_ids=true, to_apply=%region_11.0 | all-reduce | flops 1 | bytes 8 | tf_op jit(solution)/shard_map/psum | solution.py:44
  374.4 29.3 %psum.69 = f32[]{:T(128)} all-reduce(f32[]{:T(128)} %multiply_reduce_fusion.1), channel_id=1, replica_groups=mesh['scen'=8,'vec'=16] {'vec'}, use_global_device_ids=true, to_apply=%region_13.0 | all-reduce | flops 1 | bytes 8 | tf_op jit(solution)/shard_map/psum | solution.py:44
  405.1 19.6 %all_gather.11 = bf16[1536,128]{1,0:T(8,128)(2,1)} all-gather(bf16[96,128]{1,0:T(8,128)(2,1)S(1)} %fusion.69), channel_id=1, replica_groups=mesh['scen'=8,'vec'=16] {'vec'}, dimensions={0}, use_global_device_ids=true | all-gather | bytes 417792 | tf_op jit(solution)/shard_map/all_gather | solution.py:62
  424.6 1.6 gather_fusion.2
  426.9 0.9 fusion.2
  428.8 1.8 fusion.24
  430.6 89.4 %reduce-scatter.8.cloned.1.call-done = f32[96,128]{1,0:T(8,128)} async-done(((f32[1536,128]{1,0:T(8,128)}), f32[96,128]{1,0:T(8,128)}) %reduce-scatter.8.cloned.1.call-update) | async-done | bytes 49168 | tf_op jit(solution)/shard_map/reduce_scatter | solution.py:65
  520.0 23.6 %psum.70 = f32[96,128]{1,0:T(8,128)S(1)} all-reduce(f32[96,128]{1,0:T(8,128)} %reduce-scatter.8.cloned.1.call-done), channel_id=1, replica_groups=mesh['scen'=8,'vec'=16] {'scen'}, use_global_device_ids=true, to_apply=%region_15.0 | all-reduce | flops 12288 | bytes 98304 | tf_op jit(solution)/shard_map/psum | solution.py:71
  544.3 31.7 %psum.71 = f32[]{:T(128)} all-reduce(f32[]{:T(128)} %multiply_reduce_fusion), channel_id=1, replica_groups=mesh['scen'=8,'vec'=16] {'vec'}, use_global_device_ids=true, to_apply=%region_17.0 | all-reduce | flops 1 | bytes 8 | tf_op jit(solution)/shard_map/psum | solution.py:44
  (57 shorter events, 10.8 us)
Async XLA Ops:
  7.2 26.1 %copy-start = (bf16[1,24,3,128,128]{4,3,2,1,0:T(8,128)(2,1)S(1)}, bf16[1,24,3,128,128]{4,3,2,1,0:T(8,128)(2,1)}, u32[]{:S(2)}) copy-start(bf16[1,24,3,128,128]{4,3,2,1,0:T(8,128)(2,1)} %param.10) | copy-start | bytes 7077892
  7.2 105.6 %reduce-scatter.4.cloned.1.call-start = ((), (), s32[]{:S(2)}) async-start(), calls=%async_computation.3 | async-start | bytes 835584 | tf_op jit(solution)/shard_map/reduce_scatter | solution.py:65
  33.3 1.6 copy-start.1
  33.3 1.9 copy-start.4
  34.2 102.2 %copy-start.2 = (f32[96,128]{1,0:T(8,128)S(1)}, f32[96,128]{1,0:T(8,128)}, u32[]{:S(2)}) copy-start(f32[96,128]{1,0:T(8,128)} %param.7) | copy-start | bytes 147460
  34.2 102.2 %copy-start.3 = (f32[96,128]{1,0:T(8,128)S(1)}, f32[96,128]{1,0:T(8,128)}, u32[]{:S(2)}) copy-start(f32[96,128]{1,0:T(8,128)} %param.6) | copy-start | bytes 147460
  37.0 279.4 %reduce-scatter.6.cloned.1.call-start = ((), (), s32[]{:S(2)}) async-start(), calls=%async_computation.4 | async-start | bytes 835584 | tf_op jit(solution)/shard_map/reduce_scatter | solution.py:65
  226.9 293.1 %reduce-scatter.8.cloned.1.call-start = ((), (), s32[]{:S(2)}) async-start(), calls=%async_computation.5 | async-start | bytes 835584 | tf_op jit(solution)/shard_map/reduce_scatter | solution.py:65
Sparse Core Ops, SparseCore 0:
  37.1 75.6 reduce-scatter.3
  227.0 89.3 reduce-scatter.5
  430.7 89.2 reduce-scatter.7
where the time goes:
time: 595 us; the launch traced here: 585 us
  blocking collectives  285 us (48%)
  waiting for transfers between devices  255 us (43%)
  between operations  20.6 us (3%)
  matrix products  13.2 us (2%)
  other arithmetic  6.98 us (1%)
    reduce_scatter x3, waiting for transfers between devices, shards(): lax.psum_scatter(collect_rows(lifted, couple_idx, lax.axis_size('vec') *...  255 us
    psum x5, blocking collectives, inner_sums(): return lax.psum((values[0],), 'vec')  154 us
    psum x3, blocking collectives, shards(): summed = lax.psum(summed, 'scen')  71 us
    all_gather x3, blocking collectives, shards(): full16 = lax.all_gather(share16, 'vec', axis=0, tiled=True)  60.2 us
  transfers between devices with their start and end apart: 3, of which 3 were waited for; matrix products, arithmetic and copies ran while one was open for 0% of the time, Pallas kernels for 0%

commit v1 on v0

v1 whole, which is shorter than its diff:
```python
import functools

import jax
import jax.numpy as jnp
import numpy as np
from jax import lax
from jax.experimental import pallas as pl
from jax.experimental.pallas import tpu as pltpu
from jax.sharding import Mesh
from jax.sharding import PartitionSpec as P

ROWS = 24
PAD = 32
OWN = 96
WIDTH = 128
CHIPS = 64
GAMMA, DELTA = 4000, 4001
F32, BF16 = jnp.float32, jnp.bfloat16


def dot_nn(a, b):
    return lax.dot_general(a, b, (((1,), (0,)), ((), ())), preferred_element_type=F32)


def dot_nt(a, b):
    return lax.dot_general(a, b, (((1,), (1,)), ((), ())), preferred_element_type=F32)


def only_row(rows, values, r):
    return jnp.where(rows == r, values, 0.0).astype(BF16)


def split(values):
    high = values.astype(BF16).astype(F32)
    return high, values - high


def scenario_lift(y, couple, factor, reach):
    rows = lax.broadcasted_iota(jnp.int32, (PAD, WIDTH), 0)
    left, right = reach[:, 0:1], reach[:, 1:2]
    coupled = jnp.zeros((PAD, WIDTH), F32)
    for r in range(ROWS):
        coupled += dot_nt(only_row(rows, y, r), couple[r])
    coupled = coupled.astype(BF16).astype(F32)
    slots = (pltpu.roll(coupled, 1, 0) * left, coupled, pltpu.roll(coupled, PAD - 1, 0) * right)
    weighted = jnp.zeros((PAD, WIDTH), F32)
    for r in range(ROWS):
        for k in range(3):
            weighted += dot_nt(only_row(rows, slots[k], r), factor[r, k])
    weighted = weighted.astype(BF16).astype(F32)
    spread = [jnp.zeros((PAD, WIDTH), F32) for k in range(3)]
    for r in range(ROWS):
        row = only_row(rows, weighted, r)
        for k in range(3):
            spread[k] += dot_nn(row, factor[r, k])
    returned = (
        spread[1]
        + pltpu.roll(spread[0] * left, PAD - 1, 0)
        + pltpu.roll(spread[2] * right, 1, 0)
    )
    returned = returned.astype(BF16).astype(F32)
    lifted = jnp.zeros((PAD, WIDTH), F32)
    for r in range(ROWS):
        lifted += dot_nn(only_row(rows, returned, r), couple[r])
    return lifted


def message(lifted, gamma, delta, extra):
    rows = lax.broadcasted_iota(jnp.int32, (PAD, WIDTH), 0)
    out = jnp.where(rows < ROWS, lifted, 0.0)
    for place, line in enumerate(split(gamma) + split(delta) + tuple(extra)):
        out = jnp.where(rows == ROWS + place, jnp.broadcast_to(line, out.shape), out)
    return out.astype(BF16)


def column_sum(values):
    return jnp.sum(values, axis=0, keepdims=True)


def first_kernel(
    core_ref, near, far, tgt, label, reach, rhs, diag, share, couple, factor, msg_out, us_out
):
    half = OWN // 2
    core = core_ref[0]
    want = tgt[0:PAD, :]
    us = jnp.zeros((PAD, WIDTH), F32)
    for part, which in ((near, core), (far, 1 - core)):
        place = lax.broadcasted_iota(jnp.int32, (1, 16 * half), 1)
        shard = (place * 1366) >> 16
        block = place + half * shard + half * which
        us += dot_nn((want == block).astype(F32).astype(BF16), part[...])
    us_out[...] = us
    lifted = scenario_lift(us, couple, factor, reach[...])
    own = rhs[...]
    u = own * (1.0 / diag[...])
    gamma = column_sum(own * u) * 0.125
    delta = column_sum(diag[...] * u * u) * 0.125 + column_sum(us * lifted)
    msg_out[0:PAD, :] = message(lifted, gamma, delta, (label[0:1, :], label[1:2, :]))
    rows = lax.broadcasted_iota(jnp.int32, (PAD, WIDTH), 0)
    high, low = split(share[...])
    msg_out[PAD : 2 * PAD, :] = jnp.where(rows < 12, high, low).astype(BF16)


def advance(total, us, inv_s, ps, u, diag, q, d, x, r, gamma_old, alpha_old):
    gamma = jnp.sum(total[ROWS : ROWS + 1, :], axis=1, keepdims=True)
    delta = jnp.sum(total[ROWS + 1 : ROWS + 2, :], axis=1, keepdims=True)
    if gamma_old is None:
        alpha = gamma / delta
    else:
        beta = gamma / gamma_old
        alpha = gamma / (delta - beta * gamma / alpha_old)
    image = total[PAD:, :]
    s = diag * u + image
    if gamma_old is None:
        d, q = u, s
    else:
        d, q = u + beta * d, s + beta * q
    x = alpha * d if x is None else x + alpha * d
    r = r - alpha * q
    if us is not None:
        rows = lax.broadcasted_iota(jnp.int32, (PAD, WIDTH), 0)
        own = jnp.where(rows < ROWS, us + inv_s * total[0:PAD, :], 0.0)
        ps = own if ps is None else own + beta * ps
        us = us - alpha * ps
    return gamma, alpha, us, ps, d, q, x, r


def next_message(us, u, r, diag, couple, factor, reach):
    lifted = scenario_lift(us, couple, factor, reach)
    gamma = column_sum(r * u) * 0.125
    delta = column_sum(diag * u * u) * 0.125 + column_sum(us * lifted)
    return message(lifted, gamma, delta, ())


def second_kernel(
    core_ref, near, far, tgt, us, reach, rhs, diag, couple, factor,
    msg_out, hot_out, us_out, ps_out, inv_out, scal_out, d_out, q_out, x_out, r_out,
):
    core = core_ref[0]
    want = tgt[...]
    lane = lax.broadcasted_iota(jnp.int32, (1, WIDTH), 1)
    slot = lane & (PAD - 1)
    fixed = jnp.where(slot < ROWS + 2, GAMMA, jnp.where(slot < ROWS + 4, DELTA, -1))
    sums = []
    inverse = jnp.zeros((PAD, WIDTH), F32)
    for number, (part, which) in enumerate(((near, core), (far, 1 - core))):
        total = jnp.zeros((PAD + OWN, WIDTH), F32)
        for chunk in range(CHIPS // 4):
            tiles = [part[4 * chunk + m] for m in range(4)]
            ends = [t[ROWS:PAD, :].astype(F32) for t in tiles]
            ends = ends[0] + ends[1] + ends[2] + ends[3]
            found = (ends[4:5, :] * 64.0 + ends[5:6, :]).astype(jnp.int32)
            block = jnp.where(slot < ROWS, found, fixed)
            hot = (want == block).astype(F32).astype(BF16)
            hot_out[number, chunk] = hot
            total += dot_nn(hot, jnp.concatenate([t[0:PAD, :] for t in tiles], axis=0))
            place = chunk * 4 + (lane >> 5)
            member = jnp.where(slot < 12, slot, slot - 12)
            shard = (place & 15) * OWN + ((place >> 4) * 2 + which) * 12 + member
            shard = jnp.where(slot < 24, shard, -1)
            pick = (want[0:PAD, :] == shard).astype(F32).astype(BF16)
            inverse += dot_nn(pick, jnp.concatenate([t[PAD:, :] for t in tiles], axis=0))
        sums.append(total)
    total = sums[0] + sums[1]
    own = rhs[...]
    cost = diag[...]
    inv = 1.0 / cost
    gamma, alpha, u_s, p_s, d, q, x, r = advance(
        total, us[...], inverse, None, inv * own, cost, None, None, None, own, None, None
    )
    us_out[...], ps_out[...], inv_out[...] = u_s, p_s, inverse
    d_out[...], q_out[...], x_out[...], r_out[...] = d, q, x, r
    scal_out[0:1, :] = jnp.broadcast_to(gamma, (1, WIDTH))
    scal_out[1:2, :] = jnp.broadcast_to(alpha, (1, WIDTH))
    msg_out[...] = next_message(u_s, inv * r, r, cost, couple, factor, reach[...])


def gathered(near, far, hot):
    sums = []
    for number, part in enumerate((near, far)):
        total = jnp.zeros((PAD + OWN, WIDTH), F32)
        for chunk in range(CHIPS // 4):
            total += dot_nn(hot[number, chunk], part[128 * chunk : 128 * chunk + 128, :])
        sums.append(total)
    return sums[0] + sums[1]


def third_kernel(
    near, far, hot, us, ps, inv_s, scal, d, q, x, r, reach, diag, couple, factor,
    msg_out, us_out, ps_out, scal_out, d_out, q_out, x_out, r_out,
):
    total = gathered(near, far, hot)
    cost = diag[...]
    inv = 1.0 / cost
    gamma, alpha, u_s, p_s, dn, qn, xn, rn = advance(
        total, us[...], inv_s[...], ps[...], inv * r[...], cost, q[...], d[...], x[...], r[...],
        scal[0:1, 0:1], scal[1:2, 0:1],
    )
    us_out[...], ps_out[...] = u_s, p_s
    d_out[...], q_out[...], x_out[...], r_out[...] = dn, qn, xn, rn
    scal_out[0:1, :] = jnp.broadcast_to(gamma, (1, WIDTH))
    scal_out[1:2, :] = jnp.broadcast_to(alpha, (1, WIDTH))
    msg_out[...] = next_message(u_s, inv * rn, rn, cost, couple, factor, reach[...])


def last_kernel(near, far, hot, scal, d, q, x, r, diag, x_out, r_out):
    total = gathered(near, far, hot)
    cost = diag[...]
    found = advance(
        total, None, None, None, r[...] / cost, cost, q[...], d[...], x[...], r[...],
        scal[0:1, 0:1], scal[1:2, 0:1],
    )
    x_out[...], r_out[...] = found[6], found[7]


def call(kernel, shapes, *args, scalars=0):
    vmem = pl.BlockSpec(memory_space=pltpu.VMEM)
    specs = [pl.BlockSpec(memory_space=pltpu.SMEM)] * scalars + [vmem] * (len(args) - scalars)
    return pl.pallas_call(
        kernel,
        out_shape=[jax.ShapeDtypeStruct(s, t) for s, t in shapes],
        in_specs=specs,
        out_specs=[vmem] * len(shapes),
        compiler_params=pltpu.CompilerParams(vmem_limit_bytes=24 * 1024 * 1024),
    )(*args)


def share_out(block, axes, count):
    return lax.all_to_all(
        jnp.broadcast_to(block[None], (count,) + block.shape), axes, 0, 0, tiled=True
    )


def other_core(values):
    return lax.ppermute(values, "core", [(0, 1), (1, 0)])


def shards(rhs, diag, couple, couple_idx, factor, pattern):
    couple, factor = couple[0], factor[0]
    core = lax.axis_index("core")
    vec = lax.axis_index("z") * 4 + lax.axis_index("y")
    inv = 1.0 / diag
    half = OWN // 2
    sent = lax.dynamic_slice_in_dim((rhs * inv).astype(BF16), core * half, half, 0)
    near = share_out(sent, ("z", "y"), 16).reshape(16 * half, WIDTH)
    far = other_core(near)

    idx = couple_idx[0]
    tgt = jnp.concatenate(
        [idx, jnp.array([GAMMA, DELTA] + [-2] * 6, jnp.int32), vec * OWN + jnp.arange(OWN)]
    )[:, None]
    spaced = jnp.tile(jnp.pad(idx, (0, PAD - ROWS)), 4)
    spaced = jnp.where(jnp.arange(WIDTH) // PAD == lax.axis_index("y"), spaced, 0)
    label = jnp.stack([spaced >> 6, spaced & 63]).astype(F32)
    place = jnp.arange(ROWS)
    reach = jnp.stack(
        [pattern[0, :, 0] * (place > 0), pattern[0, :, 1] * (place < ROWS - 1)], axis=1
    ).astype(F32)
    reach = jnp.pad(reach, ((0, PAD - ROWS), (0, 0)))
    eighth = lax.dynamic_slice_in_dim(inv, (lax.axis_index("x") * 2 + core) * 12, 12, 0)
    share = jnp.concatenate([eighth, eighth, jnp.zeros((8, WIDTH), F32)], axis=0)
    core_arg = core[None]

    scen, own, msg = ((PAD, WIDTH), F32), ((OWN, WIDTH), F32), ((PAD, WIDTH), BF16)
    scal = ((2, WIDTH), F32)
    sent, us = call(
        first_kernel, [((2 * PAD, WIDTH), BF16), scen],
        core_arg, near, far, tgt, label, reach, rhs, diag, share, couple, factor, scalars=1,
    )
    near = share_out(sent, ("x", "z", "y"), CHIPS)
    far = other_core(near)
    sent, hot, us, ps, inv_s, sc, d, q, x, r = call(
        second_kernel,
        [msg, ((2, CHIPS // 4, PAD + OWN, WIDTH), BF16), scen, scen, scen, scal, own, own, own, own],
        core_arg, near, far, tgt, us, reach, rhs, diag, couple, factor, scalars=1,
    )
    near = share_out(sent, ("x", "z", "y"), CHIPS).reshape(CHIPS * PAD, WIDTH)
    far = other_core(near)
    sent, us, ps, sc, d, q, x, r = call(
        third_kernel, [msg, scen, scen, scal, own, own, own, own],
        near, far, hot, us, ps, inv_s, sc, d, q, x, r, reach, diag, couple, factor,
    )
    near = share_out(sent, ("x", "z", "y"), CHIPS).reshape(CHIPS * PAD, WIDTH)
    far = other_core(near)
    x, r = call(last_kernel, [own, own], near, far, hot, sc, d, q, x, r, diag)
    return x, r


def solution(mesh):
    fine = Mesh(np.array(mesh.devices).reshape(4, 2, 4, 4), ("x", "core", "z", "y"))
    vec, scen = ("z", "y"), ("x", "core", "z", "y")
    in_specs = (
        P(vec, None),
        P(vec, None),
        P(scen, None, None, None),
        P(scen, None),
        P(scen, None, None, None, None),
        P(scen, None, None),
    )
    out_specs = (P(vec, None), P(vec, None))
    return jax.shard_map(shards, mesh=fine, in_specs=in_specs, out_specs=out_specs, check_vma=False)
```

time: 595 us -> 114 us (0.19); the launches traced: 585 us -> 113 us
  waiting for transfers between devices: 255 us -> 10.9 us
  blocking collectives: 285 us -> 56 us
  between operations: 20.6 us -> 0.76 us
  Pallas kernels: 0 us -> 18.6 us
  starting transfers between devices: 0.12 us -> 17.3 us
  matrix products: 13.2 us -> 0 us
    reduce_scatter x3 -> x0, waiting for transfers between devices: 255 us -> none  [shards(): lax.psum_scatter(collect_rows(lifted, couple_idx, lax.axis_size('vec') *...]
    psum x8 -> x0, blocking collectives: 225 us -> none  [the longest x5 154 us: inner_sums(): return lax.psum((values[0],), 'vec')]
    all_gather x3 -> x0, blocking collectives: 60.2 us -> none  [shards(): full16 = lax.all_gather(share16, 'vec', axis=0, tiled=True)]
    all_to_all x0 -> x3, blocking collectives: none -> 56 us  [share_out(): lax.all_to_all(jnp.broadcast_to(block[None], (count,) + block.shape), axe...]
    pallas_call x0 -> x4, Pallas kernels: none -> 18.6 us  [call(): pl.pallas_call(kernel, out_shape=[jax.ShapeDtypeStruct(s, t) for s, t in...]
    dot_general x15 -> x0, matrix products: 13.2 us -> none  [the longest x3 5.26 us: collect_rows(): jnp.einsum('srf,srj->fj', onehot, lifted, precision=lax.Precision.HIGHEST)]
    ppermute x0 -> x4, starting transfers between devices: none -> 8.73 us  [other_core(): return lax.ppermute(values, 'core', [(0, 1), (1, 0)])]
    all_to_all x0 -> x1, starting transfers between devices: none -> 8.6 us  [share_out(): lax.all_to_all(jnp.broadcast_to(block[None], (count,) + block.shape), axe...]
  transfers between devices with their start and end apart: 3 -> 5, of which waited for: 3 -> 5; matrix products, arithmetic and copies ran while one was open for 0% -> 2% of each run, Pallas kernels for 0% -> 0%
where the time goes in v1:
time: 114 us; the launch traced here: 113 us
  blocking collectives  56 us (49%)
  Pallas kernels  18.6 us (16%)
  starting transfers between devices  17.3 us (15%)
  waiting for transfers between devices  10.9 us (10%)
  local copies, waits for them, and re-layouts  6.53 us (6%)
  other arithmetic  3.18 us (3%)
    all_to_all x3, blocking collectives, share_out(): lax.all_to_all(jnp.broadcast_to(block[None], (count,) + block.shape), axe...  56 us
    pallas_call x4, Pallas kernels, call(): pl.pallas_call(kernel, out_shape=[jax.ShapeDtypeStruct(s, t) for s, t in...  18.6 us
    ppermute x4, starting transfers between devices, other_core(): return lax.ppermute(values, 'core', [(0, 1), (1, 0)])  8.73 us
    all_to_all x1, starting transfers between devices, share_out(): lax.all_to_all(jnp.broadcast_to(block[None], (count,) + block.shape), axe...  8.6 us
    ppermute x4, waiting for transfers between devices, other_core(): return lax.ppermute(values, 'core', [(0, 1), (1, 0)])  6.36 us
    all_to_all x1, waiting for transfers between devices, share_out(): lax.all_to_all(jnp.broadcast_to(block[None], (count,) + block.shape), axe...  4.56 us
    unnamed x12, local copies, waits for them, and re-layouts  4.4 us
  transfers between devices with their start and end apart: 5, of which 5 were waited for; matrix products, arithmetic and copies ran while one was open for 2% of the time, Pallas kernels for 0%

profile of v1, /device:TPU:1, one launch (start us, length us, event | category | flops | bytes accessed | tf_op | source)
XLA Modules:
  0.0 113.2 jit_solution(17195303454656303587)
XLA Ops:
  0.6 0.8 broadcast_divide_fusion
  1.5 0.8 fusion
  2.9 8.6 %all-to-all-start = ((bf16[16,48,128]{2,1,0:T(8,128)(2,1)}), bf16[16,48,128]{2,1,0:T(8,128)(2,1)S(1)}, u32[]{:S(2)}, u32[]{:S(2)}) async-start(bf16[16,48,128]{2,1,0:T(8,128)(2,1)} %broadcast_in_dim.17), calls=%async_computation | async-start | bytes 393216 | tf_op jit(solution)/shard_map/all_to_all | solution.py:229
  12.2 0.8 compare_select_fusion.1
  14.1 4.6 %all-to-all-done = bf16[16,48,128]{2,1,0:T(8,128)(2,1)S(1)} async-done(((bf16[16,48,128]{2,1,0:T(8,128)(2,1)}), bf16[16,48,128]{2,1,0:T(8,128)(2,1)S(1)}, u32[]{:S(2)}, u32[]{:S(2)}) %all-to-all-start) | async-done | bytes 196640 | tf_op jit(solution)/shard_map/all_to_all | solution.py:229
  18.7 2.1 %collective-permute-start = (bf16[768,128]{1,0:T(8,128)(2,1)S(1)}, bf16[768,128]{1,0:T(8,128)(2,1)S(1)}, u32[]{:S(2)}, u32[]{:S(2)}) collective-permute-start(bf16[768,128]{1,0:T(8,128)(2,1)S(1)} %bitcast.23), channel_id=1, source_target_pairs={{0,16},{16,0},{1,17},{17,1},{2,18},{18,2},{3,19},{19,3},{4,20},{20... | collective-permute-start | bytes 589832 | tf_op jit(solution)/shard_map/ppermute | solution.py:235
  20.9 1.0 collective-permute-done.far
  21.9 1.7 %copy-done = bf16[1,24,3,128,128]{4,3,2,1,0:T(8,128)(2,1)S(1)} copy-done((bf16[1,24,3,128,128]{4,3,2,1,0:T(8,128)(2,1)S(1)}, bf16[1,24,3,128,128]{4,3,2,1,0:T(8,128)(2,1)}, u32[]{:S(2)}) %copy-start) | copy-done | bytes 2359320
  23.5 1.1 copy-done.2
  24.7 0.8 copy-done.3
  25.5 0.8 copy-done.5
  26.3 5.5 %shard_map.86 = (bf16[64,128]{1,0:T(8,128)(2,1)S(1)}, f32[32,128]{1,0:T(8,128)S(1)}) custom-call(s32[1]{0:T(128)} %bitcast.core_ref, bf16[768,128]{1,0:T(8,128)(2,1)S(1)} %bitcast.24, bf16[768,128]{1,0:T(8,128)(2,1)S(1)} %collective-permute-done.far, s32[128,1]{1,0:T(8,128)S(1)} %copy.17.tgt, f32[2,128]{1,0:T(2,128)S(1)} %add_convert_fusion.label, ...), custom_call_target="tpu_custom_call" | custom-call | tf_op jit(solution)/shard_map/pallas_call | solution.py:219
  32.0 23.2 %all_to_all.20.near = bf16[64,64,128]{2,1,0:T(8,128)(2,1)S(1)} all-to-all(bf16[64,64,128]{2,1,0:T(8,128)(2,1)S(1)} %broadcast_in_dim.20), channel_id=1, replica_groups=mesh['x'=4,'core'=2,'z'=4,'y'=4] {'x','z','y'}, dimensions={0} | all-to-all | bytes 2097152 | tf_op jit(solution)/shard_map/all_to_all | solution.py:229
  55.2 2.5 %collective-permute-start.1 = (bf16[64,64,128]{2,1,0:T(8,128)(2,1)S(1)}, bf16[64,64,128]{2,1,0:T(8,128)(2,1)S(1)}, u32[]{:S(2)}, u32[]{:S(2)}) collective-permute-start(bf16[64,64,128]{2,1,0:T(8,128)(2,1)S(1)} %all_to_all.20.near), channel_id=1, source_target_pairs={{0,16},{16,0},{1,17},{17,1},{2,18},{18,2},{3,19},{19,3},{4,20},{20... | collective-permute-start | bytes 3145736 | tf_op jit(solution)/shard_map/ppermute | solution.py:235
  57.7 2.3 %collective-permute-done.1.far = bf16[64,64,128]{2,1,0:T(8,128)(2,1)S(1)} collective-permute-done((bf16[64,64,128]{2,1,0:T(8,128)(2,1)S(1)}, bf16[64,64,128]{2,1,0:T(8,128)(2,1)S(1)}, u32[]{:S(2)}, u32[]{:S(2)}) %collective-permute-start.1) | collective-permute-done | bytes 1048608 | tf_op jit(solution)/shard_map/ppermute | solution.py:235
  60.0 6.1 %shard_map.87 = (bf16[32,128]{1,0:T(8,128)(2,1)S(1)}, bf16[2,16,128,128]{3,2,1,0:T(8,128)(2,1)S(1)}, f32[32,128]{1,0:T(8,128)S(1)}, f32[32,128]{1,0:T(8,128)S(1)...) custom-call(s32[1]{0:T(128)} %bitcast.core_ref, ...), custom_call_target="tpu_custom_call" | custom-call | tf_op jit(solution)/shard_map/pallas_call | solution.py:219
  66.2 16.3 %all_to_all.21 = bf16[64,32,128]{2,1,0:T(8,128)(2,1)S(1)} all-to-all(bf16[64,32,128]{2,1,0:T(8,128)(2,1)S(1)} %broadcast_in_dim.40), channel_id=1, replica_groups=mesh['x'=4,'core'=2,'z'=4,'y'=4] {'x','z','y'}, dimensions={0} | all-to-all | bytes 1048576 | tf_op jit(solution)/shard_map/all_to_all | solution.py:229
  82.6 2.1 %collective-permute-start.2 = (bf16[2048,128]{1,0:T(8,128)(2,1)S(1)}, bf16[2048,128]{1,0:T(8,128)(2,1)S(1)}, u32[]{:S(2)}, u32[]{:S(2)}) collective-permute-start(bf16[2048,128]{1,0:T(8,128)(2,1)S(1)} %bitcast.19), channel_id=1, source_target_pairs={{0,16},{16,0},{1,17},{17,1},{2,18},{18,2},{3,19},{19,3},{4,20},{20... | collective-permute-start | bytes 1572872 | tf_op jit(solution)/shard_map/ppermute | solution.py:235
  84.7 1.5 %collective-permute-done.2.far = bf16[2048,128]{1,0:T(8,128)(2,1)S(1)} collective-permute-done((bf16[2048,128]{1,0:T(8,128)(2,1)S(1)}, bf16[2048,128]{1,0:T(8,128)(2,1)S(1)}, u32[]{:S(2)}, u32[]{:S(2)}) %collective-permute-start.2) | collective-permute-done | bytes 524320 | tf_op jit(solution)/shard_map/ppermute | solution.py:235
  86.2 5.8 %shard_map.88 = (bf16[32,128]{1,0:T(8,128)(2,1)S(1)}, f32[32,128]{1,0:T(8,128)}, f32[32,128]{1,0:T(8,128)}, f32[2,128]{1,0:T(2,128)S(1)}, f32[96,128]{1,0:T(8,12...) custom-call(bf16[2048,128]{1,0:T(8,128)(2,1)S(1)} %bitcast.20, ...), custom_call_target="tpu_custom_call" | custom-call | tf_op jit(solution)/shard_map/pallas_call | solution.py:219
  92.0 16.4 %all_to_all.22 = bf16[64,32,128]{2,1,0:T(8,128)(2,1)S(1)} all-to-all(bf16[64,32,128]{2,1,0:T(8,128)(2,1)S(1)} %broadcast_in_dim.41), channel_id=1, replica_groups=mesh['x'=4,'core'=2,'z'=4,'y'=4] {'x','z','y'}, dimensions={0} | all-to-all | bytes 1048576 | tf_op jit(solution)/shard_map/all_to_all | solution.py:229
  108.4 2.1 %collective-permute-start.3 = (bf16[2048,128]{1,0:T(8,128)(2,1)S(1)}, bf16[2048,128]{1,0:T(8,128)(2,1)S(1)}, u32[]{:S(2)}, u32[]{:S(2)}) collective-permute-start(bf16[2048,128]{1,0:T(8,128)(2,1)S(1)} %bitcast.21), channel_id=1, source_target_pairs={{0,16},{16,0},{1,17},{17,1},{2,18},{18,2},{3,19},{19,3},{4,20},{20... | collective-permute-start | bytes 1572872 | tf_op jit(solution)/shard_map/ppermute | solution.py:235
  110.5 1.5 %collective-permute-done.3.far = bf16[2048,128]{1,0:T(8,128)(2,1)S(1)} collective-permute-done((bf16[2048,128]{1,0:T(8,128)(2,1)S(1)}, bf16[2048,128]{1,0:T(8,128)(2,1)S(1)}, u32[]{:S(2)}, u32[]{:S(2)}) %collective-permute-start.3) | collective-permute-done | bytes 524320 | tf_op jit(solution)/shard_map/ppermute | solution.py:235
  112.1 1.2 %shard_map.89 = (f32[96,128]{1,0:T(8,128)}, f32[96,128]{1,0:T(8,128)}) custom-call(bf16[2048,128]{1,0:T(8,128)(2,1)S(1)} %bitcast.22, bf16[2048,128]{1,0:T(8,128)(2,1)S(1)} %collective-permute-done.3.far, bf16[2,16,128,128]{3,2,1,0:T(8,128)(2,1)S(1)} %get-tuple-element.23.hot, f32[2,128]{1,0:T(2,128)S(1)} %get-tuple-element.33.scal, ...), custom_call_target="tpu_custom_call" | custom-call | tf_op jit(solution)/shard_map/pallas_call | solution.py:219
  (28 shorter events, 3.0 us)
Async XLA Ops:
  2.9 15.8 %all-to-all-start = ((bf16[16,48,128]{2,1,0:T(8,128)(2,1)}), bf16[16,48,128]{2,1,0:T(8,128)(2,1)S(1)}, u32[]{:S(2)}, u32[]{:S(2)}) async-start(bf16[16,48,128]{2,1,0:T(8,128)(2,1)} %broadcast_in_dim.17), calls=%async_computation | async-start | bytes 393216 | tf_op jit(solution)/shard_map/all_to_all | solution.py:229
  18.7 3.2 %collective-permute-start = (bf16[768,128]{1,0:T(8,128)(2,1)S(1)}, bf16[768,128]{1,0:T(8,128)(2,1)S(1)}, u32[]{:S(2)}, u32[]{:S(2)}) collective-permute-start(bf16[768,128]{1,0:T(8,128)(2,1)S(1)} %bitcast.23), channel_id=1, source_target_pairs={{0,16},{16,0},{1,17},{17,1},{2,18},{18,2},{3,19},{19,3},{4,20},{20... | collective-permute-start | bytes 589832 | tf_op jit(solution)/shard_map/ppermute | solution.py:235
  21.9 1.7 %copy-start = (bf16[1,24,3,128,128]{4,3,2,1,0:T(8,128)(2,1)S(1)}, bf16[1,24,3,128,128]{4,3,2,1,0:T(8,128)(2,1)}, u32[]{:S(2)}) copy-start(bf16[1,24,3,128,128]{4,3,2,1,0:T(8,128)(2,1)} %param.11) | copy-start | bytes 7077892
  23.5 1.1 %copy-start.2 = (bf16[1,24,128,128]{3,2,1,0:T(8,128)(2,1)S(1)}, bf16[1,24,128,128]{3,2,1,0:T(8,128)(2,1)}, u32[]{:S(2)}) copy-start(bf16[1,24,128,128]{3,2,1,0:T(8,128)(2,1)} %param.9) | copy-start | bytes 2359300
  24.7 0.8 copy-start.3
  25.5 0.8 copy-start.5
  31.8 28.2 %copy-start.1 = (bf16[1,24,3,128,128]{4,3,2,1,0:T(8,128)(2,1)S(1)}, bf16[1,24,3,128,128]{4,3,2,1,0:T(8,128)(2,1)}, u32[]{:S(2)}) copy-start(bf16[1,24,3,128,128]{4,3,2,1,0:T(8,128)(2,1)} %param.11) | copy-start | bytes 7077892
  55.2 4.8 %collective-permute-start.1 = (bf16[64,64,128]{2,1,0:T(8,128)(2,1)S(1)}, bf16[64,64,128]{2,1,0:T(8,128)(2,1)S(1)}, u32[]{:S(2)}, u32[]{:S(2)}) collective-permute-start(bf16[64,64,128]{2,1,0:T(8,128)(2,1)S(1)} %all_to_all.20.near), channel_id=1, source_target_pairs={{0,16},{16,0},{1,17},{17,1},{2,18},{18,2},{3,19},{19,3},{4,20},{20... | collective-permute-start | bytes 3145736 | tf_op jit(solution)/shard_map/ppermute | solution.py:235
  60.0 26.2 %copy-start.4 = (f32[96,128]{1,0:T(8,128)S(1)}, f32[96,128]{1,0:T(8,128)}, u32[]{:S(2)}) copy-start(f32[96,128]{1,0:T(8,128)} %diag.7) | copy-start | bytes 147460
  82.6 3.6 %collective-permute-start.2 = (bf16[2048,128]{1,0:T(8,128)(2,1)S(1)}, bf16[2048,128]{1,0:T(8,128)(2,1)S(1)}, u32[]{:S(2)}, u32[]{:S(2)}) collective-permute-start(bf16[2048,128]{1,0:T(8,128)(2,1)S(1)} %bitcast.19), channel_id=1, source_target_pairs={{0,16},{16,0},{1,17},{17,1},{2,18},{18,2},{3,19},{19,3},{4,20},{20... | collective-permute-start | bytes 1572872 | tf_op jit(solution)/shard_map/ppermute | solution.py:235
  108.4 3.6 %collective-permute-start.3 = (bf16[2048,128]{1,0:T(8,128)(2,1)S(1)}, bf16[2048,128]{1,0:T(8,128)(2,1)S(1)}, u32[]{:S(2)}, u32[]{:S(2)}) collective-permute-start(bf16[2048,128]{1,0:T(8,128)(2,1)S(1)} %bitcast.21), channel_id=1, source_target_pairs={{0,16},{16,0},{1,17},{17,1},{2,18},{18,2},{3,19},{19,3},{4,20},{20... | collective-permute-start | bytes 1572872 | tf_op jit(solution)/shard_map/ppermute | solution.py:235

commit v2 on v1

v2 whole, which is shorter than its diff:
```python
import jax
import jax.numpy as jnp
import numpy as np
from jax import lax
from jax.experimental import pallas as pl
from jax.experimental.pallas import tpu as pltpu
from jax.sharding import Mesh
from jax.sharding import PartitionSpec as P

ROWS = 24
PAD = 32
OWN = 96
HALF = OWN // 2
WIDTH = 128
CHIPS = 64
PLANE = 16
GAMMA, DELTA = 4000, 4001
INVERSE = 2048
F32, BF16 = jnp.float32, jnp.bfloat16


def dot_nn(a, b):
    return lax.dot_general(a, b, (((1,), (0,)), ((), ())), preferred_element_type=F32)


def dot_nt(a, b):
    return lax.dot_general(a, b, (((1,), (1,)), ((), ())), preferred_element_type=F32)


def split(values):
    high = values.astype(BF16).astype(F32)
    return high, values - high


def hot_of(mask):
    return mask.astype(F32).astype(BF16)


def by_row(values):
    rows = lax.broadcasted_iota(jnp.int32, (PAD, WIDTH), 0)
    return jnp.concatenate(
        [jnp.where(rows == r, values, 0.0).astype(BF16) for r in range(ROWS)], axis=1
    )


def fetch(first_hbm, second_hbm, first, second, sems):
    copies = (
        pltpu.make_async_copy(first_hbm, first, sems.at[0]),
        pltpu.make_async_copy(second_hbm, second, sems.at[1]),
    )
    for copy in copies:
        copy.start()
    return copies


def scenario_lift(y, copies, couple, factor, reach):
    left, right = reach[:, 0:1], reach[:, 1:2]
    copies[0].wait()
    beside = jnp.concatenate([couple[r] for r in range(ROWS)], axis=1)
    coupled = dot_nt(by_row(y), beside).astype(BF16).astype(F32)
    slots = jnp.concatenate(
        [pltpu.roll(coupled, 1, 0) * left, coupled, pltpu.roll(coupled, PAD - 1, 0) * right], axis=1
    ).astype(BF16)
    copies[1].wait()
    lane = lax.broadcasted_iota(jnp.int32, (WIDTH, PAD), 1)
    weighted = jnp.zeros((WIDTH, PAD), F32)
    for r in range(ROWS):
        blocks = jnp.concatenate([factor[r, k] for k in range(3)], axis=1)
        weighted = jnp.where(lane == r, dot_nt(blocks, slots), weighted)
    weighted = weighted.T.astype(BF16).astype(F32)
    rows = lax.broadcasted_iota(jnp.int32, (PAD, WIDTH), 0)
    spread = jnp.zeros((PAD, 3 * WIDTH), F32)
    for r in range(0, ROWS, 2):
        pair = [jnp.where(rows == r + i, weighted, 0.0).astype(BF16) for i in range(2)]
        blocks = [factor[r : r + 2, k].reshape(2 * WIDTH, WIDTH) for k in range(3)]
        spread += dot_nn(jnp.concatenate(pair, axis=1), jnp.concatenate(blocks, axis=1))
    returned = (
        spread[:, WIDTH : 2 * WIDTH]
        + pltpu.roll(spread[:, :WIDTH] * left, PAD - 1, 0)
        + pltpu.roll(spread[:, 2 * WIDTH :] * right, 1, 0)
    )
    returned = returned.astype(BF16).astype(F32)
    return dot_nn(by_row(returned), couple[...].reshape(ROWS * WIDTH, WIDTH))


def message(lifted, gamma, delta, extra):
    rows = lax.broadcasted_iota(jnp.int32, (PAD, WIDTH), 0)
    out = jnp.where(rows < ROWS, lifted, 0.0)
    for place, line in enumerate(split(gamma) + split(delta) + tuple(extra)):
        out = jnp.where(rows == ROWS + place, jnp.broadcast_to(line, out.shape), out)
    return out.astype(BF16)


def column_sum(values):
    return jnp.sum(values, axis=0, keepdims=True)


def next_message(us, u, r, cost, copies, couple, factor, reach, extra=()):
    lifted = scenario_lift(us, copies, couple, factor, reach)
    gamma = column_sum(r * u) * 0.125
    delta = column_sum(cost * u * u) * 0.125 + column_sum(us * lifted)
    return message(lifted, gamma, delta, extra)


def opening_kernel(core_ref, rhs_hbm, diag_hbm, msg_out, r_out, cost_out, rhs, diag, sems):
    for copy in fetch(rhs_hbm, diag_hbm, rhs, diag, sems):
        copy.wait()
    r_out[...], cost_out[...] = rhs[...], diag[...]
    mine = pl.ds(pl.multiple_of(core_ref[0] * HALF, HALF), HALF)
    inverse = 1.0 / diag[mine, :]
    u = (rhs[mine, :] * inverse).astype(BF16)
    inverse = inverse.astype(BF16)
    for place in range(PLANE):
        msg_out[place, 0:HALF, :] = u
        msg_out[place, HALF:OWN, :] = inverse


def first_kernel(
    core_ref, near, far, tgt, label, reach, own, cost, couple_hbm, factor_hbm,
    msg_out, us_out, inv_out, couple, factor, sems,
):
    copies = fetch(couple_hbm, factor_hbm, couple, factor, sems)
    core = core_ref[0]
    want = tgt[0:PAD, :]
    want = jnp.concatenate([want, want + INVERSE], axis=0)
    found = jnp.zeros((2 * PAD, WIDTH), F32)
    for part, which in ((near, core), (far, 1 - core)):
        place = lax.broadcasted_iota(jnp.int32, (1, PLANE * OWN), 1)
        member = place - OWN * ((place * 683) >> 16)
        block = place + HALF * which + jnp.where(member < HALF, 0, INVERSE - HALF)
        found += dot_nn(hot_of(want == block), part[...])
    us = found[0:PAD, :]
    us_out[...], inv_out[...] = us, found[PAD:, :]
    r, d = own[...], cost[...]
    msg_out[...] = next_message(
        us, r * (1.0 / d), r, d, copies, couple, factor, reach[...], (label[0:1, :], label[1:2, :])
    )


def advance(total, us, inv_s, ps, u, cost, q, d, x, r, gamma_old, alpha_old):
    gamma = jnp.sum(total[ROWS : ROWS + 1, :], axis=1, keepdims=True)
    delta = jnp.sum(total[ROWS + 1 : ROWS + 2, :], axis=1, keepdims=True)
    if gamma_old is None:
        alpha = gamma / delta
    else:
        beta = gamma / gamma_old
        alpha = gamma / (delta - beta * gamma / alpha_old)
    s = cost * u + total[PAD:, :]
    if gamma_old is None:
        d, q = u, s
    else:
        d, q = u + beta * d, s + beta * q
    x = alpha * d if x is None else x + alpha * d
    r = r - alpha * q
    if us is not None:
        rows = lax.broadcasted_iota(jnp.int32, (PAD, WIDTH), 0)
        own = jnp.where(rows < ROWS, us + inv_s * total[0:PAD, :], 0.0)
        ps = own if ps is None else own + beta * ps
        us = us - alpha * ps
    return gamma, alpha, us, ps, d, q, x, r


def second_kernel(
    near, far, tgt, us, inv_s, reach, own, cost, couple_hbm, factor_hbm,
    msg_out, hot_out, us_out, ps_out, scal_out, d_out, q_out, x_out, r_out,
    couple, factor, sems,
):
    copies = fetch(couple_hbm, factor_hbm, couple, factor, sems)
    want = tgt[...]
    lane = lax.broadcasted_iota(jnp.int32, (1, WIDTH), 1)
    slot = lane & (PAD - 1)
    fixed = jnp.where(slot < ROWS + 2, GAMMA, jnp.where(slot < ROWS + 4, DELTA, -1))
    sums = []
    for number, part in enumerate((near, far)):
        for chunk in range(CHIPS // 4):
            start = WIDTH * chunk
            ends = [part[start + PAD * m + 16 : start + PAD * (m + 1), :].astype(F32) for m in range(4)]
            ends = ends[0] + ends[1] + ends[2] + ends[3]
            found = (ends[12:13, :] * 64.0 + ends[13:14, :]).astype(jnp.int32)
            block = jnp.where(slot < ROWS, found, fixed)
            hot_out[number, :, start : start + WIDTH] = hot_of(want == block)
        sums.append(dot_nn(hot_out[number], part[...]))
    total = sums[0] + sums[1]
    d = cost[...]
    inv = 1.0 / d
    r = own[...]
    gamma, alpha, u_s, p_s, dn, qn, xn, rn = advance(
        total, us[...], inv_s[...], None, inv * r, d, None, None, None, r, None, None
    )
    us_out[...], ps_out[...] = u_s, p_s
    d_out[...], q_out[...], x_out[...], r_out[...] = dn, qn, xn, rn
    scal_out[0:1, :] = jnp.broadcast_to(gamma, (1, WIDTH))
    scal_out[1:2, :] = jnp.broadcast_to(alpha, (1, WIDTH))
    msg_out[...] = next_message(u_s, inv * rn, rn, d, copies, couple, factor, reach[...])


def third_kernel(
    near, far, hot, us, ps, inv_s, scal, d, q, x, r, reach, cost, couple_hbm, factor_hbm,
    msg_out, scal_out, d_out, q_out, x_out, r_out,
    couple, factor, sems,
):
    copies = fetch(couple_hbm, factor_hbm, couple, factor, sems)
    total = dot_nn(hot[0], near[...]) + dot_nn(hot[1], far[...])
    c = cost[...]
    inv = 1.0 / c
    gamma, alpha, u_s, p_s, dn, qn, xn, rn = advance(
        total, us[...], inv_s[...], ps[...], inv * r[...], c, q[...], d[...], x[...], r[...],
        scal[0:1, 0:1], scal[1:2, 0:1],
    )
    d_out[...], q_out[...], x_out[...], r_out[...] = dn, qn, xn, rn
    scal_out[0:1, :] = jnp.broadcast_to(gamma, (1, WIDTH))
    scal_out[1:2, :] = jnp.broadcast_to(alpha, (1, WIDTH))
    msg_out[...] = next_message(u_s, inv * rn, rn, c, copies, couple, factor, reach[...])


def last_kernel(near, far, hot, scal, d, q, x, r, cost, x_out, r_out):
    total = dot_nn(hot[0], near[...]) + dot_nn(hot[1], far[...])
    c = cost[...]
    found = advance(
        total, None, None, None, r[...] / c, c, q[...], d[...], x[...], r[...],
        scal[0:1, 0:1], scal[1:2, 0:1],
    )
    x_out[...], r_out[...] = found[6], found[7]


def call(kernel, shapes, *args, scalars=0, weights=()):
    vmem = pl.BlockSpec(memory_space=pltpu.VMEM)
    specs = [pl.BlockSpec(memory_space=pltpu.SMEM)] * scalars + [vmem] * (len(args) - scalars)
    specs += [pl.BlockSpec(memory_space=pltpu.HBM)] * len(weights)
    scratch = [pltpu.VMEM(w.shape, w.dtype) for w in weights]
    if weights:
        scratch.append(pltpu.SemaphoreType.DMA((len(weights),)))
    return pl.pallas_call(
        kernel,
        out_shape=[jax.ShapeDtypeStruct(s, t) for s, t in shapes],
        in_specs=specs,
        out_specs=[vmem] * len(shapes),
        scratch_shapes=scratch,
        compiler_params=pltpu.CompilerParams(vmem_limit_bytes=48 * 1024 * 1024),
    )(*args, *weights)


def in_hbm(*arrays):
    return [pltpu.with_memory_space_constraint(a, pltpu.HBM) for a in arrays]


def other_core(values):
    return lax.ppermute(values, "core", [(0, 1), (1, 0)])


def exchange(sent):
    copies = jnp.broadcast_to(sent[None], (CHIPS,) + sent.shape)
    near = lax.all_to_all(copies, ("x", "z", "y"), 0, 0, tiled=True).reshape(CHIPS * PAD, WIDTH)
    return near, other_core(near)


def shards(rhs, diag, couple, couple_idx, factor, pattern):
    weights = in_hbm(couple[0], factor[0])
    scen, own, msg = ((PAD, WIDTH), F32), ((OWN, WIDTH), F32), ((PAD, WIDTH), BF16)
    scal = ((2, WIDTH), F32)
    core = lax.axis_index("core")[None]
    vec = lax.axis_index("z") * 4 + lax.axis_index("y")
    sent, r, cost = call(
        opening_kernel, [((PLANE, OWN, WIDTH), BF16), own, own], core, scalars=1, weights=in_hbm(rhs, diag)
    )
    near = lax.all_to_all(sent, ("z", "y"), 0, 0, tiled=True).reshape(PLANE * OWN, WIDTH)
    far = other_core(near)

    idx = couple_idx[0]
    tgt = jnp.concatenate(
        [idx, jnp.array([GAMMA, DELTA] + [-9] * 6, jnp.int32), vec * OWN + jnp.arange(OWN)]
    )[:, None]
    spaced = jnp.tile(jnp.pad(idx, (0, PAD - ROWS)), 4)
    spaced = jnp.where(jnp.arange(WIDTH) // PAD == lax.axis_index("y"), spaced, 0)
    label = jnp.stack([spaced >> 6, spaced & 63]).astype(F32)
    place = jnp.arange(ROWS)
    reach = jnp.stack(
        [pattern[0, :, 0] * (place > 0), pattern[0, :, 1] * (place < ROWS - 1)], axis=1
    ).astype(F32)
    reach = jnp.pad(reach, ((0, PAD - ROWS), (0, 0)))

    sent, us, inv_s = call(
        first_kernel, [msg, scen, scen],
        core, near, far, tgt, label, reach, r, cost, scalars=1, weights=weights,
    )
    near, far = exchange(sent)
    sent, hot, us, ps, sc, d, q, x, r = call(
        second_kernel,
        [msg, ((2, PAD + OWN, CHIPS * PAD), BF16), scen, scen, scal, own, own, own, own],
        near, far, tgt, us, inv_s, reach, r, cost, weights=weights,
    )
    near, far = exchange(sent)
    sent, sc, d, q, x, r = call(
        third_kernel, [msg, scal, own, own, own, own],
        near, far, hot, us, ps, inv_s, sc, d, q, x, r, reach, cost, weights=weights,
    )
    near, far = exchange(sent)
    return call(last_kernel, [own, own], near, far, hot, sc, d, q, x, r, cost)


def solution(mesh):
    fine = Mesh(np.array(mesh.devices).reshape(4, 2, 4, 4), ("x", "core", "z", "y"))
    vec, scen = ("z", "y"), ("x", "core", "z", "y")
    in_specs = (
        P(vec, None),
        P(vec, None),
        P(scen, None, None, None),
        P(scen, None),
        P(scen, None, None, None, None),
        P(scen, None, None),
    )
    out_specs = (P(vec, None), P(vec, None))
    return jax.shard_map(shards, mesh=fine, in_specs=in_specs, out_specs=out_specs, check_vma=False)
```

time: 114 us -> 98.9 us (0.87)
  local copies, waits for them, and re-layouts: 6.53 us -> 1.16 us
  blocking collectives: 56 us -> 50.8 us
  Pallas kernels: 18.6 us -> 14.9 us
  waiting for transfers between devices: 10.9 us -> 12.6 us
  other arithmetic: 3.18 us -> 1.54 us
    all_to_all x3, blocking collectives: 56 us -> 50.8 us  [exchange(): lax.all_to_all(copies, ('x', 'z', 'y'), 0, 0, tiled=True)]
    unnamed x12 -> x0, local copies, waits for them, and re-layouts: 4.4 us -> none
    pallas_call x4 -> x5, Pallas kernels: 18.6 us -> 14.9 us  [call(): pl.pallas_call(kernel, out_shape=[jax.ShapeDtypeStruct(s, t) for s, t in...]
    all_to_all x1, waiting for transfers between devices: 4.56 us -> 7.55 us  [shards(): lax.all_to_all(sent, ('z', 'y'), 0, 0, tiled=True)]
    ppermute x4, waiting for transfers between devices: 6.36 us -> 5.06 us  [other_core(): return lax.ppermute(values, 'core', [(0, 1), (1, 0)])]
  transfers between devices with their start and end apart: 5 -> 5, of which waited for: 5 -> 5; matrix products, arithmetic and copies ran while one was open for 2% -> 3% of each run, Pallas kernels for 0% -> 0%
where the time goes in v2:
time: 98.9 us; the launch traced here: 98.4 us
  blocking collectives  50.8 us (51%)
  starting transfers between devices  16.7 us (17%)
  Pallas kernels  14.9 us (15%)
  waiting for transfers between devices  12.6 us (13%)
  other arithmetic  1.54 us (2%)
  local copies, waits for them, and re-layouts  1.16 us (1%)
    all_to_all x3, blocking collectives, exchange(): lax.all_to_all(copies, ('x', 'z', 'y'), 0, 0, tiled=True)  50.8 us
    pallas_call x5, Pallas kernels, call(): pl.pallas_call(kernel, out_shape=[jax.ShapeDtypeStruct(s, t) for s, t in...  14.9 us
    all_to_all x1, starting transfers between devices, shards(): lax.all_to_all(sent, ('z', 'y'), 0, 0, tiled=True)  8.61 us
    ppermute x4, starting transfers between devices, other_core(): return lax.ppermute(values, 'core', [(0, 1), (1, 0)])  8.1 us
    all_to_all x1, waiting for transfers between devices, shards(): lax.all_to_all(sent, ('z', 'y'), 0, 0, tiled=True)  7.55 us
    ppermute x4, waiting for transfers between devices, other_core(): return lax.ppermute(values, 'core', [(0, 1), (1, 0)])  5.06 us
  transfers between devices with their start and end apart: 5, of which 5 were waited for; matrix products, arithmetic and copies ran while one was open for 3% of the time, Pallas kernels for 0%

profile of v2, /device:TPU:1, one launch (start us, length us, event | category | flops | bytes accessed | tf_op | source)
XLA Modules:
  0.0 98.4 jit_solution(7909556581172675059)
XLA Ops:
  0.6 1.6 %shard_map.86 = (bf16[16,96,128]{2,1,0:T(8,128)(2,1)}, f32[96,128]{1,0:T(8,128)S(1)}, f32[96,128]{1,0:T(8,128)S(1)}) custom-call(s32[1]{0:T(128)} %bitcast.core_ref, f32[96,128]{1,0:T(8,128)} %rhs_hbm.1, f32[96,128]{1,0:T(8,128)} %diag_hbm.1), custom_call_target="tpu_custom_call" | custom-call | tf_op jit(solution)/shard_map/pallas_call | solution.py:233
  2.3 8.6 %all-to-all-start = ((bf16[16,96,128]{2,1,0:T(8,128)(2,1)}), bf16[16,96,128]{2,1,0:T(8,128)(2,1)S(1)}, u32[]{:S(2)}, u32[]{:S(2)}) async-start(bf16[16,96,128]{2,1,0:T(8,128)(2,1)} %get-tuple-element.23), calls=%async_computation | async-start | bytes 786432 | tf_op jit(solution)/shard_map/all_to_all | solution.py:266
  10.9 0.8 compare_select_fusion.1
  11.7 0.7 pad.8
  12.3 0.1 tile.10
  12.4 0.1 copy.16
  12.5 7.5 %all-to-all-done = bf16[16,96,128]{2,1,0:T(8,128)(2,1)S(1)} async-done(((bf16[16,96,128]{2,1,0:T(8,128)(2,1)}), bf16[16,96,128]{2,1,0:T(8,128)(2,1)S(1)}, u32[]{:S(2)}, u32[]{:S(2)}) %all-to-all-start) | async-done | bytes 393248 | tf_op jit(solution)/shard_map/all_to_all | solution.py:266
  20.1 1.9 %collective-permute-start = (bf16[1536,128]{1,0:T(8,128)(2,1)S(1)}, bf16[1536,128]{1,0:T(8,128)(2,1)S(1)}, u32[]{:S(2)}, u32[]{:S(2)}) collective-permute-start(bf16[1536,128]{1,0:T(8,128)(2,1)S(1)} %bitcast.20), channel_id=1, source_target_pairs={{0,16},{16,0},{1,17},{17,1},{2,18},{18,2},{3,19},{19,3},{4,20},{20... | collective-permute-start | bytes 1179656 | tf_op jit(solution)/shard_map/ppermute | solution.py:248
  21.9 0.7 add_bitcast_fusion
  22.7 0.1 copy.17.tgt
  22.8 0.5 collective-permute-done.far
  23.3 3.9 %shard_map.87 = (bf16[32,128]{1,0:T(8,128)(2,1)S(1)}, f32[32,128]{1,0:T(8,128)S(1)}, f32[32,128]{1,0:T(8,128)S(1)}) custom-call(s32[1]{0:T(128)} %bitcast.core_ref, bf16[1536,128]{1,0:T(8,128)(2,1)S(1)} %bitcast.21, bf16[1536,128]{1,0:T(8,128)(2,1)S(1)} %collective-permute-done.far, s32[128,1]{1,0:T(8,128)S(1)} %copy.17.tgt, ...), custom_call_target="tpu_custom_call" | custom-call | tf_op jit(solution)/shard_map/pallas_call | solution.py:233
  27.3 18.0 %all_to_all.20 = bf16[64,32,128]{2,1,0:T(8,128)(2,1)S(1)} all-to-all(bf16[64,32,128]{2,1,0:T(8,128)(2,1)S(1)} %broadcast_in_dim.14), channel_id=1, replica_groups=mesh['x'=4,'core'=2,'z'=4,'y'=4] {'x','z','y'}, dimensions={0} | all-to-all | bytes 1048576 | tf_op jit(solution)/shard_map/all_to_all | solution.py:253
  45.2 2.1 %collective-permute-start.1 = (bf16[2048,128]{1,0:T(8,128)(2,1)S(1)}, bf16[2048,128]{1,0:T(8,128)(2,1)S(1)}, u32[]{:S(2)}, u32[]{:S(2)}) collective-permute-start(bf16[2048,128]{1,0:T(8,128)(2,1)S(1)} %bitcast.16), channel_id=1, source_target_pairs={{0,16},{16,0},{1,17},{17,1},{2,18},{18,2},{3,19},{19,3},{4,20},{20... | collective-permute-start | bytes 1572872 | tf_op jit(solution)/shard_map/ppermute | solution.py:248
  47.3 1.5 %collective-permute-done.1.far = bf16[2048,128]{1,0:T(8,128)(2,1)S(1)} collective-permute-done((bf16[2048,128]{1,0:T(8,128)(2,1)S(1)}, bf16[2048,128]{1,0:T(8,128)(2,1)S(1)}, u32[]{:S(2)}, u32[]{:S(2)}) %collective-permute-start.1) | collective-permute-done | bytes 524320 | tf_op jit(solution)/shard_map/ppermute | solution.py:248
  48.9 4.3 %shard_map.88 = (bf16[32,128]{1,0:T(8,128)(2,1)S(1)}, bf16[2,128,2048]{2,1,0:T(8,128)(2,1)S(1)}, f32[32,128]{1,0:T(8,128)S(1)}, f32[32,128]{1,0:T(8,128)S(1)}, f...) custom-call(bf16[2048,128]{1,0:T(8,128)(2,1)S(1)} %bitcast.17, ...), custom_call_target="tpu_custom_call" | custom-call | tf_op jit(solution)/shard_map/pallas_call | solution.py:233
  53.3 16.4 %all_to_all.21 = bf16[64,32,128]{2,1,0:T(8,128)(2,1)S(1)} all-to-all(bf16[64,32,128]{2,1,0:T(8,128)(2,1)S(1)} %broadcast_in_dim.15), channel_id=1, replica_groups=mesh['x'=4,'core'=2,'z'=4,'y'=4] {'x','z','y'}, dimensions={0} | all-to-all | bytes 1048576 | tf_op jit(solution)/shard_map/all_to_all | solution.py:253
  69.7 2.1 %collective-permute-start.2 = (bf16[2048,128]{1,0:T(8,128)(2,1)S(1)}, bf16[2048,128]{1,0:T(8,128)(2,1)S(1)}, u32[]{:S(2)}, u32[]{:S(2)}) collective-permute-start(bf16[2048,128]{1,0:T(8,128)(2,1)S(1)} %bitcast.14), channel_id=1, source_target_pairs={{0,16},{16,0},{1,17},{17,1},{2,18},{18,2},{3,19},{19,3},{4,20},{20... | collective-permute-start | bytes 1572872 | tf_op jit(solution)/shard_map/ppermute | solution.py:248
  71.8 1.5 %collective-permute-done.2.far = bf16[2048,128]{1,0:T(8,128)(2,1)S(1)} collective-permute-done((bf16[2048,128]{1,0:T(8,128)(2,1)S(1)}, bf16[2048,128]{1,0:T(8,128)(2,1)S(1)}, u32[]{:S(2)}, u32[]{:S(2)}) %collective-permute-start.2) | collective-permute-done | bytes 524320 | tf_op jit(solution)/shard_map/ppermute | solution.py:248
  73.3 3.8 %shard_map.89 = (bf16[32,128]{1,0:T(8,128)(2,1)S(1)}, f32[2,128]{1,0:T(2,128)S(1)}, f32[96,128]{1,0:T(8,128)S(1)}, f32[96,128]{1,0:T(8,128)S(1)}, f32[96,128]{1,0:T(8,128)S(1)}, /*index=5*/f32[96,128]{1,0:T(8,128)S(1)}) custom-call(bf16[2048,128]{1,0:T(8,128)(2,1)S(1)} %bitcast.15, bf16[2048,128]{1,0:T(8,128)(2,1)S(1)} %collective-permute-done.2.far, ...), custom_call_target="tpu_custom_call" | custom-call | tf_op jit(solution)/shard_map/pallas_call | solution.py:233
  77.2 16.4 %all_to_all.22 = bf16[64,32,128]{2,1,0:T(8,128)(2,1)S(1)} all-to-all(bf16[64,32,128]{2,1,0:T(8,128)(2,1)S(1)} %broadcast_in_dim.30), channel_id=1, replica_groups=mesh['x'=4,'core'=2,'z'=4,'y'=4] {'x','z','y'}, dimensions={0} | all-to-all | bytes 1048576 | tf_op jit(solution)/shard_map/all_to_all | solution.py:253
  93.6 2.1 %collective-permute-start.3 = (bf16[2048,128]{1,0:T(8,128)(2,1)S(1)}, bf16[2048,128]{1,0:T(8,128)(2,1)S(1)}, u32[]{:S(2)}, u32[]{:S(2)}) collective-permute-start(bf16[2048,128]{1,0:T(8,128)(2,1)S(1)} %bitcast.18), channel_id=1, source_target_pairs={{0,16},{16,0},{1,17},{17,1},{2,18},{18,2},{3,19},{19,3},{4,20},{20... | collective-permute-start | bytes 1572872 | tf_op jit(solution)/shard_map/ppermute | solution.py:248
  95.7 1.5 %collective-permute-done.3.far = bf16[2048,128]{1,0:T(8,128)(2,1)S(1)} collective-permute-done((bf16[2048,128]{1,0:T(8,128)(2,1)S(1)}, bf16[2048,128]{1,0:T(8,128)(2,1)S(1)}, u32[]{:S(2)}, u32[]{:S(2)}) %collective-permute-start.3) | collective-permute-done | bytes 524320 | tf_op jit(solution)/shard_map/ppermute | solution.py:248
  97.2 1.2 %shard_map.90 = (f32[96,128]{1,0:T(8,128)}, f32[96,128]{1,0:T(8,128)}) custom-call(bf16[2048,128]{1,0:T(8,128)(2,1)S(1)} %bitcast.19, bf16[2048,128]{1,0:T(8,128)(2,1)S(1)} %collective-permute-done.3.far, bf16[2,128,2048]{2,1,0:T(8,128)(2,1)S(1)} %get-tuple-element.30.hot, f32[2,128]{1,0:T(2,128)S(1)} %get-tuple-element.39.scal, ...), custom_call_target="tpu_custom_call" | custom-call | tf_op jit(solution)/shard_map/pallas_call | solution.py:233
  (10 shorter events, 0.3 us)
Async XLA Ops:
  2.3 17.8 %all-to-all-start = ((bf16[16,96,128]{2,1,0:T(8,128)(2,1)}), bf16[16,96,128]{2,1,0:T(8,128)(2,1)S(1)}, u32[]{:S(2)}, u32[]{:S(2)}) async-start(bf16[16,96,128]{2,1,0:T(8,128)(2,1)} %get-tuple-element.23), calls=%async_computation | async-start | bytes 786432 | tf_op jit(solution)/shard_map/all_to_all | solution.py:266
  20.1 3.2 %collective-permute-start = (bf16[1536,128]{1,0:T(8,128)(2,1)S(1)}, bf16[1536,128]{1,0:T(8,128)(2,1)S(1)}, u32[]{:S(2)}, u32[]{:S(2)}) collective-permute-start(bf16[1536,128]{1,0:T(8,128)(2,1)S(1)} %bitcast.20), channel_id=1, source_target_pairs={{0,16},{16,0},{1,17},{17,1},{2,18},{18,2},{3,19},{19,3},{4,20},{20... | collective-permute-start | bytes 1179656 | tf_op jit(solution)/shard_map/ppermute | solution.py:248
  45.2 3.6 %collective-permute-start.1 = (bf16[2048,128]{1,0:T(8,128)(2,1)S(1)}, bf16[2048,128]{1,0:T(8,128)(2,1)S(1)}, u32[]{:S(2)}, u32[]{:S(2)}) collective-permute-start(bf16[2048,128]{1,0:T(8,128)(2,1)S(1)} %bitcast.16), channel_id=1, source_target_pairs={{0,16},{16,0},{1,17},{17,1},{2,18},{18,2},{3,19},{19,3},{4,20},{20... | collective-permute-start | bytes 1572872 | tf_op jit(solution)/shard_map/ppermute | solution.py:248
  69.7 3.6 %collective-permute-start.2 = (bf16[2048,128]{1,0:T(8,128)(2,1)S(1)}, bf16[2048,128]{1,0:T(8,128)(2,1)S(1)}, u32[]{:S(2)}, u32[]{:S(2)}) collective-permute-start(bf16[2048,128]{1,0:T(8,128)(2,1)S(1)} %bitcast.14), channel_id=1, source_target_pairs={{0,16},{16,0},{1,17},{17,1},{2,18},{18,2},{3,19},{19,3},{4,20},{20... | collective-permute-start | bytes 1572872 | tf_op jit(solution)/shard_map/ppermute | solution.py:248
  93.6 3.6 %collective-permute-start.3 = (bf16[2048,128]{1,0:T(8,128)(2,1)S(1)}, bf16[2048,128]{1,0:T(8,128)(2,1)S(1)}, u32[]{:S(2)}, u32[]{:S(2)}) collective-permute-start(bf16[2048,128]{1,0:T(8,128)(2,1)S(1)} %bitcast.18), channel_id=1, source_target_pairs={{0,16},{16,0},{1,17},{17,1},{2,18},{18,2},{3,19},{19,3},{4,20},{20... | collective-permute-start | bytes 1572872 | tf_op jit(solution)/shard_map/ppermute | solution.py:248

commit v3 on v2

v3 whole, which is shorter than its diff:
```python
import jax
import jax.numpy as jnp
import numpy as np
from jax import lax
from jax.experimental import pallas as pl
from jax.experimental.pallas import tpu as pltpu
from jax.sharding import Mesh
from jax.sharding import PartitionSpec as P

ROWS = 24
PAD = 32
OWN = 96
HALF = OWN // 2
WIDTH = 128
CHIPS = 64
PLANE = 16
BANDS = 5
GAMMA, DELTA = 4000, 4001
INVERSE = 2048
F32, BF16 = jnp.float32, jnp.bfloat16


def dot_nn(a, b):
    return lax.dot_general(a, b, (((1,), (0,)), ((), ())), preferred_element_type=F32)


def dot_nt(a, b):
    return lax.dot_general(a, b, (((1,), (1,)), ((), ())), preferred_element_type=F32)


def split(values):
    high = values.astype(BF16).astype(F32)
    return high, values - high


def hot_of(mask):
    return mask.astype(F32).astype(BF16)


def only_row(values, r):
    rows = lax.broadcasted_iota(jnp.int32, (PAD, WIDTH), 0)
    return jnp.where(rows == r, values, 0.0).astype(BF16)


def scenario_lift(y, normal):
    spread = jnp.zeros((PAD, BANDS * WIDTH), F32)
    for r in range(0, ROWS, 2):
        pair = jnp.concatenate([only_row(y, r), only_row(y, r + 1)], axis=1)
        spread += dot_nn(pair, normal[r : r + 2].reshape(2 * WIDTH, BANDS * WIDTH))
    lifted = spread[:, 2 * WIDTH : 3 * WIDTH]
    for band in (0, 1, 3, 4):
        part = spread[:, band * WIDTH : (band + 1) * WIDTH]
        lifted += pltpu.roll(part, (band - 2) % PAD, 0)
    return lifted


def message(lifted, gamma, delta, extra):
    rows = lax.broadcasted_iota(jnp.int32, (PAD, WIDTH), 0)
    out = jnp.where(rows < ROWS, lifted, 0.0)
    for place, line in enumerate(split(gamma) + split(delta) + tuple(extra)):
        out = jnp.where(rows == ROWS + place, jnp.broadcast_to(line, out.shape), out)
    return out.astype(BF16)


def column_sum(values):
    return jnp.sum(values, axis=0, keepdims=True)


def next_message(us, u, r, cost, normal, extra=()):
    lifted = scenario_lift(us, normal)
    gamma = column_sum(r * u) * 0.125
    delta = column_sum(cost * u * u) * 0.125 + column_sum(us * lifted)
    return message(lifted, gamma, delta, extra)


def opening_kernel(ids, rhs_hbm, diag_hbm, msg_out, r_out, cost_out, rhs, diag, sems):
    copies = (
        pltpu.make_async_copy(rhs_hbm, rhs, sems.at[0]),
        pltpu.make_async_copy(diag_hbm, diag, sems.at[1]),
    )
    for copy in copies:
        copy.start()
    for copy in copies:
        copy.wait()
    r_out[...], cost_out[...] = rhs[...], diag[...]
    mine = pl.ds(pl.multiple_of(ids[0] * HALF, HALF), HALF)
    inverse = 1.0 / diag[mine, :]
    u = (rhs[mine, :] * inverse).astype(BF16)
    inverse = inverse.astype(BF16)
    for place in range(PLANE):
        msg_out[place, 0:HALF, :] = u
        msg_out[place, HALF:OWN, :] = inverse


def normal_kernel(
    ids, idx, pattern, couple_hbm, factor_hbm, normal, tgt, label, couple, factor, prod, flip, sems
):
    third = ROWS // 3
    copies = [pltpu.make_async_copy(couple_hbm, couple, sems.at[0])]
    for part in range(3):
        rows = pl.ds(part * third, third)
        copies.append(
            pltpu.make_async_copy(factor_hbm.at[rows], factor.at[rows], sems.at[1 + part])
        )
    for copy in copies:
        copy.start()

    square = (ROWS, ROWS)
    same = lax.broadcasted_iota(jnp.int32, square, 0) == lax.broadcasted_iota(jnp.int32, square, 1)
    column = jnp.where(same, jnp.broadcast_to(idx[...], square), 0)
    column = jnp.sum(column.astype(F32), axis=1, keepdims=True).astype(jnp.int32)
    rows = lax.broadcasted_iota(jnp.int32, (PAD + OWN, WIDTH), 0)
    fixed = jnp.where(rows < ROWS + 2, rows - ROWS + GAMMA, -9)
    fixed = jnp.where(rows < PAD, fixed, rows - PAD + ids[2] * OWN)
    tgt[...] = fixed
    column = jnp.broadcast_to(column, (ROWS, WIDTH))
    tgt[0:ROWS, :] = column
    lanes = lax.broadcasted_iota(jnp.int32, (ROWS, WIDTH), 1)
    place = lax.broadcasted_iota(jnp.int32, (ROWS, WIDTH), 0) + PAD * ids[1]
    for line, values in enumerate((column >> 6, column & 63)):
        label[line : line + 1, :] = column_sum(jnp.where(lanes == place, values, 0).astype(F32))

    side = pattern[...].astype(F32)
    zeros = jnp.zeros((WIDTH, WIDTH), BF16)
    copies[0].wait()
    for r in range(ROWS):
        if r % third == 0:
            copies[1 + r // third].wait()
        for k in range(3):
            c = r + k - 1
            if not 0 <= c < ROWS:
                continue
            block = dot_nn(factor[r, k], couple[c])
            if k != 1:
                block = block * side[r : r + 1, k // 2 : k // 2 + 1]
            block = block.astype(BF16)
            prod[r, k] = block
            flip[c, :, (2 - k) * WIDTH : (3 - k) * WIDTH] = block.T
    for d in range(ROWS):
        for band in range(BANDS):
            c = d + band - 2
            if not 0 <= c < ROWS:
                normal[d, :, band * WIDTH : (band + 1) * WIDTH] = zeros
                continue
            if band < 2:
                continue
            terms = [r for r in (d - 1, d, d + 1) if 0 <= r < ROWS and abs(r - c) <= 1]
            first = terms[0] - d + 1
            left = flip[d, :, first * WIDTH : (first + len(terms)) * WIDTH]
            right = jnp.concatenate([prod[r, c - r + 1] for r in terms], axis=0)
            block = dot_nn(left, right).astype(BF16)
            normal[d, :, band * WIDTH : (band + 1) * WIDTH] = block
            if c != d:
                normal[c, :, (4 - band) * WIDTH : (5 - band) * WIDTH] = block.T


def first_kernel(ids, near, far, tgt, label, own, cost, normal, msg_out, us_out, inv_out):
    want = tgt[0:PAD, 0:1]
    want = jnp.concatenate([want, want + INVERSE], axis=0)
    found = jnp.zeros((2 * PAD, WIDTH), F32)
    for part, which in ((near, ids[0]), (far, 1 - ids[0])):
        place = lax.broadcasted_iota(jnp.int32, (1, PLANE * OWN), 1)
        member = place - OWN * ((place * 683) >> 16)
        block = place + HALF * which + jnp.where(member < HALF, 0, INVERSE - HALF)
        found += dot_nn(hot_of(want == block), part[...])
    us = found[0:PAD, :]
    us_out[...], inv_out[...] = us, found[PAD:, :]
    r, d = own[...], cost[...]
    msg_out[...] = next_message(us, r * (1.0 / d), r, d, normal, (label[0:1, :], label[1:2, :]))


def label_sum(part, tgt, hot_out, sum_out):
    want = tgt[...]
    lane = lax.broadcasted_iota(jnp.int32, (1, WIDTH), 1)
    slot = lane & (PAD - 1)
    fixed = jnp.where(slot < ROWS + 2, GAMMA, jnp.where(slot < ROWS + 4, DELTA, -1))
    for chunk in range(CHIPS // 4):
        start = WIDTH * chunk
        ends = [part[start + PAD * m + 16 : start + PAD * (m + 1), :].astype(F32) for m in range(4)]
        ends = ends[0] + ends[1] + ends[2] + ends[3]
        found = (ends[12:13, :] * 64.0 + ends[13:14, :]).astype(jnp.int32)
        block = jnp.where(slot < ROWS, found, fixed)
        hot_out[:, start : start + WIDTH] = hot_of(want == block)
    sum_out[...] = dot_nn(hot_out[...], part[...])


def near_sum(part, hot, sum_out):
    sum_out[...] = dot_nn(hot[...], part[...])


def advance(total, us, inv_s, ps, u, cost, q, d, x, r, gamma_old, alpha_old):
    gamma = jnp.sum(total[ROWS : ROWS + 1, :], axis=1, keepdims=True)
    delta = jnp.sum(total[ROWS + 1 : ROWS + 2, :], axis=1, keepdims=True)
    if gamma_old is None:
        alpha = gamma / delta
    else:
        beta = gamma / gamma_old
        alpha = gamma / (delta - beta * gamma / alpha_old)
    s = cost * u + total[PAD:, :]
    if gamma_old is None:
        d, q = u, s
    else:
        d, q = u + beta * d, s + beta * q
    x = alpha * d if x is None else x + alpha * d
    r = r - alpha * q
    if us is not None:
        rows = lax.broadcasted_iota(jnp.int32, (PAD, WIDTH), 0)
        own = jnp.where(rows < ROWS, us + inv_s * total[0:PAD, :], 0.0)
        ps = own if ps is None else own + beta * ps
        us = us - alpha * ps
    return gamma, alpha, us, ps, d, q, x, r


def second_kernel(
    far, tgt, half, us, inv_s, own, cost, normal,
    msg_out, hot_out, us_out, ps_out, scal_out, d_out, q_out, x_out, r_out, other,
):
    label_sum(far, tgt, hot_out, other)
    total = half[...] + other[...]
    d = cost[...]
    inv = 1.0 / d
    r = own[...]
    gamma, alpha, u_s, p_s, dn, qn, xn, rn = advance(
        total, us[...], inv_s[...], None, inv * r, d, None, None, None, r, None, None
    )
    us_out[...], ps_out[...] = u_s, p_s
    d_out[...], q_out[...], x_out[...], r_out[...] = dn, qn, xn, rn
    scal_out[0:1, :] = jnp.broadcast_to(gamma, (1, WIDTH))
    scal_out[1:2, :] = jnp.broadcast_to(alpha, (1, WIDTH))
    msg_out[...] = next_message(u_s, inv * rn, rn, d, normal)


def third_kernel(
    far, hot, half, us, ps, inv_s, scal, d, q, x, r, cost, normal,
    msg_out, scal_out, d_out, q_out, x_out, r_out,
):
    total = half[...] + dot_nn(hot[...], far[...])
    c = cost[...]
    inv = 1.0 / c
    gamma, alpha, u_s, p_s, dn, qn, xn, rn = advance(
        total, us[...], inv_s[...], ps[...], inv * r[...], c, q[...], d[...], x[...], r[...],
        scal[0:1, 0:1], scal[1:2, 0:1],
    )
    d_out[...], q_out[...], x_out[...], r_out[...] = dn, qn, xn, rn
    scal_out[0:1, :] = jnp.broadcast_to(gamma, (1, WIDTH))
    scal_out[1:2, :] = jnp.broadcast_to(alpha, (1, WIDTH))
    msg_out[...] = next_message(u_s, inv * rn, rn, c, normal)


def last_kernel(far, hot, half, scal, d, q, x, r, cost, x_out, r_out):
    total = half[...] + dot_nn(hot[...], far[...])
    c = cost[...]
    found = advance(
        total, None, None, None, r[...] / c, c, q[...], d[...], x[...], r[...],
        scal[0:1, 0:1], scal[1:2, 0:1],
    )
    x_out[...], r_out[...] = found[6], found[7]


def call(kernel, shapes, *args, scalars=0, weights=(), scratch=(), sems=0):
    vmem = pl.BlockSpec(memory_space=pltpu.VMEM)
    specs = [pl.BlockSpec(memory_space=pltpu.SMEM)] * scalars + [vmem] * (len(args) - scalars)
    specs += [pl.BlockSpec(memory_space=pltpu.HBM)] * len(weights)
    scratch = [pltpu.VMEM(s, t) for s, t in scratch]
    if sems:
        scratch.append(pltpu.SemaphoreType.DMA((sems,)))
    return pl.pallas_call(
        kernel,
        out_shape=[jax.ShapeDtypeStruct(s, t) for s, t in shapes],
        in_specs=specs,
        out_specs=[vmem] * len(shapes),
        scratch_shapes=scratch,
        compiler_params=pltpu.CompilerParams(vmem_limit_bytes=32 * 1024 * 1024),
    )(*args, *weights)


def in_hbm(*arrays):
    return [pltpu.with_memory_space_constraint(a, pltpu.HBM) for a in arrays]


def other_core(values):
    return lax.ppermute(values, "core", [(0, 1), (1, 0)])


def exchange(sent):
    copies = jnp.broadcast_to(sent[None], (CHIPS,) + sent.shape)
    near = lax.all_to_all(copies, ("x", "z", "y"), 0, 0, tiled=True).reshape(CHIPS * PAD, WIDTH)
    return near, other_core(near)


def shards(rhs, diag, couple, couple_idx, factor, pattern):
    scen, own, msg = ((PAD, WIDTH), F32), ((OWN, WIDTH), F32), ((PAD, WIDTH), BF16)
    scal, sums = ((2, WIDTH), F32), ((PAD + OWN, WIDTH), F32)
    hots = ((PAD + OWN, CHIPS * PAD), BF16)
    vec = lax.axis_index("z") * 4 + lax.axis_index("y")
    ids = jnp.stack([lax.axis_index("core"), lax.axis_index("y"), vec]).astype(jnp.int32)
    sent, r, cost = call(
        opening_kernel, [((PLANE, OWN, WIDTH), BF16), own, own],
        ids, scalars=1, weights=in_hbm(rhs, diag), scratch=[own, own], sems=2,
    )
    near = lax.all_to_all(sent, ("z", "y"), 0, 0, tiled=True).reshape(PLANE * OWN, WIDTH)
    far = other_core(near)
    block = (ROWS, WIDTH, WIDTH)
    triple, wide = (ROWS, 3, WIDTH, WIDTH), (ROWS, WIDTH, 3 * WIDTH)
    normal, tgt, label = call(
        normal_kernel,
        [((ROWS, WIDTH, BANDS * WIDTH), BF16), ((PAD + OWN, WIDTH), jnp.int32), scal],
        ids, couple_idx, pattern[0], scalars=1, weights=in_hbm(couple[0], factor[0]),
        scratch=[(block, BF16), (triple, BF16), (triple, BF16), (wide, BF16)], sems=4,
    )
    sent, us, inv_s = call(
        first_kernel, [msg, scen, scen], ids, near, far, tgt, label, r, cost, normal, scalars=1
    )

    near, far = exchange(sent)
    hot_near, half = call(label_sum, [hots, sums], near, tgt)
    sent, hot_far, us, ps, sc, d, q, x, r = call(
        second_kernel, [msg, hots, scen, scen, scal, own, own, own, own],
        far, tgt, half, us, inv_s, r, cost, normal, scratch=[sums],
    )
    near, far = exchange(sent)
    half = call(near_sum, [sums], near, hot_near)[0]
    sent, sc, d, q, x, r = call(
        third_kernel, [msg, scal, own, own, own, own],
        far, hot_far, half, us, ps, inv_s, sc, d, q, x, r, cost, normal,
    )
    near, far = exchange(sent)
    half = call(near_sum, [sums], near, hot_near)[0]
    return call(last_kernel, [own, own], far, hot_far, half, sc, d, q, x, r, cost)


def solution(mesh):
    fine = Mesh(np.array(mesh.devices).reshape(4, 2, 4, 4), ("x", "core", "z", "y"))
    vec, scen = ("z", "y"), ("x", "core", "z", "y")
    in_specs = (
        P(vec, None),
        P(vec, None),
        P(scen, None, None, None),
        P(scen, None),
        P(scen, None, None, None, None),
        P(scen, None, None),
    )
    out_specs = (P(vec, None), P(vec, None))
    return jax.shard_map(shards, mesh=fine, in_specs=in_specs, out_specs=out_specs, check_vma=False)
```

time: 98.9 us -> 94.5 us (0.956)
  blocking collectives: 50.8 us -> 68.6 us
  waiting for transfers between devices: 12.6 us -> 3.64 us
  starting transfers between devices: 16.7 us -> 7.83 us
  Pallas kernels: 14.9 us -> 11.6 us
  other arithmetic: 1.54 us -> 0.08 us
    all_to_all x0 -> x1, blocking collectives: none -> 17.6 us  [shards(): lax.all_to_all(sent, ('z', 'y'), 0, 0, tiled=True)]
    all_to_all x1 -> x0, starting transfers between devices: 8.61 us -> none  [shards(): lax.all_to_all(sent, ('z', 'y'), 0, 0, tiled=True)]
    all_to_all x1 -> x0, waiting for transfers between devices: 7.55 us -> none  [shards(): lax.all_to_all(sent, ('z', 'y'), 0, 0, tiled=True)]
    pallas_call x5 -> x9, Pallas kernels: 14.9 us -> 11.6 us  [call(): pl.pallas_call(kernel, out_shape=[jax.ShapeDtypeStruct(s, t) for s, t in...]
    ppermute x4, waiting for transfers between devices: 5.06 us -> 3.64 us  [other_core(): return lax.ppermute(values, 'core', [(0, 1), (1, 0)])]
  transfers between devices with their start and end apart: 5 -> 4, of which waited for: 5 -> 3; matrix products, arithmetic and copies ran while one was open for 3% -> 1% of each run, Pallas kernels for 0% -> 6%
where the time goes in v3:
time: 94.5 us; the launch traced here: 94.1 us
  blocking collectives  68.6 us (73%)
  Pallas kernels  11.6 us (12%)
  starting transfers between devices  7.83 us (8%)
  waiting for transfers between devices  3.64 us (4%)
  local copies, waits for them, and re-layouts  1.62 us (2%)
    all_to_all x3, blocking collectives, exchange(): lax.all_to_all(copies, ('x', 'z', 'y'), 0, 0, tiled=True)  51 us
    all_to_all x1, blocking collectives, shards(): lax.all_to_all(sent, ('z', 'y'), 0, 0, tiled=True)  17.6 us
    pallas_call x9, Pallas kernels, call(): pl.pallas_call(kernel, out_shape=[jax.ShapeDtypeStruct(s, t) for s, t in...  11.6 us
    ppermute x4, starting transfers between devices, other_core(): return lax.ppermute(values, 'core', [(0, 1), (1, 0)])  7.83 us
    ppermute x4, waiting for transfers between devices, other_core(): return lax.ppermute(values, 'core', [(0, 1), (1, 0)])  3.64 us
  transfers between devices with their start and end apart: 4, of which 3 were waited for; matrix products, arithmetic and copies ran while one was open for 1% of the time, Pallas kernels for 6%

profile of v3, /device:TPU:1, one launch (start us, length us, event | category | flops | bytes accessed | tf_op | source)
XLA Modules:
  0.0 94.1 jit_solution(10796528885790635667)
XLA Ops:
  0.6 0.1 pad_add_fusion.ids
  0.7 1.4 %shard_map.77 = (bf16[16,96,128]{2,1,0:T(8,128)(2,1)S(1)}, f32[96,128]{1,0:T(8,128)S(1)}, f32[96,128]{1,0:T(8,128)S(1)}) custom-call(s32[3]{0:T(128)S(1)} %pad_add_fusion.ids, f32[96,128]{1,0:T(8,128)} %rhs_hbm.1, f32[96,128]{1,0:T(8,128)} %diag_hbm.1), custom_call_target="tpu_custom_call" | custom-call | tf_op jit(solution)/shard_map/pallas_call | solution.py:267
  2.1 17.6 %all_to_all.20 = bf16[16,96,128]{2,1,0:T(8,128)(2,1)S(1)} all-to-all(bf16[16,96,128]{2,1,0:T(8,128)(2,1)S(1)} %get-tuple-element.28), channel_id=1, replica_groups=mesh['x'=4,'core'=2,'z'=4,'y'=4] {'z','y'}, dimensions={0} | all-to-all | bytes 786432 | tf_op jit(solution)/shard_map/all_to_all | solution.py:301
  19.7 1.9 %collective-permute-start = (bf16[1536,128]{1,0:T(8,128)(2,1)S(1)}, bf16[1536,128]{1,0:T(8,128)(2,1)S(1)}, u32[]{:S(2)}, u32[]{:S(2)}) collective-permute-start(bf16[1536,128]{1,0:T(8,128)(2,1)S(1)} %bitcast.16), channel_id=1, source_target_pairs={{0,16},{16,0},{1,17},{17,1},{2,18},{18,2},{3,19},{19,3},{4,20},{20... | collective-permute-start | bytes 1179656 | tf_op jit(solution)/shard_map/ppermute | solution.py:282
  21.6 0.8 copy.8.pattern
  22.3 0.7 copy-done
  23.0 4.5 %shard_map.78 = (bf16[24,128,640]{2,1,0:T(8,128)(2,1)S(1)}, s32[128,128]{1,0:T(8,128)S(1)}, f32[2,128]{1,0:T(2,128)S(1)}) custom-call(s32[3]{0:T(128)S(1)} %pad_add_fusion.ids, s32[1,24]{1,0:T(1,128)S(1)} %copy-done, s32[24,2]{1,0:T(8,128)S(1)} %copy.8.pattern, bf16[24,128,128]{2,1,0:T(8,128)(2,1)} %bitcast.19, bf16[24,3,128,128]{3,2,1,0:T(8,128)(2,1)} %bitcast.18), custom_call_target="tpu_custom_call" | custom-call | tf_op jit(solution)/shard_map/pallas_call | solution.py:267
  27.5 1.5 %shard_map.79 = (bf16[32,128]{1,0:T(8,128)(2,1)S(1)}, f32[32,128]{1,0:T(8,128)S(1)}, f32[32,128]{1,0:T(8,128)S(1)}) custom-call(s32[3]{0:T(128)S(1)} %pad_add_fusion.ids, bf16[1536,128]{1,0:T(8,128)(2,1)S(1)} %bitcast.17, bf16[1536,128]{1,0:T(8,128)(2,1)S(1)} %collective-permute-done.far, s32[128,128]{1,0:T(8,128)S(1)} %get-tuple-element.29.tgt, ...), custom_call_target="tpu_custom_call" | custom-call | tf_op jit(solution)/shard_map/pallas_call | solution.py:267
  29.1 18.2 %all_to_all.21 = bf16[64,32,128]{2,1,0:T(8,128)(2,1)S(1)} all-to-all(bf16[64,32,128]{2,1,0:T(8,128)(2,1)S(1)} %broadcast_in_dim.6), channel_id=1, replica_groups=mesh['x'=4,'core'=2,'z'=4,'y'=4] {'x','z','y'}, dimensions={0} | all-to-all | bytes 1048576 | tf_op jit(solution)/shard_map/all_to_all | solution.py:287
  47.3 1.8 %collective-permute-start.1 = (bf16[2048,128]{1,0:T(8,128)(2,1)S(1)}, bf16[2048,128]{1,0:T(8,128)(2,1)S(1)}, u32[]{:S(2)}, u32[]{:S(2)}) collective-permute-start(bf16[2048,128]{1,0:T(8,128)(2,1)S(1)} %bitcast.10), channel_id=1, source_target_pairs={{0,16},{16,0},{1,17},{17,1},{2,18},{18,2},{3,19},{19,3},{4,20},{20... | collective-permute-start | bytes 1572872 | tf_op jit(solution)/shard_map/ppermute | solution.py:282
  49.1 0.4 shard_map.80
  49.5 1.2 %collective-permute-done.1.far = bf16[2048,128]{1,0:T(8,128)(2,1)S(1)} collective-permute-done((bf16[2048,128]{1,0:T(8,128)(2,1)S(1)}, bf16[2048,128]{1,0:T(8,128)(2,1)S(1)}, u32[]{:S(2)}, u32[]{:S(2)}) %collective-permute-start.1) | collective-permute-done | bytes 524320 | tf_op jit(solution)/shard_map/ppermute | solution.py:282
  50.7 1.1 %shard_map.81 = (bf16[32,128]{1,0:T(8,128)(2,1)S(1)}, bf16[128,2048]{1,0:T(8,128)(2,1)S(1)}, f32[32,128]{1,0:T(8,128)S(1)}, f32[32,128]{1,0:T(8,128)S(1)}, f32[2...) custom-call(bf16[2048,128]{1,0:T(8,128)(2,1)S(1)} %collective-permut, ...), custom_call_target="tpu_custom_call" | custom-call | tf_op jit(solution)/shard_map/pallas_call | solution.py:267
  51.8 0.1 broadcast_in_dim.7
  51.9 16.4 %all_to_all.22 = bf16[64,32,128]{2,1,0:T(8,128)(2,1)S(1)} all-to-all(bf16[64,32,128]{2,1,0:T(8,128)(2,1)S(1)} %broadcast_in_dim.7), channel_id=1, replica_groups=mesh['x'=4,'core'=2,'z'=4,'y'=4] {'x','z','y'}, dimensions={0} | all-to-all | bytes 1048576 | tf_op jit(solution)/shard_map/all_to_all | solution.py:287
  68.3 2.1 %collective-permute-start.2 = (bf16[2048,128]{1,0:T(8,128)(2,1)S(1)}, bf16[2048,128]{1,0:T(8,128)(2,1)S(1)}, u32[]{:S(2)}, u32[]{:S(2)}) collective-permute-start(bf16[2048,128]{1,0:T(8,128)(2,1)S(1)} %bitcast.12), channel_id=1, source_target_pairs={{0,16},{16,0},{1,17},{17,1},{2,18},{18,2},{3,19},{19,3},{4,20},{20... | collective-permute-start | bytes 1572872 | tf_op jit(solution)/shard_map/ppermute | solution.py:282
  70.4 0.3 shard_map.82.half
  70.7 1.2 %collective-permute-done.2.far = bf16[2048,128]{1,0:T(8,128)(2,1)S(1)} collective-permute-done((bf16[2048,128]{1,0:T(8,128)(2,1)S(1)}, bf16[2048,128]{1,0:T(8,128)(2,1)S(1)}, u32[]{:S(2)}, u32[]{:S(2)}) %collective-permute-start.2) | collective-permute-done | bytes 524320 | tf_op jit(solution)/shard_map/ppermute | solution.py:282
  71.9 1.1 %shard_map.83 = (bf16[32,128]{1,0:T(8,128)(2,1)S(1)}, f32[2,128]{1,0:T(2,128)S(1)}, f32[96,128]{1,0:T(8,128)S(1)}, f32[96,128]{1,0:T(8,128)S(1)}, f32[96,128]{1,0:T(8,128)S(1)}, /*index=5*/f32[96,128]{1,0:T(8,128)S(1)}) custom-call(bf16[2048,128]{1,0:T(8,128)(2,1)S(1)} %collective-permute-done.2.far, bf16[128,2048]{1,0:T(8,128)(2,1)S(1)} %get-tuple-element.39.hot, ...), custom_call_target="tpu_custom_call" | custom-call | tf_op jit(solution)/shard_map/pallas_call | solution.py:267
  73.1 16.4 %all_to_all.23 = bf16[64,32,128]{2,1,0:T(8,128)(2,1)S(1)} all-to-all(bf16[64,32,128]{2,1,0:T(8,128)(2,1)S(1)} %broadcast_in_dim.8), channel_id=1, replica_groups=mesh['x'=4,'core'=2,'z'=4,'y'=4] {'x','z','y'}, dimensions={0} | all-to-all | bytes 1048576 | tf_op jit(solution)/shard_map/all_to_all | solution.py:287
  89.5 2.1 %collective-permute-start.3 = (bf16[2048,128]{1,0:T(8,128)(2,1)S(1)}, bf16[2048,128]{1,0:T(8,128)(2,1)S(1)}, u32[]{:S(2)}, u32[]{:S(2)}) collective-permute-start(bf16[2048,128]{1,0:T(8,128)(2,1)S(1)} %bitcast.14), channel_id=1, source_target_pairs={{0,16},{16,0},{1,17},{17,1},{2,18},{18,2},{3,19},{19,3},{4,20},{20... | collective-permute-start | bytes 1572872 | tf_op jit(solution)/shard_map/ppermute | solution.py:282
  91.5 0.3 shard_map.84.half
  91.8 1.2 %collective-permute-done.3.far = bf16[2048,128]{1,0:T(8,128)(2,1)S(1)} collective-permute-done((bf16[2048,128]{1,0:T(8,128)(2,1)S(1)}, bf16[2048,128]{1,0:T(8,128)(2,1)S(1)}, u32[]{:S(2)}, u32[]{:S(2)}) %collective-permute-start.3) | collective-permute-done | bytes 524320 | tf_op jit(solution)/shard_map/ppermute | solution.py:282
  93.1 1.0 %shard_map.85 = (f32[96,128]{1,0:T(8,128)}, f32[96,128]{1,0:T(8,128)}) custom-call(bf16[2048,128]{1,0:T(8,128)(2,1)S(1)} %collective-permute-done.3.far, bf16[128,2048]{1,0:T(8,128)(2,1)S(1)} %get-tuple-element.39.hot, f32[128,128]{1,0:T(8,128)S(1)} %shard_map.84.half, f32[2,128]{1,0:T(2,128)S(1)} %get-tuple-element.49.scal, ...), custom_call_target="tpu_custom_call" | custom-call | tf_op jit(solution)/shard_map/pallas_call | solution.py:267
  (4 shorter events, 0.1 us)
Async XLA Ops:
  19.7 7.8 %collective-permute-start = (bf16[1536,128]{1,0:T(8,128)(2,1)S(1)}, bf16[1536,128]{1,0:T(8,128)(2,1)S(1)}, u32[]{:S(2)}, u32[]{:S(2)}) collective-permute-start(bf16[1536,128]{1,0:T(8,128)(2,1)S(1)} %bitcast.16), channel_id=1, source_target_pairs={{0,16},{16,0},{1,17},{17,1},{2,18},{18,2},{3,19},{19,3},{4,20},{20... | collective-permute-start | bytes 1179656 | tf_op jit(solution)/shard_map/ppermute | solution.py:282
  22.3 0.7 copy-start
  47.3 3.4 %collective-permute-start.1 = (bf16[2048,128]{1,0:T(8,128)(2,1)S(1)}, bf16[2048,128]{1,0:T(8,128)(2,1)S(1)}, u32[]{:S(2)}, u32[]{:S(2)}) collective-permute-start(bf16[2048,128]{1,0:T(8,128)(2,1)S(1)} %bitcast.10), channel_id=1, source_target_pairs={{0,16},{16,0},{1,17},{17,1},{2,18},{18,2},{3,19},{19,3},{4,20},{20... | collective-permute-start | bytes 1572872 | tf_op jit(solution)/shard_map/ppermute | solution.py:282
  68.3 3.6 %collective-permute-start.2 = (bf16[2048,128]{1,0:T(8,128)(2,1)S(1)}, bf16[2048,128]{1,0:T(8,128)(2,1)S(1)}, u32[]{:S(2)}, u32[]{:S(2)}) collective-permute-start(bf16[2048,128]{1,0:T(8,128)(2,1)S(1)} %bitcast.12), channel_id=1, source_target_pairs={{0,16},{16,0},{1,17},{17,1},{2,18},{18,2},{3,19},{19,3},{4,20},{20... | collective-permute-start | bytes 1572872 | tf_op jit(solution)/shard_map/ppermute | solution.py:282
  89.5 3.6 %collective-permute-start.3 = (bf16[2048,128]{1,0:T(8,128)(2,1)S(1)}, bf16[2048,128]{1,0:T(8,128)(2,1)S(1)}, u32[]{:S(2)}, u32[]{:S(2)}) collective-permute-start(bf16[2048,128]{1,0:T(8,128)(2,1)S(1)} %bitcast.14), channel_id=1, source_target_pairs={{0,16},{16,0},{1,17},{17,1},{2,18},{18,2},{3,19},{19,3},{4,20},{20... | collective-permute-start | bytes 1572872 | tf_op jit(solution)/shard_map/ppermute | solution.py:282

commit v4 on v3

--- a/solution.py
+++ b/solution.py
@@ -73,11 +73,20 @@
     return message(lifted, gamma, delta, extra)
 
 
-def opening_kernel(ids, rhs_hbm, diag_hbm, msg_out, r_out, cost_out, rhs, diag, sems):
-    copies = (
-        pltpu.make_async_copy(rhs_hbm, rhs, sems.at[0]),
-        pltpu.make_async_copy(diag_hbm, diag, sems.at[1]),
-    )
+def as_column(row):
+    square = (ROWS, ROWS)
+    same = lax.broadcasted_iota(jnp.int32, square, 0) == lax.broadcasted_iota(jnp.int32, square, 1)
+    found = jnp.where(same, jnp.broadcast_to(row, square), 0).astype(F32)
+    return jnp.broadcast_to(jnp.sum(found, axis=1, keepdims=True), (ROWS, WIDTH))
+
+
+def opening_kernel(
+    ids, rhs_hbm, diag_hbm, idx_hbm, pattern_hbm,
+    msg_out, r_out, cost_out, scen_tgt, own_tgt, label, side,
+    rhs, diag, idx, pattern, sems,
+):
+    pairs = ((rhs_hbm, rhs), (diag_hbm, diag), (idx_hbm, idx), (pattern_hbm, pattern))
+    copies = [pltpu.make_async_copy(a, b, sems.at[i]) for i, (a, b) in enumerate(pairs)]
     for copy in copies:
         copy.start()
     for copy in copies:
@@ -85,58 +94,57 @@
     r_out[...], cost_out[...] = rhs[...], diag[...]
     mine = pl.ds(pl.multiple_of(ids[0] * HALF, HALF), HALF)
     inverse = 1.0 / diag[mine, :]
-    u = (rhs[mine, :] * inverse).astype(BF16)
-    inverse = inverse.astype(BF16)
-    for place in range(PLANE):
-        msg_out[place, 0:HALF, :] = u
-        msg_out[place, HALF:OWN, :] = inverse
-
-
-def normal_kernel(
-    ids, idx, pattern, couple_hbm, factor_hbm, normal, tgt, label, couple, factor, prod, flip, sems
-):
-    third = ROWS // 3
-    copies = [pltpu.make_async_copy(couple_hbm, couple, sems.at[0])]
-    for part in range(3):
-        rows = pl.ds(part * third, third)
-        copies.append(
-            pltpu.make_async_copy(factor_hbm.at[rows], factor.at[rows], sems.at[1 + part])
-        )
-    for copy in copies:
-        copy.start()
-
-    square = (ROWS, ROWS)
-    same = lax.broadcasted_iota(jnp.int32, square, 0) == lax.broadcasted_iota(jnp.int32, square, 1)
-    column = jnp.where(same, jnp.broadcast_to(idx[...], square), 0)
-    column = jnp.sum(column.astype(F32), axis=1, keepdims=True).astype(jnp.int32)
-    rows = lax.broadcasted_iota(jnp.int32, (PAD + OWN, WIDTH), 0)
-    fixed = jnp.where(rows < ROWS + 2, rows - ROWS + GAMMA, -9)
-    fixed = jnp.where(rows < PAD, fixed, rows - PAD + ids[2] * OWN)
-    tgt[...] = fixed
-    column = jnp.broadcast_to(column, (ROWS, WIDTH))
-    tgt[0:ROWS, :] = column
+    msg_out[0:HALF, :] = (rhs[mine, :] * inverse).astype(BF16)
+    msg_out[HALF:OWN, :] = inverse.astype(BF16)
+
+    column = as_column(idx[...]).astype(jnp.int32)
+    rows = lax.broadcasted_iota(jnp.int32, (PAD, WIDTH), 0)
+    scen_tgt[...] = jnp.where(rows < ROWS + 2, rows - ROWS + GAMMA, -9)
+    scen_tgt[0:ROWS, :] = column
+    own_tgt[...] = lax.broadcasted_iota(jnp.int32, (OWN, WIDTH), 0) + ids[2] * OWN
     lanes = lax.broadcasted_iota(jnp.int32, (ROWS, WIDTH), 1)
     place = lax.broadcasted_iota(jnp.int32, (ROWS, WIDTH), 0) + PAD * ids[1]
     for line, values in enumerate((column >> 6, column & 63)):
         label[line : line + 1, :] = column_sum(jnp.where(lanes == place, values, 0).astype(F32))
-
-    side = pattern[...].astype(F32)
+    for k in range(2):
+        side[k] = as_column(pattern[k : k + 1, :])
+
+
+def copy_parts(source, target, sems, first, parts):
+    step = source.shape[0] // parts
+    copies = []
+    for part in range(parts):
+        rows = pl.ds(part * step, step)
+        copies.append(
+            pltpu.make_async_copy(source.at[rows], target.at[rows], sems.at[first + part])
+        )
+    return copies
+
+
+def normal_kernel(
+    side, couple_hbm, factor_hbm, normal_hbm, couple, factor, prod, flip, normal, sems
+):
+    couples = copy_parts(couple_hbm, couple, sems, 0, 3)
+    factors = copy_parts(factor_hbm, factor, sems, 3, 6)
+    outs = copy_parts(normal, normal_hbm, sems, 9, 6)
+    for part in range(3):
+        for copy in (couples[part], factors[2 * part], factors[2 * part + 1]):
+            copy.start()
     zeros = jnp.zeros((WIDTH, WIDTH), BF16)
-    copies[0].wait()
-    for r in range(ROWS):
-        if r % third == 0:
-            copies[1 + r // third].wait()
+
+    def product_row(r):
         for k in range(3):
             c = r + k - 1
             if not 0 <= c < ROWS:
                 continue
             block = dot_nn(factor[r, k], couple[c])
             if k != 1:
-                block = block * side[r : r + 1, k // 2 : k // 2 + 1]
+                block = block * side[k // 2, r : r + 1, :]
             block = block.astype(BF16)
             prod[r, k] = block
             flip[c, :, (2 - k) * WIDTH : (3 - k) * WIDTH] = block.T
-    for d in range(ROWS):
+
+    def normal_row(d):
         for band in range(BANDS):
             c = d + band - 2
             if not 0 <= c < ROWS:
@@ -153,9 +161,46 @@
             if c != d:
                 normal[c, :, (4 - band) * WIDTH : (5 - band) * WIDTH] = block.T
 
-
-def first_kernel(ids, near, far, tgt, label, own, cost, normal, msg_out, us_out, inv_out):
-    want = tgt[0:PAD, 0:1]
+    for copy in couples[:2] + factors[:2]:
+        copy.wait()
+    for r in range(8):
+        product_row(r)
+    for copy in couples[2:] + factors[2:4]:
+        copy.wait()
+    for r in range(8, 16):
+        product_row(r)
+    for d in range(7):
+        normal_row(d)
+    outs[0].start()
+    for copy in factors[4:]:
+        copy.wait()
+    for r in range(16, 24):
+        product_row(r)
+    for d in range(7, 12):
+        normal_row(d)
+    outs[1].start()
+    outs[2].start()
+    for d in range(12, 18):
+        normal_row(d)
+    outs[3].start()
+    for d in range(18, 24):
+        normal_row(d)
+    outs[4].start()
+    outs[5].start()
+    for copy in outs:
+        copy.wait()
+
+
+def load_kernel(normal_hbm, normal, sems):
+    copies = copy_parts(normal_hbm, normal, sems, 0, 6)
+    for copy in copies:
+        copy.start()
+    for copy in copies:
+        copy.wait()
+
+
+def first_kernel(ids, near, far, scen_tgt, label, own, cost, normal, msg_out, us_out, inv_out):
+    want = scen_tgt[:, 0:1]
     want = jnp.concatenate([want, want + INVERSE], axis=0)
     found = jnp.zeros((2 * PAD, WIDTH), F32)
     for part, which in ((near, ids[0]), (far, 1 - ids[0])):
@@ -169,8 +214,14 @@
     msg_out[...] = next_message(us, r * (1.0 / d), r, d, normal, (label[0:1, :], label[1:2, :]))
 
 
-def label_sum(part, tgt, hot_out, sum_out):
-    want = tgt[...]
+def give_and_keep(found, keep, give):
+    keep[...] = found[0 : PAD + OWN, :]
+    give[0:PAD, :] = found[PAD + OWN :, :]
+    give[PAD:, :] = found[PAD : PAD + OWN, :]
+
+
+def label_sum(part, scen_tgt, own_tgt, other_tgt, hot, keep, give):
+    want = jnp.concatenate([scen_tgt[...], own_tgt[...], other_tgt[...]], axis=0)
     lane = lax.broadcasted_iota(jnp.int32, (1, WIDTH), 1)
     slot = lane & (PAD - 1)
     fixed = jnp.where(slot < ROWS + 2, GAMMA, jnp.where(slot < ROWS + 4, DELTA, -1))
@@ -180,12 +231,12 @@
         ends = ends[0] + ends[1] + ends[2] + ends[3]
         found = (ends[12:13, :] * 64.0 + ends[13:14, :]).astype(jnp.int32)
         block = jnp.where(slot < ROWS, found, fixed)
-        hot_out[:, start : start + WIDTH] = hot_of(want == block)
-    sum_out[...] = dot_nn(hot_out[...], part[...])
-
-
-def near_sum(part, hot, sum_out):
-    sum_out[...] = dot_nn(hot[...], part[...])
+        hot[:, start : start + WIDTH] = hot_of(want == block)
+    give_and_keep(dot_nn(hot[...], part[...]), keep, give)
+
+
+def message_sum(part, hot, keep, give):
+    give_and_keep(dot_nn(hot[...], part[...]), keep, give)
 
 
 def advance(total, us, inv_s, ps, u, cost, q, d, x, r, gamma_old, alpha_old):
@@ -212,11 +263,10 @@
 
 
 def second_kernel(
-    far, tgt, half, us, inv_s, own, cost, normal,
-    msg_out, hot_out, us_out, ps_out, scal_out, d_out, q_out, x_out, r_out, other,
+    keep, got, us, inv_s, own, cost, normal,
+    msg_out, us_out, ps_out, scal_out, d_out, q_out, x_out, r_out,
 ):
-    label_sum(far, tgt, hot_out, other)
-    total = half[...] + other[...]
+    total = keep[...] + got[...]
     d = cost[...]
     inv = 1.0 / d
     r = own[...]
@@ -231,10 +281,10 @@
 
 
 def third_kernel(
-    far, hot, half, us, ps, inv_s, scal, d, q, x, r, cost, normal,
+    keep, got, us, ps, inv_s, scal, d, q, x, r, cost, normal,
     msg_out, scal_out, d_out, q_out, x_out, r_out,
 ):
-    total = half[...] + dot_nn(hot[...], far[...])
+    total = keep[...] + got[...]
     c = cost[...]
     inv = 1.0 / c
     gamma, alpha, u_s, p_s, dn, qn, xn, rn = advance(
@@ -247,8 +297,8 @@
     msg_out[...] = next_message(u_s, inv * rn, rn, c, normal)
 
 
-def last_kernel(far, hot, half, scal, d, q, x, r, cost, x_out, r_out):
-    total = half[...] + dot_nn(hot[...], far[...])
+def last_kernel(keep, got, scal, d, q, x, r, cost, x_out, r_out):
+    total = keep[...] + got[...]
     c = cost[...]
     found = advance(
         total, None, None, None, r[...] / c, c, q[...], d[...], x[...], r[...],
@@ -257,7 +307,7 @@
     x_out[...], r_out[...] = found[6], found[7]
 
 
-def call(kernel, shapes, *args, scalars=0, weights=(), scratch=(), sems=0):
+def call(kernel, shapes, *args, scalars=0, weights=(), scratch=(), sems=0, hbm_out=False):
     vmem = pl.BlockSpec(memory_space=pltpu.VMEM)
     specs = [pl.BlockSpec(memory_space=pltpu.SMEM)] * scalars + [vmem] * (len(args) - scalars)
     specs += [pl.BlockSpec(memory_space=pltpu.HBM)] * len(weights)
@@ -266,9 +316,9 @@
         scratch.append(pltpu.SemaphoreType.DMA((sems,)))
     return pl.pallas_call(
         kernel,
-        out_shape=[jax.ShapeDtypeStruct(s, t) for s, t in shapes],
+        out_shape=[(pltpu.HBM if hbm_out else jax.ShapeDtypeStruct)(s, t) for s, t in shapes],
         in_specs=specs,
-        out_specs=[vmem] * len(shapes),
+        out_specs=[pl.BlockSpec(memory_space=pltpu.HBM) if hbm_out else vmem] * len(shapes),
         scratch_shapes=scratch,
         compiler_params=pltpu.CompilerParams(vmem_limit_bytes=32 * 1024 * 1024),
     )(*args, *weights)
@@ -282,51 +332,57 @@
     return lax.ppermute(values, "core", [(0, 1), (1, 0)])
 
 
-def exchange(sent):
-    copies = jnp.broadcast_to(sent[None], (CHIPS,) + sent.shape)
-    near = lax.all_to_all(copies, ("x", "z", "y"), 0, 0, tiled=True).reshape(CHIPS * PAD, WIDTH)
-    return near, other_core(near)
+def to_all(sent, axes, count):
+    copies = jnp.broadcast_to(sent[None], (count,) + sent.shape)
+    return lax.all_to_all(copies, axes, 0, 0, tiled=True).reshape(-1, WIDTH)
 
 
 def shards(rhs, diag, couple, couple_idx, factor, pattern):
     scen, own, msg = ((PAD, WIDTH), F32), ((OWN, WIDTH), F32), ((PAD, WIDTH), BF16)
     scal, sums = ((2, WIDTH), F32), ((PAD + OWN, WIDTH), F32)
-    hots = ((PAD + OWN, CHIPS * PAD), BF16)
+    hots = ((PAD + OWN + PAD, CHIPS * PAD), BF16)
     vec = lax.axis_index("z") * 4 + lax.axis_index("y")
     ids = jnp.stack([lax.axis_index("core"), lax.axis_index("y"), vec]).astype(jnp.int32)
-    sent, r, cost = call(
-        opening_kernel, [((PLANE, OWN, WIDTH), BF16), own, own],
-        ids, scalars=1, weights=in_hbm(rhs, diag), scratch=[own, own], sems=2,
-    )
-    near = lax.all_to_all(sent, ("z", "y"), 0, 0, tiled=True).reshape(PLANE * OWN, WIDTH)
+    sent, r, cost, scen_tgt, own_tgt, label, side = call(
+        opening_kernel,
+        [
+            ((OWN, WIDTH), BF16), own, own, ((PAD, WIDTH), jnp.int32), ((OWN, WIDTH), jnp.int32),
+            scal, ((2, ROWS, WIDTH), F32),
+        ],
+        ids, scalars=1, weights=in_hbm(rhs, diag, couple_idx, pattern[0].T),
+        scratch=[own, own, ((1, ROWS), jnp.int32), ((2, ROWS), jnp.int32)], sems=4,
+    )
+    near = to_all(sent, ("z", "y"), PLANE)
+    other_tgt = other_core(scen_tgt)
+    triple, wide = (ROWS, 3, WIDTH, WIDTH), (ROWS, WIDTH, 3 * WIDTH)
+    bands = ((ROWS, WIDTH, BANDS * WIDTH), BF16)
+    normal = call(
+        normal_kernel, [bands], side, weights=in_hbm(couple[0], factor[0]), hbm_out=True,
+        scratch=[((ROWS, WIDTH, WIDTH), BF16), (triple, BF16), (triple, BF16), (wide, BF16), bands],
+        sems=15,
+    )[0]
+    near, normal, other_tgt = lax.optimization_barrier((near, normal, other_tgt))
     far = other_core(near)
-    block = (ROWS, WIDTH, WIDTH)
-    triple, wide = (ROWS, 3, WIDTH, WIDTH), (ROWS, WIDTH, 3 * WIDTH)
-    normal, tgt, label = call(
-        normal_kernel,
-        [((ROWS, WIDTH, BANDS * WIDTH), BF16), ((PAD + OWN, WIDTH), jnp.int32), scal],
-        ids, couple_idx, pattern[0], scalars=1, weights=in_hbm(couple[0], factor[0]),
-        scratch=[(block, BF16), (triple, BF16), (triple, BF16), (wide, BF16)], sems=4,
-    )
+    normal = call(load_kernel, [bands], weights=in_hbm(normal), sems=6)[0]
     sent, us, inv_s = call(
-        first_kernel, [msg, scen, scen], ids, near, far, tgt, label, r, cost, normal, scalars=1
-    )
-
-    near, far = exchange(sent)
-    hot_near, half = call(label_sum, [hots, sums], near, tgt)
-    sent, hot_far, us, ps, sc, d, q, x, r = call(
-        second_kernel, [msg, hots, scen, scen, scal, own, own, own, own],
-        far, tgt, half, us, inv_s, r, cost, normal, scratch=[sums],
-    )
-    near, far = exchange(sent)
-    half = call(near_sum, [sums], near, hot_near)[0]
+        first_kernel, [msg, scen, scen], ids, near, far, scen_tgt, label, r, cost, normal, scalars=1
+    )
+
+    near = to_all(sent, ("x", "z", "y"), CHIPS)
+    hot, keep, give = call(label_sum, [hots, sums, sums], near, scen_tgt, own_tgt, other_tgt)
+    sent, us, ps, sc, d, q, x, r = call(
+        second_kernel, [msg, scen, scen, scal, own, own, own, own],
+        keep, other_core(give), us, inv_s, r, cost, normal,
+    )
+    near = to_all(sent, ("x", "z", "y"), CHIPS)
+    keep, give = call(message_sum, [sums, sums], near, hot)
     sent, sc, d, q, x, r = call(
         third_kernel, [msg, scal, own, own, own, own],
-        far, hot_far, half, us, ps, inv_s, sc, d, q, x, r, cost, normal,
-    )
-    near, far = exchange(sent)
-    half = call(near_sum, [sums], near, hot_near)[0]
-    return call(last_kernel, [own, own], far, hot_far, half, sc, d, q, x, r, cost)
+        keep, other_core(give), us, ps, inv_s, sc, d, q, x, r, cost, normal,
+    )
+    near = to_all(sent, ("x", "z", "y"), CHIPS)
+    keep, give = call(message_sum, [sums, sums], near, hot)
+    return call(last_kernel, [own, own], keep, other_core(give), sc, d, q, x, r, cost)
 
 
 def solution(mesh):

time: 94.5 us -> 90.4 us (0.957)
  blocking collectives: 68.6 us -> 51.1 us
  starting transfers between devices: 7.83 us -> 17.7 us
  waiting for transfers between devices: 3.64 us -> 5.9 us
  Pallas kernels: 11.6 us -> 13.5 us
    all_to_all x4 -> x3, blocking collectives: 68.6 us -> 51.1 us  [to_all(): return lax.all_to_all(copies, axes, 0, 0, tiled=True).reshape(-1, WIDTH)]
    all_to_all x0 -> x1, starting transfers between devices: none -> 8.6 us  [to_all(): return lax.all_to_all(copies, axes, 0, 0, tiled=True).reshape(-1, WIDTH)]
    all_to_all x0 -> x1, waiting for transfers between devices: none -> 3.19 us  [to_all(): return lax.all_to_all(copies, axes, 0, 0, tiled=True).reshape(-1, WIDTH)]
    pallas_call x9 -> x10, Pallas kernels: 11.6 us -> 13.5 us  [call(): pl.pallas_call(kernel, out_shape=[(pltpu.HBM if hbm_out else jax.ShapeDty...]
    ppermute x4 -> x5, starting transfers between devices: 7.83 us -> 9.06 us  [other_core(): return lax.ppermute(values, 'core', [(0, 1), (1, 0)])]
    ppermute x4 -> x5, waiting for transfers between devices: 3.64 us -> 2.71 us  [other_core(): return lax.ppermute(values, 'core', [(0, 1), (1, 0)])]
  transfers between devices with their start and end apart: 4 -> 6, of which waited for: 3 -> 4; matrix products, arithmetic and copies ran while one was open for 1% -> 0% of each run, Pallas kernels for 6% -> 8%
where the time goes in v4:
time: 90.4 us; the launch traced here: 90 us
  blocking collectives  51.1 us (57%)
  starting transfers between devices  17.7 us (20%)
  Pallas kernels  13.5 us (15%)
  waiting for transfers between devices  5.9 us (7%)
  local copies, waits for them, and re-layouts  1.01 us (1%)
    all_to_all x3, blocking collectives, to_all(): return lax.all_to_all(copies, axes, 0, 0, tiled=True).reshape(-1, WIDTH)  51.1 us
    pallas_call x10, Pallas kernels, call(): pl.pallas_call(kernel, out_shape=[(pltpu.HBM if hbm_out else jax.ShapeDty...  13.5 us
    ppermute x5, starting transfers between devices, other_core(): return lax.ppermute(values, 'core', [(0, 1), (1, 0)])  9.06 us
    all_to_all x1, starting transfers between devices, to_all(): return lax.all_to_all(copies, axes, 0, 0, tiled=True).reshape(-1, WIDTH)  8.6 us
    all_to_all x1, waiting for transfers between devices, to_all(): return lax.all_to_all(copies, axes, 0, 0, tiled=True).reshape(-1, WIDTH)  3.19 us
    ppermute x5, waiting for transfers between devices, other_core(): return lax.ppermute(values, 'core', [(0, 1), (1, 0)])  2.71 us
  transfers between devices with their start and end apart: 6, of which 4 were waited for; matrix products, arithmetic and copies ran while one was open for 0% of the time, Pallas kernels for 8%

profile of v4, /device:TPU:1, one launch (start us, length us, event | category | flops | bytes accessed | tf_op | source)
XLA Modules:
  0.0 90.0 jit_solution(12350921029751059938)
XLA Ops:
  0.7 1.5 %shard_map.77 = (bf16[96,128]{1,0:T(8,128)(2,1)S(1)}, f32[96,128]{1,0:T(8,128)S(1)}, f32[96,128]{1,0:T(8,128)S(1)}, s32[32,128]{1,0:T(8,128)S(1)}, s32[96,128]{1...) custom-call(s32[3]{0:T(128)S(1)} %pad_add_fusion.ids, f32[96,128]{1,0:T(8,128)} %rhs_hbm.1, ...), custom_call_target="tpu_custom_call" | custom-call | tf_op jit(solution)/shard_map/pallas_call | solution.py:317
  2.2 0.8 broadcast_in_dim.8
  3.0 8.6 %all-to-all-start = ((bf16[16,96,128]{2,1,0:T(8,128)(2,1)}), bf16[16,96,128]{2,1,0:T(8,128)(2,1)S(1)}, u32[]{:S(2)}, u32[]{:S(2)}) async-start(bf16[16,96,128]{2,1,0:T(8,128)(2,1)} %broadcast_in_dim.8), calls=%async_computation | async-start | bytes 786432 | tf_op jit(solution)/shard_map/all_to_all | solution.py:337
  11.6 1.0 %collective-permute-start = (s32[32,128]{1,0:T(8,128)S(1)}, s32[32,128]{1,0:T(8,128)S(1)}, u32[]{:S(2)}, u32[]{:S(2)}) collective-permute-start(s32[32,128]{1,0:T(8,128)S(1)} %get-tuple-element.38.scen_tgt), channel_id=1, source_target_pairs={{0,16},{16,0},{1,17},{17,1},{2,18},{18,2},{3,19},{19,3},{4,20},{20... | collective-permute-start | bytes 49160 | tf_op jit(solution)/shard_map/ppermute | solution.py:332
  12.7 4.9 %shard_map.78.normal_hbm = bf16[24,128,640]{2,1,0:T(8,128)(2,1)} custom-call(f32[2,24,128]{2,1,0:T(8,128)S(1)} %get-tuple-element.37.side, bf16[24,128,128]{2,1,0:T(8,128)(2,1)} %bitcast.18, bf16[24,3,128,128]{3,2,1,0:T(8,128)(2,1)} %bitcast.17), custom_call_target="tpu_custom_call" | custom-call | tf_op jit(solution)/shard_map/pallas_call | solution.py:317
  17.6 3.2 %all-to-all-done = bf16[16,96,128]{2,1,0:T(8,128)(2,1)S(1)} async-done(((bf16[16,96,128]{2,1,0:T(8,128)(2,1)}), bf16[16,96,128]{2,1,0:T(8,128)(2,1)S(1)}, u32[]{:S(2)}, u32[]{:S(2)}) %all-to-all-start) | async-done | bytes 393248 | tf_op jit(solution)/shard_map/all_to_all | solution.py:337
  20.8 1.9 %collective-permute-start.1 = (bf16[1536,128]{1,0:T(8,128)(2,1)S(1)}, bf16[1536,128]{1,0:T(8,128)(2,1)S(1)}, u32[]{:S(2)}, u32[]{:S(2)}) collective-permute-start(bf16[1536,128]{1,0:T(8,128)(2,1)S(1)} %bitcast.15), channel_id=1, source_target_pairs={{0,16},{16,0},{1,17},{17,1},{2,18},{18,2},{3,19},{19,3},{4,20},{20... | collective-permute-start | bytes 1179656 | tf_op jit(solution)/shard_map/ppermute | solution.py:332
  22.7 2.1 %shard_map.79.normal = bf16[24,128,640]{2,1,0:T(8,128)(2,1)S(1)} custom-call(bf16[24,128,640]{2,1,0:T(8,128)(2,1)} %shard_map.78.normal_hbm), custom_call_target="tpu_custom_call" | custom-call | tf_op jit(solution)/shard_map/pallas_call | solution.py:317
  24.8 1.5 %shard_map.80 = (bf16[32,128]{1,0:T(8,128)(2,1)S(1)}, f32[32,128]{1,0:T(8,128)S(1)}, f32[32,128]{1,0:T(8,128)S(1)}) custom-call(s32[3]{0:T(128)S(1)} %pad_add_fusion.ids, bf16[1536,128]{1,0:T(8,128)(2,1)S(1)} %bitcast.16, bf16[1536,128]{1,0:T(8,128)(2,1)S(1)} %collective-permute-done.1.far, s32[32,128]{1,0:T(8,128)S(1)} %get-tuple-element.38.scen_tgt, ...), custom_call_target="tpu_custom_call" | custom-call | tf_op jit(solution)/shard_map/pallas_call | solution.py:317
  26.4 18.2 %all_to_all.20 = bf16[64,32,128]{2,1,0:T(8,128)(2,1)S(1)} all-to-all(bf16[64,32,128]{2,1,0:T(8,128)(2,1)S(1)} %broadcast_in_dim.9), channel_id=1, replica_groups=mesh['x'=4,'core'=2,'z'=4,'y'=4] {'x','z','y'}, dimensions={0} | all-to-all | bytes 1048576 | tf_op jit(solution)/shard_map/all_to_all | solution.py:337
  44.6 0.4 shard_map.81
  45.1 1.9 %collective-permute-start.2 = (f32[128,128]{1,0:T(8,128)S(1)}, f32[128,128]{1,0:T(8,128)S(1)}, u32[]{:S(2)}, u32[]{:S(2)}) collective-permute-start(f32[128,128]{1,0:T(8,128)S(1)} %get-tuple-element.48), channel_id=1, source_target_pairs={{0,16},{16,0},{1,17},{17,1},{2,18},{18,2},{3,19},{19,3},{4,20},{20... | collective-permute-start | bytes 196616 | tf_op jit(solution)/shard_map/ppermute | solution.py:332
  47.0 0.9 %collective-permute-done.2.got = f32[128,128]{1,0:T(8,128)S(1)} collective-permute-done((f32[128,128]{1,0:T(8,128)S(1)}, f32[128,128]{1,0:T(8,128)S(1)}, u32[]{:S(2)}, u32[]{:S(2)}) %collective-permute-start.2) | collective-permute-done | bytes 65568 | tf_op jit(solution)/shard_map/ppermute | solution.py:332
  47.9 0.8 shard_map.82
  48.8 16.4 %all_to_all.21 = bf16[64,32,128]{2,1,0:T(8,128)(2,1)S(1)} all-to-all(bf16[64,32,128]{2,1,0:T(8,128)(2,1)S(1)} %broadcast_in_dim.10), channel_id=1, replica_groups=mesh['x'=4,'core'=2,'z'=4,'y'=4] {'x','z','y'}, dimensions={0} | all-to-all | bytes 1048576 | tf_op jit(solution)/shard_map/all_to_all | solution.py:337
  65.2 0.3 shard_map.83
  65.5 2.1 %collective-permute-start.3 = (f32[128,128]{1,0:T(8,128)S(1)}, f32[128,128]{1,0:T(8,128)S(1)}, u32[]{:S(2)}, u32[]{:S(2)}) collective-permute-start(f32[128,128]{1,0:T(8,128)S(1)} %get-tuple-element.54), channel_id=1, source_target_pairs={{0,16},{16,0},{1,17},{17,1},{2,18},{18,2},{3,19},{19,3},{4,20},{20... | collective-permute-start | bytes 196616 | tf_op jit(solution)/shard_map/ppermute | solution.py:332
  67.6 0.9 %collective-permute-done.3.got = f32[128,128]{1,0:T(8,128)S(1)} collective-permute-done((f32[128,128]{1,0:T(8,128)S(1)}, f32[128,128]{1,0:T(8,128)S(1)}, u32[]{:S(2)}, u32[]{:S(2)}) %collective-permute-start.3) | collective-permute-done | bytes 65568 | tf_op jit(solution)/shard_map/ppermute | solution.py:332
  68.5 0.8 shard_map.84
  69.4 16.4 %all_to_all.22 = bf16[64,32,128]{2,1,0:T(8,128)(2,1)S(1)} all-to-all(bf16[64,32,128]{2,1,0:T(8,128)(2,1)S(1)} %broadcast_in_dim.11), channel_id=1, replica_groups=mesh['x'=4,'core'=2,'z'=4,'y'=4] {'x','z','y'}, dimensions={0} | all-to-all | bytes 1048576 | tf_op jit(solution)/shard_map/all_to_all | solution.py:337
  85.9 0.3 shard_map.85
  86.2 2.1 %collective-permute-start.4 = (f32[128,128]{1,0:T(8,128)S(1)}, f32[128,128]{1,0:T(8,128)S(1)}, u32[]{:S(2)}, u32[]{:S(2)}) collective-permute-start(f32[128,128]{1,0:T(8,128)S(1)} %get-tuple-element.64), channel_id=1, source_target_pairs={{0,16},{16,0},{1,17},{17,1},{2,18},{18,2},{3,19},{19,3},{4,20},{20... | collective-permute-start | bytes 196616 | tf_op jit(solution)/shard_map/ppermute | solution.py:332
  88.3 0.9 %collective-permute-done.4.got = f32[128,128]{1,0:T(8,128)S(1)} collective-permute-done((f32[128,128]{1,0:T(8,128)S(1)}, f32[128,128]{1,0:T(8,128)S(1)}, u32[]{:S(2)}, u32[]{:S(2)}) %collective-permute-start.4) | collective-permute-done | bytes 65568 | tf_op jit(solution)/shard_map/ppermute | solution.py:332
  89.2 0.8 shard_map.86
  (6 shorter events, 0.3 us)
Async XLA Ops:
  3.0 17.8 %all-to-all-start = ((bf16[16,96,128]{2,1,0:T(8,128)(2,1)}), bf16[16,96,128]{2,1,0:T(8,128)(2,1)S(1)}, u32[]{:S(2)}, u32[]{:S(2)}) async-start(bf16[16,96,128]{2,1,0:T(8,128)(2,1)} %broadcast_in_dim.8), calls=%async_computation | async-start | bytes 786432 | tf_op jit(solution)/shard_map/all_to_all | solution.py:337
  11.6 6.0 %collective-permute-start = (s32[32,128]{1,0:T(8,128)S(1)}, s32[32,128]{1,0:T(8,128)S(1)}, u32[]{:S(2)}, u32[]{:S(2)}) collective-permute-start(s32[32,128]{1,0:T(8,128)S(1)} %get-tuple-element.38.scen_tgt), channel_id=1, source_target_pairs={{0,16},{16,0},{1,17},{17,1},{2,18},{18,2},{3,19},{19,3},{4,20},{20... | collective-permute-start | bytes 49160 | tf_op jit(solution)/shard_map/ppermute | solution.py:332
  20.8 4.0 %collective-permute-start.1 = (bf16[1536,128]{1,0:T(8,128)(2,1)S(1)}, bf16[1536,128]{1,0:T(8,128)(2,1)S(1)}, u32[]{:S(2)}, u32[]{:S(2)}) collective-permute-start(bf16[1536,128]{1,0:T(8,128)(2,1)S(1)} %bitcast.15), channel_id=1, source_target_pairs={{0,16},{16,0},{1,17},{17,1},{2,18},{18,2},{3,19},{19,3},{4,20},{20... | collective-permute-start | bytes 1179656 | tf_op jit(solution)/shard_map/ppermute | solution.py:332
  45.1 2.8 %collective-permute-start.2 = (f32[128,128]{1,0:T(8,128)S(1)}, f32[128,128]{1,0:T(8,128)S(1)}, u32[]{:S(2)}, u32[]{:S(2)}) collective-permute-start(f32[128,128]{1,0:T(8,128)S(1)} %get-tuple-element.48), channel_id=1, source_target_pairs={{0,16},{16,0},{1,17},{17,1},{2,18},{18,2},{3,19},{19,3},{4,20},{20... | collective-permute-start | bytes 196616 | tf_op jit(solution)/shard_map/ppermute | solution.py:332
  65.5 3.0 %collective-permute-start.3 = (f32[128,128]{1,0:T(8,128)S(1)}, f32[128,128]{1,0:T(8,128)S(1)}, u32[]{:S(2)}, u32[]{:S(2)}) collective-permute-start(f32[128,128]{1,0:T(8,128)S(1)} %get-tuple-element.54), channel_id=1, source_target_pairs={{0,16},{16,0},{1,17},{17,1},{2,18},{18,2},{3,19},{19,3},{4,20},{20... | collective-permute-start | bytes 196616 | tf_op jit(solution)/shard_map/ppermute | solution.py:332
  86.2 3.0 %collective-permute-start.4 = (f32[128,128]{1,0:T(8,128)S(1)}, f32[128,128]{1,0:T(8,128)S(1)}, u32[]{:S(2)}, u32[]{:S(2)}) collective-permute-start(f32[128,128]{1,0:T(8,128)S(1)} %get-tuple-element.64), channel_id=1, source_target_pairs={{0,16},{16,0},{1,17},{17,1},{2,18},{18,2},{3,19},{19,3},{4,20},{20... | collective-permute-start | bytes 196616 | tf_op jit(solution)/shard_map/ppermute | solution.py:332

commit v5 on v4

--- a/solution.py
+++ b/solution.py
@@ -9,6 +9,7 @@
 
 ROWS = 24
 PAD = 32
+SENT = 26
 OWN = 96
 HALF = OWN // 2
 WIDTH = 128
@@ -16,7 +17,6 @@
 PLANE = 16
 BANDS = 5
 GAMMA, DELTA = 4000, 4001
-INVERSE = 2048
 F32, BF16 = jnp.float32, jnp.bfloat16
 
 
@@ -54,23 +54,32 @@
     return lifted
 
 
-def message(lifted, gamma, delta, extra):
+def write_message(msg_out, lifted, lines):
     rows = lax.broadcasted_iota(jnp.int32, (PAD, WIDTH), 0)
-    out = jnp.where(rows < ROWS, lifted, 0.0)
-    for place, line in enumerate(split(gamma) + split(delta) + tuple(extra)):
+    out = lifted
+    for place, line in enumerate(lines):
         out = jnp.where(rows == ROWS + place, jnp.broadcast_to(line, out.shape), out)
-    return out.astype(BF16)
+    for pair in range(SENT // 2):
+        msg_out[pair] = out[2 * pair : 2 * pair + 2, :].astype(BF16)
 
 
 def column_sum(values):
     return jnp.sum(values, axis=0, keepdims=True)
 
 
-def next_message(us, u, r, cost, normal, extra=()):
+def products(us, lifted, ru, cuu):
+    return column_sum(ru) * 0.125, column_sum(cuu) * 0.125 + column_sum(us * lifted)
+
+
+def folded(values):
+    lane = lax.broadcasted_iota(jnp.int32, (1, WIDTH), 1)
+    high, low = split(values + pltpu.roll(values, WIDTH // 2, 1))
+    return jnp.where(lane < WIDTH // 2, high, low)
+
+
+def next_message(msg_out, us, u, r, cost, normal):
     lifted = scenario_lift(us, normal)
-    gamma = column_sum(r * u) * 0.125
-    delta = column_sum(cost * u * u) * 0.125 + column_sum(us * lifted)
-    return message(lifted, gamma, delta, extra)
+    write_message(msg_out, lifted, [folded(v) for v in products(us, lifted, r * u, cost * u * u)])
 
 
 def as_column(row):
@@ -80,34 +89,32 @@
     return jnp.broadcast_to(jnp.sum(found, axis=1, keepdims=True), (ROWS, WIDTH))
 
 
-def opening_kernel(
-    ids, rhs_hbm, diag_hbm, idx_hbm, pattern_hbm,
-    msg_out, r_out, cost_out, scen_tgt, own_tgt, label, side,
-    rhs, diag, idx, pattern, sems,
-):
-    pairs = ((rhs_hbm, rhs), (diag_hbm, diag), (idx_hbm, idx), (pattern_hbm, pattern))
-    copies = [pltpu.make_async_copy(a, b, sems.at[i]) for i, (a, b) in enumerate(pairs)]
+def scenario_targets(idx):
+    rows = lax.broadcasted_iota(jnp.int32, (PAD - ROWS, WIDTH), 0)
+    rest = jnp.where(rows < 2, rows + GAMMA, -9)
+    return jnp.concatenate([as_column(idx).astype(jnp.int32), rest], axis=0)
+
+
+def opening_kernel(ids, rhs_hbm, diag_hbm, msg_hbm, rhs, diag, msg, sems):
+    copies = (
+        pltpu.make_async_copy(rhs_hbm, rhs, sems.at[0]),
+        pltpu.make_async_copy(diag_hbm, diag, sems.at[1]),
+    )
     for copy in copies:
         copy.start()
     for copy in copies:
         copy.wait()
-    r_out[...], cost_out[...] = rhs[...], diag[...]
     mine = pl.ds(pl.multiple_of(ids[0] * HALF, HALF), HALF)
     inverse = 1.0 / diag[mine, :]
-    msg_out[0:HALF, :] = (rhs[mine, :] * inverse).astype(BF16)
-    msg_out[HALF:OWN, :] = inverse.astype(BF16)
-
-    column = as_column(idx[...]).astype(jnp.int32)
-    rows = lax.broadcasted_iota(jnp.int32, (PAD, WIDTH), 0)
-    scen_tgt[...] = jnp.where(rows < ROWS + 2, rows - ROWS + GAMMA, -9)
-    scen_tgt[0:ROWS, :] = column
-    own_tgt[...] = lax.broadcasted_iota(jnp.int32, (OWN, WIDTH), 0) + ids[2] * OWN
-    lanes = lax.broadcasted_iota(jnp.int32, (ROWS, WIDTH), 1)
-    place = lax.broadcasted_iota(jnp.int32, (ROWS, WIDTH), 0) + PAD * ids[1]
-    for line, values in enumerate((column >> 6, column & 63)):
-        label[line : line + 1, :] = column_sum(jnp.where(lanes == place, values, 0).astype(F32))
-    for k in range(2):
-        side[k] = as_column(pattern[k : k + 1, :])
+    msg[:, 0:WIDTH] = (rhs[mine, :] * inverse).astype(BF16)
+    msg[:, WIDTH:] = inverse.astype(BF16)
+    copies = [
+        pltpu.make_async_copy(msg, msg_hbm.at[place], sems.at[2 + place]) for place in range(PLANE)
+    ]
+    for copy in copies:
+        copy.start()
+    for copy in copies:
+        copy.wait()
 
 
 def copy_parts(source, target, sems, first, parts):
@@ -122,7 +129,8 @@
 
 
 def normal_kernel(
-    side, couple_hbm, factor_hbm, normal_hbm, couple, factor, prod, flip, normal, sems
+    pattern_hbm, couple_hbm, factor_hbm, normal_hbm,
+    pattern, couple, factor, prod, flip, normal, sems,
 ):
     couples = copy_parts(couple_hbm, couple, sems, 0, 3)
     factors = copy_parts(factor_hbm, factor, sems, 3, 6)
@@ -130,6 +138,10 @@
     for part in range(3):
         for copy in (couples[part], factors[2 * part], factors[2 * part + 1]):
             copy.start()
+    copy = pltpu.make_async_copy(pattern_hbm, pattern, sems.at[15])
+    copy.start()
+    copy.wait()
+    side = [as_column(pattern[k : k + 1, :]) for k in range(2)]
     zeros = jnp.zeros((WIDTH, WIDTH), BF16)
 
     def product_row(r):
@@ -139,7 +151,7 @@
                 continue
             block = dot_nn(factor[r, k], couple[c])
             if k != 1:
-                block = block * side[k // 2, r : r + 1, :]
+                block = block * side[k // 2][r : r + 1, :]
             block = block.astype(BF16)
             prod[r, k] = block
             flip[c, :, (2 - k) * WIDTH : (3 - k) * WIDTH] = block.T
@@ -191,27 +203,39 @@
         copy.wait()
 
 
-def load_kernel(normal_hbm, normal, sems):
+def load_kernel(normal_hbm, rhs_hbm, diag_hbm, idx_hbm, normal, rhs, diag, idx, sems):
     copies = copy_parts(normal_hbm, normal, sems, 0, 6)
+    for place, pair in enumerate(((rhs_hbm, rhs), (diag_hbm, diag), (idx_hbm, idx))):
+        copies.append(pltpu.make_async_copy(*pair, sems.at[6 + place]))
     for copy in copies:
         copy.start()
     for copy in copies:
         copy.wait()
 
 
-def first_kernel(ids, near, far, scen_tgt, label, own, cost, normal, msg_out, us_out, inv_out):
-    want = scen_tgt[:, 0:1]
-    want = jnp.concatenate([want, want + INVERSE], axis=0)
-    found = jnp.zeros((2 * PAD, WIDTH), F32)
+def first_kernel(ids, near, far, idx, own, cost, normal, msg_out, us_out, inv_out):
+    want = scenario_targets(idx[...])
+    found = jnp.zeros((PAD, 2 * WIDTH), F32)
     for part, which in ((near, ids[0]), (far, 1 - ids[0])):
-        place = lax.broadcasted_iota(jnp.int32, (1, PLANE * OWN), 1)
-        member = place - OWN * ((place * 683) >> 16)
-        block = place + HALF * which + jnp.where(member < HALF, 0, INVERSE - HALF)
-        found += dot_nn(hot_of(want == block), part[...])
-    us = found[0:PAD, :]
-    us_out[...], inv_out[...] = us, found[PAD:, :]
-    r, d = own[...], cost[...]
-    msg_out[...] = next_message(us, r * (1.0 / d), r, d, normal, (label[0:1, :], label[1:2, :]))
+        place = lax.broadcasted_iota(jnp.int32, (1, PLANE * HALF), 1)
+        block = place + HALF * ((place * 1366) >> 16) + HALF * which
+        found += dot_nn(hot_of(want[:, 0:1] == block), part[...])
+    us = found[:, 0:WIDTH]
+    us_out[...], inv_out[...] = us, found[:, WIDTH:]
+    lifted = scenario_lift(us, normal)
+    r = own[...]
+    ru = r * (r * (1.0 / cost[...]))
+    lane = lax.broadcasted_iota(jnp.int32, (1, WIDTH), 1)
+    turned = (lane - SENT * ids[1]) & (WIDTH - 1)
+    parts = []
+    for line in products(us, lifted, ru, ru):
+        high, low = split(jnp.sum(line, axis=1, keepdims=True))
+        parts.append(jnp.where(turned == ROWS, high, jnp.where(turned == ROWS + 1, low, 0.0)))
+    rows = lax.broadcasted_iota(jnp.int32, (ROWS, WIDTH), 0)
+    column = want[0:ROWS, :]
+    for line, values in enumerate((column >> 8, column & 255)):
+        parts[line] += column_sum(jnp.where(rows == turned, values, 0).astype(F32))
+    write_message(msg_out, lifted, parts)
 
 
 def give_and_keep(found, keep, give):
@@ -220,19 +244,34 @@
     give[PAD:, :] = found[PAD : PAD + OWN, :]
 
 
-def label_sum(part, scen_tgt, own_tgt, other_tgt, hot, keep, give):
-    want = jnp.concatenate([scen_tgt[...], own_tgt[...], other_tgt[...]], axis=0)
-    lane = lax.broadcasted_iota(jnp.int32, (1, WIDTH), 1)
-    slot = lane & (PAD - 1)
-    fixed = jnp.where(slot < ROWS + 2, GAMMA, jnp.where(slot < ROWS + 4, DELTA, -1))
-    for chunk in range(CHIPS // 4):
+def label_sum(ids, part, idx, other_idx, hot, keep, give):
+    own = lax.broadcasted_iota(jnp.int32, (OWN, WIDTH), 0) + ids[2] * OWN
+    want = [scenario_targets(idx[...]), own, scenario_targets(other_idx[...])]
+    want = jnp.concatenate(want, axis=0)
+    row = lax.broadcasted_iota(jnp.int32, (2 * CHIPS, CHIPS * SENT), 0)
+    place = lax.broadcasted_iota(jnp.int32, (2 * CHIPS, CHIPS * SENT), 1)
+    line = SENT * (row & (CHIPS - 1)) + ROWS + jnp.where(row < CHIPS, 0, 1)
+    ends = dot_nn(hot_of(place == line), part[...])
+    first, second = ends[0:CHIPS, :], ends[CHIPS:, :]
+    message = lax.broadcasted_iota(jnp.int32, (CHIPS, WIDTH), 0) * SENT
+    lane = lax.broadcasted_iota(jnp.int32, (CHIPS, WIDTH), 1)
+    turned = (lane - message) & (WIDTH - 1)
+    inner = [
+        column_sum(jnp.where((turned >= ROWS) & (turned < SENT), e, 0.0)) for e in (first, second)
+    ]
+    labels = jnp.where(turned < ROWS, first * 256.0 + second, 0.0)
+    at_chunk = (message + turned) >> 7
+    for chunk in range(CHIPS * SENT // WIDTH):
         start = WIDTH * chunk
-        ends = [part[start + PAD * m + 16 : start + PAD * (m + 1), :].astype(F32) for m in range(4)]
-        ends = ends[0] + ends[1] + ends[2] + ends[3]
-        found = (ends[12:13, :] * 64.0 + ends[13:14, :]).astype(jnp.int32)
-        block = jnp.where(slot < ROWS, found, fixed)
+        found = column_sum(jnp.where(at_chunk == chunk, labels, 0.0)).astype(jnp.int32)
+        place = lax.broadcasted_iota(jnp.int32, (1, WIDTH), 1) + start
+        slot = place - SENT * ((place * 2521) >> 16)
+        block = jnp.where(slot < ROWS, found, slot - ROWS + GAMMA)
         hot[:, start : start + WIDTH] = hot_of(want == block)
     give_and_keep(dot_nn(hot[...], part[...]), keep, give)
+    for ref in (keep, give):
+        for k in range(2):
+            ref[ROWS + k : ROWS + k + 1, :] = inner[k]
 
 
 def message_sum(part, hot, keep, give):
@@ -277,7 +316,7 @@
     d_out[...], q_out[...], x_out[...], r_out[...] = dn, qn, xn, rn
     scal_out[0:1, :] = jnp.broadcast_to(gamma, (1, WIDTH))
     scal_out[1:2, :] = jnp.broadcast_to(alpha, (1, WIDTH))
-    msg_out[...] = next_message(u_s, inv * rn, rn, d, normal)
+    next_message(msg_out, u_s, inv * rn, rn, d, normal)
 
 
 def third_kernel(
@@ -294,7 +333,7 @@
     d_out[...], q_out[...], x_out[...], r_out[...] = dn, qn, xn, rn
     scal_out[0:1, :] = jnp.broadcast_to(gamma, (1, WIDTH))
     scal_out[1:2, :] = jnp.broadcast_to(alpha, (1, WIDTH))
-    msg_out[...] = next_message(u_s, inv * rn, rn, c, normal)
+    next_message(msg_out, u_s, inv * rn, rn, c, normal)
 
 
 def last_kernel(keep, got, scal, d, q, x, r, cost, x_out, r_out):
@@ -332,55 +371,61 @@
     return lax.ppermute(values, "core", [(0, 1), (1, 0)])
 
 
-def to_all(sent, axes, count):
-    copies = jnp.broadcast_to(sent[None], (count,) + sent.shape)
-    return lax.all_to_all(copies, axes, 0, 0, tiled=True).reshape(-1, WIDTH)
+def to_all(sent):
+    copies = jnp.broadcast_to(sent[None], (CHIPS,) + sent.shape)
+    near = lax.all_to_all(copies, ("x", "z", "y"), 0, 0, tiled=True)
+    return near.reshape(CHIPS * SENT, WIDTH)
 
 
 def shards(rhs, diag, couple, couple_idx, factor, pattern):
-    scen, own, msg = ((PAD, WIDTH), F32), ((OWN, WIDTH), F32), ((PAD, WIDTH), BF16)
+    scen, own, msg = ((PAD, WIDTH), F32), ((OWN, WIDTH), F32), ((SENT // 2, 2, WIDTH), BF16)
     scal, sums = ((2, WIDTH), F32), ((PAD + OWN, WIDTH), F32)
-    hots = ((PAD + OWN + PAD, CHIPS * PAD), BF16)
+    hots = ((PAD + OWN + PAD, CHIPS * SENT), BF16)
+    index = ((1, ROWS), jnp.int32)
     vec = lax.axis_index("z") * 4 + lax.axis_index("y")
-    ids = jnp.stack([lax.axis_index("core"), lax.axis_index("y"), vec]).astype(jnp.int32)
-    sent, r, cost, scen_tgt, own_tgt, label, side = call(
-        opening_kernel,
-        [
-            ((OWN, WIDTH), BF16), own, own, ((PAD, WIDTH), jnp.int32), ((OWN, WIDTH), jnp.int32),
-            scal, ((2, ROWS, WIDTH), F32),
-        ],
-        ids, scalars=1, weights=in_hbm(rhs, diag, couple_idx, pattern[0].T),
-        scratch=[own, own, ((1, ROWS), jnp.int32), ((2, ROWS), jnp.int32)], sems=4,
-    )
-    near = to_all(sent, ("z", "y"), PLANE)
-    other_tgt = other_core(scen_tgt)
+    ids = [lax.axis_index("core"), lax.axis_index("x") * PLANE + vec, vec]
+    ids = jnp.stack(ids).astype(jnp.int32)
+    sent = call(
+        opening_kernel, [((PLANE, HALF, 2 * WIDTH), BF16)], ids, scalars=1, hbm_out=True,
+        weights=in_hbm(rhs, diag), scratch=[own, own, ((HALF, 2 * WIDTH), BF16)], sems=2 + PLANE,
+    )[0]
+    near = lax.all_to_all(sent, ("z", "y"), 0, 0, tiled=True).reshape(PLANE * HALF, 2 * WIDTH)
+    other_idx = other_core(couple_idx)
     triple, wide = (ROWS, 3, WIDTH, WIDTH), (ROWS, WIDTH, 3 * WIDTH)
     bands = ((ROWS, WIDTH, BANDS * WIDTH), BF16)
     normal = call(
-        normal_kernel, [bands], side, weights=in_hbm(couple[0], factor[0]), hbm_out=True,
-        scratch=[((ROWS, WIDTH, WIDTH), BF16), (triple, BF16), (triple, BF16), (wide, BF16), bands],
-        sems=15,
+        normal_kernel, [bands], hbm_out=True, sems=16,
+        weights=in_hbm(pattern[0].T, couple[0], factor[0]),
+        scratch=[
+            ((2, ROWS), jnp.int32), ((ROWS, WIDTH, WIDTH), BF16), (triple, BF16),
+            (triple, BF16), (wide, BF16), bands,
+        ],
     )[0]
-    near, normal, other_tgt = lax.optimization_barrier((near, normal, other_tgt))
+    near, normal, other_idx = lax.optimization_barrier((near, normal, other_idx))
     far = other_core(near)
-    normal = call(load_kernel, [bands], weights=in_hbm(normal), sems=6)[0]
+    normal, r, cost, idx = call(
+        load_kernel, [bands, own, own, index], sems=9,
+        weights=in_hbm(normal, rhs, diag, couple_idx),
+    )
     sent, us, inv_s = call(
-        first_kernel, [msg, scen, scen], ids, near, far, scen_tgt, label, r, cost, normal, scalars=1
-    )
-
-    near = to_all(sent, ("x", "z", "y"), CHIPS)
-    hot, keep, give = call(label_sum, [hots, sums, sums], near, scen_tgt, own_tgt, other_tgt)
+        first_kernel, [msg, scen, scen], ids, near, far, idx, r, cost, normal, scalars=1
+    )
+
+    near = to_all(sent)
+    hot, keep, give = call(
+        label_sum, [hots, sums, sums], ids, near, idx, other_idx, scalars=1
+    )
     sent, us, ps, sc, d, q, x, r = call(
         second_kernel, [msg, scen, scen, scal, own, own, own, own],
         keep, other_core(give), us, inv_s, r, cost, normal,
     )
-    near = to_all(sent, ("x", "z", "y"), CHIPS)
+    near = to_all(sent)
     keep, give = call(message_sum, [sums, sums], near, hot)
     sent, sc, d, q, x, r = call(
         third_kernel, [msg, scal, own, own, own, own],
         keep, other_core(give), us, ps, inv_s, sc, d, q, x, r, cost, normal,
     )
-    near = to_all(sent, ("x", "z", "y"), CHIPS)
+    near = to_all(sent)
     keep, give = call(message_sum, [sums, sums], near, hot)
     return call(last_kernel, [own, own], keep, other_core(give), sc, d, q, x, r, cost)
 

time: 90.4 us -> 89.1 us (0.986)
  blocking collectives: 51.1 us -> 48 us
  Pallas kernels: 13.5 us -> 16 us
    all_to_all x3, blocking collectives: 51.1 us -> 48 us  [to_all(): near = lax.all_to_all(copies, ('x', 'z', 'y'), 0, 0, tiled=True)]
    pallas_call x10, Pallas kernels: 13.5 us -> 16 us  [call(): pl.pallas_call(kernel, out_shape=[(pltpu.HBM if hbm_out else jax.ShapeDty...]
  transfers between devices with their start and end apart: 6 -> 6, of which waited for: 4 -> 4; matrix products, arithmetic and copies ran while one was open for 0% -> 0% of each run, Pallas kernels for 8% -> 9%
where the time goes in v5:
time: 89.1 us; the launch traced here: 88.7 us
  blocking collectives  48 us (54%)
  starting transfers between devices  17.9 us (20%)
  Pallas kernels  16 us (18%)
  waiting for transfers between devices  5.45 us (6%)
    all_to_all x3, blocking collectives, to_all(): near = lax.all_to_all(copies, ('x', 'z', 'y'), 0, 0, tiled=True)  48 us
    pallas_call x10, Pallas kernels, call(): pl.pallas_call(kernel, out_shape=[(pltpu.HBM if hbm_out else jax.ShapeDty...  16 us
    ppermute x5, starting transfers between devices, other_core(): return lax.ppermute(values, 'core', [(0, 1), (1, 0)])  9.25 us
    all_to_all x1, starting transfers between devices, shards(): lax.all_to_all(sent, ('z', 'y'), 0, 0, tiled=True)  8.61 us
    all_to_all x1, waiting for transfers between devices, shards(): lax.all_to_all(sent, ('z', 'y'), 0, 0, tiled=True)  2.73 us
    ppermute x5, waiting for transfers between devices, other_core(): return lax.ppermute(values, 'core', [(0, 1), (1, 0)])  2.71 us
  transfers between devices with their start and end apart: 6, of which 4 were waited for; matrix products, arithmetic and copies ran while one was open for 0% of the time, Pallas kernels for 9%

profile of v5, /device:TPU:1, one launch (start us, length us, event | category | flops | bytes accessed | tf_op | source)
XLA Modules:
  0.0 88.7 jit_solution(17233481386977586105)
XLA Ops:
  0.7 2.3 %shard_map.77 = bf16[16,48,256]{2,1,0:T(8,128)(2,1)} custom-call(s32[3]{0:T(128)S(1)} %pad_add_fusion.ids, f32[96,128]{1,0:T(8,128)} %rhs_hbm.3, f32[96,128]{1,0:T(8,128)} %diag_hbm.3), custom_call_target="tpu_custom_call" | custom-call | tf_op jit(solution)/shard_map/pallas_call | solution.py:356
  3.0 8.6 %all-to-all-start = ((bf16[16,48,256]{2,1,0:T(8,128)(2,1)}), bf16[16,48,256]{2,1,0:T(8,128)(2,1)S(1)}, u32[]{:S(2)}, u32[]{:S(2)}) async-start(bf16[16,48,256]{2,1,0:T(8,128)(2,1)} %shard_map.77), calls=%async_computation | async-start | bytes 786432 | tf_op jit(solution)/shard_map/all_to_all | solution.py:392
  11.6 1.0 %collective-permute-start = (s32[1,24]{1,0:T(1,128)}, s32[1,24]{1,0:T(1,128)S(1)}, u32[]{:S(2)}, u32[]{:S(2)}) collective-permute-start(s32[1,24]{1,0:T(1,128)} %idx_hbm.1), channel_id=1, source_target_pairs={{0,16},{16,0},{1,17},{17,1},{2,18},{18,2},{3,19},{19,3},{4,20},{20... | collective-permute-start | bytes 296 | tf_op jit(solution)/shard_map/ppermute | solution.py:371
  12.7 5.4 %shard_map.78.normal_hbm = bf16[24,128,640]{2,1,0:T(8,128)(2,1)} custom-call(s32[2,24]{1,0:T(2,128)} %bitcast.19, bf16[24,128,128]{2,1,0:T(8,128)(2,1)} %bitcast.18, bf16[24,3,128,128]{3,2,1,0:T(8,128)(2,1)} %bitcast.17), custom_call_target="tpu_custom_call" | custom-call | tf_op jit(solution)/shard_map/pallas_call | solution.py:356
  18.1 2.7 %all-to-all-done = bf16[16,48,256]{2,1,0:T(8,128)(2,1)S(1)} async-done(((bf16[16,48,256]{2,1,0:T(8,128)(2,1)}), bf16[16,48,256]{2,1,0:T(8,128)(2,1)S(1)}, u32[]{:S(2)}, u32[]{:S(2)}) %all-to-all-start) | async-done | bytes 393248 | tf_op jit(solution)/shard_map/all_to_all | solution.py:392
  20.8 1.9 %collective-permute-start.1 = (bf16[768,256]{1,0:T(8,128)(2,1)S(1)}, bf16[768,256]{1,0:T(8,128)(2,1)S(1)}, u32[]{:S(2)}, u32[]{:S(2)}) collective-permute-start(bf16[768,256]{1,0:T(8,128)(2,1)S(1)} %bitcast.15), channel_id=1, source_target_pairs={{0,16},{16,0},{1,17},{17,1},{2,18},{18,2},{3,19},{19,3},{4,20},{20... | collective-permute-start | bytes 1179656 | tf_op jit(solution)/shard_map/ppermute | solution.py:371
  22.7 2.2 %shard_map.79 = (bf16[24,128,640]{2,1,0:T(8,128)(2,1)S(1)}, f32[96,128]{1,0:T(8,128)S(1)}, f32[96,128]{1,0:T(8,128)S(1)}, s32[1,24]{1,0:T(1,128)S(1)}) custom-call(bf16[24,128,640]{2,1,0:T(8,128)(2,1)} %shard_map.78.normal_hbm, f32[96,128]{1,0:T(8,128)} %rhs_hbm.3, f32[96,128]{1,0:T(8,128)} %diag_hbm.3, s32[1,24]{1,0:T(1,128)} %idx_hbm.1), custom_call_target="tpu_custom_call" | custom-call | tf_op jit(solution)/shard_map/pallas_call | solution.py:356
  24.8 1.8 %shard_map.80 = (bf16[13,2,128]{2,1,0:T(2,128)(2,1)S(1)}, f32[32,128]{1,0:T(8,128)S(1)}, f32[32,128]{1,0:T(8,128)S(1)}) custom-call(s32[3]{0:T(128)S(1)} %pad_add_fusion.ids, bf16[768,256]{1,0:T(8,128)(2,1)S(1)} %bitcast.16, bf16[768,256]{1,0:T(8,128)(2,1)S(1)} %collective-permute-done.1.far, s32[1,24]{1,0:T(1,128)S(1)} %get-tuple-element.35.idx, ...), custom_call_target="tpu_custom_call" | custom-call | tf_op jit(solution)/shard_map/pallas_call | solution.py:356
  26.9 17.3 %all_to_all.20 = bf16[64,13,2,128]{3,2,1,0:T(2,128)(2,1)S(1)} all-to-all(bf16[64,13,2,128]{3,2,1,0:T(2,128)(2,1)S(1)} %broadcast_in_dim.6), channel_id=1, replica_groups=mesh['x'=4,'core'=2,'z'=4,'y'=4] {'x','z','y'}, dimensions={0} | all-to-all | bytes 851968 | tf_op jit(solution)/shard_map/all_to_all | solution.py:376
  44.2 1.2 %shard_map.81 = (bf16[160,1664]{1,0:T(8,128)(2,1)S(1)}, f32[128,128]{1,0:T(8,128)S(1)}, f32[128,128]{1,0:T(8,128)S(1)}) custom-call(s32[3]{0:T(128)S(1)} %pad_add_fusion.ids, bf16[1664,128]{1,0:T(8,128)(2,1)S(1)} %bitcast.12, s32[1,24]{1,0:T(1,128)S(1)} %get-tuple-element.35.idx, s32[1,24]{1,0:T(1,128)S(1)} %collective-permute-done.other_idx), custom_call_target="tpu_custom_call" | custom-call | tf_op jit(solution)/shard_map/pallas_call | solution.py:356
  45.4 1.9 %collective-permute-start.2 = (f32[128,128]{1,0:T(8,128)S(1)}, f32[128,128]{1,0:T(8,128)S(1)}, u32[]{:S(2)}, u32[]{:S(2)}) collective-permute-start(f32[128,128]{1,0:T(8,128)S(1)} %get-tuple-element.42), channel_id=1, source_target_pairs={{0,16},{16,0},{1,17},{17,1},{2,18},{18,2},{3,19},{19,3},{4,20},{20... | collective-permute-start | bytes 196616 | tf_op jit(solution)/shard_map/ppermute | solution.py:371
  47.2 0.9 %collective-permute-done.2.got = f32[128,128]{1,0:T(8,128)S(1)} collective-permute-done((f32[128,128]{1,0:T(8,128)S(1)}, f32[128,128]{1,0:T(8,128)S(1)}, u32[]{:S(2)}, u32[]{:S(2)}) %collective-permute-start.2) | collective-permute-done | bytes 65568 | tf_op jit(solution)/shard_map/ppermute | solution.py:371
  48.1 0.9 shard_map.82
  49.0 0.2 broadcast_in_dim.7
  49.2 15.4 %all_to_all.21 = bf16[64,13,2,128]{3,2,1,0:T(2,128)(2,1)S(1)} all-to-all(bf16[64,13,2,128]{3,2,1,0:T(2,128)(2,1)S(1)} %broadcast_in_dim.7), channel_id=1, replica_groups=mesh['x'=4,'core'=2,'z'=4,'y'=4] {'x','z','y'}, dimensions={0} | all-to-all | bytes 851968 | tf_op jit(solution)/shard_map/all_to_all | solution.py:376
  64.6 0.3 shard_map.83
  64.9 2.2 %collective-permute-start.3 = (f32[128,128]{1,0:T(8,128)S(1)}, f32[128,128]{1,0:T(8,128)S(1)}, u32[]{:S(2)}, u32[]{:S(2)}) collective-permute-start(f32[128,128]{1,0:T(8,128)S(1)} %get-tuple-element.48), channel_id=1, source_target_pairs={{0,16},{16,0},{1,17},{17,1},{2,18},{18,2},{3,19},{19,3},{4,20},{20... | collective-permute-start | bytes 196616 | tf_op jit(solution)/shard_map/ppermute | solution.py:371
  67.1 0.9 %collective-permute-done.3.got = f32[128,128]{1,0:T(8,128)S(1)} collective-permute-done((f32[128,128]{1,0:T(8,128)S(1)}, f32[128,128]{1,0:T(8,128)S(1)}, u32[]{:S(2)}, u32[]{:S(2)}) %collective-permute-start.3) | collective-permute-done | bytes 65568 | tf_op jit(solution)/shard_map/ppermute | solution.py:371
  68.0 0.9 %shard_map.84 = (bf16[13,2,128]{2,1,0:T(2,128)(2,1)S(1)}, f32[2,128]{1,0:T(2,128)S(1)}, f32[96,128]{1,0:T(8,128)S(1)}, f32[96,128]{1,0:T(8,128)S(1)}, f32[96,128]{1,0:T(8,128)S(1)}, /*index=5*/f32[96,128]{1,0:T(8,128)S(1)}) custom-call(f32[128,128]{1,0:T(8,128)S(1)} %get-tuple-element.47.keep, f32[128,128]{1,0:T(8,128)S(1)} %collective-permute-done.3.got, ...), custom_call_target="tpu_custom_call" | custom-call | tf_op jit(solution)/shard_map/pallas_call | solution.py:356
  69.2 15.3 %all_to_all.22 = bf16[64,13,2,128]{3,2,1,0:T(2,128)(2,1)S(1)} all-to-all(bf16[64,13,2,128]{3,2,1,0:T(2,128)(2,1)S(1)} %broadcast_in_dim.8), channel_id=1, replica_groups=mesh['x'=4,'core'=2,'z'=4,'y'=4] {'x','z','y'}, dimensions={0} | all-to-all | bytes 851968 | tf_op jit(solution)/shard_map/all_to_all | solution.py:376
  84.5 0.3 shard_map.85
  84.8 2.2 %collective-permute-start.4 = (f32[128,128]{1,0:T(8,128)S(1)}, f32[128,128]{1,0:T(8,128)S(1)}, u32[]{:S(2)}, u32[]{:S(2)}) collective-permute-start(f32[128,128]{1,0:T(8,128)S(1)} %get-tuple-element.58), channel_id=1, source_target_pairs={{0,16},{16,0},{1,17},{17,1},{2,18},{18,2},{3,19},{19,3},{4,20},{20... | collective-permute-start | bytes 196616 | tf_op jit(solution)/shard_map/ppermute | solution.py:371
  87.0 0.9 %collective-permute-done.4.got = f32[128,128]{1,0:T(8,128)S(1)} collective-permute-done((f32[128,128]{1,0:T(8,128)S(1)}, f32[128,128]{1,0:T(8,128)S(1)}, u32[]{:S(2)}, u32[]{:S(2)}) %collective-permute-start.4) | collective-permute-done | bytes 65568 | tf_op jit(solution)/shard_map/ppermute | solution.py:371
  87.9 0.8 shard_map.86
  (5 shorter events, 0.5 us)
Async XLA Ops:
  3.0 17.8 %all-to-all-start = ((bf16[16,48,256]{2,1,0:T(8,128)(2,1)}), bf16[16,48,256]{2,1,0:T(8,128)(2,1)S(1)}, u32[]{:S(2)}, u32[]{:S(2)}) async-start(bf16[16,48,256]{2,1,0:T(8,128)(2,1)} %shard_map.77), calls=%async_computation | async-start | bytes 786432 | tf_op jit(solution)/shard_map/all_to_all | solution.py:392
  11.6 6.4 %collective-permute-start = (s32[1,24]{1,0:T(1,128)}, s32[1,24]{1,0:T(1,128)S(1)}, u32[]{:S(2)}, u32[]{:S(2)}) collective-permute-start(s32[1,24]{1,0:T(1,128)} %idx_hbm.1), channel_id=1, source_target_pairs={{0,16},{16,0},{1,17},{17,1},{2,18},{18,2},{3,19},{19,3},{4,20},{20... | collective-permute-start | bytes 296 | tf_op jit(solution)/shard_map/ppermute | solution.py:371
  20.8 4.0 %collective-permute-start.1 = (bf16[768,256]{1,0:T(8,128)(2,1)S(1)}, bf16[768,256]{1,0:T(8,128)(2,1)S(1)}, u32[]{:S(2)}, u32[]{:S(2)}) collective-permute-start(bf16[768,256]{1,0:T(8,128)(2,1)S(1)} %bitcast.15), channel_id=1, source_target_pairs={{0,16},{16,0},{1,17},{17,1},{2,18},{18,2},{3,19},{19,3},{4,20},{20... | collective-permute-start | bytes 1179656 | tf_op jit(solution)/shard_map/ppermute | solution.py:371
  45.4 2.8 %collective-permute-start.2 = (f32[128,128]{1,0:T(8,128)S(1)}, f32[128,128]{1,0:T(8,128)S(1)}, u32[]{:S(2)}, u32[]{:S(2)}) collective-permute-start(f32[128,128]{1,0:T(8,128)S(1)} %get-tuple-element.42), channel_id=1, source_target_pairs={{0,16},{16,0},{1,17},{17,1},{2,18},{18,2},{3,19},{19,3},{4,20},{20... | collective-permute-start | bytes 196616 | tf_op jit(solution)/shard_map/ppermute | solution.py:371
  64.9 3.1 %collective-permute-start.3 = (f32[128,128]{1,0:T(8,128)S(1)}, f32[128,128]{1,0:T(8,128)S(1)}, u32[]{:S(2)}, u32[]{:S(2)}) collective-permute-start(f32[128,128]{1,0:T(8,128)S(1)} %get-tuple-element.48), channel_id=1, source_target_pairs={{0,16},{16,0},{1,17},{17,1},{2,18},{18,2},{3,19},{19,3},{4,20},{20... | collective-permute-start | bytes 196616 | tf_op jit(solution)/shard_map/ppermute | solution.py:371
  84.8 3.1 %collective-permute-start.4 = (f32[128,128]{1,0:T(8,128)S(1)}, f32[128,128]{1,0:T(8,128)S(1)}, u32[]{:S(2)}, u32[]{:S(2)}) collective-permute-start(f32[128,128]{1,0:T(8,128)S(1)} %get-tuple-element.58), channel_id=1, source_target_pairs={{0,16},{16,0},{1,17},{17,1},{2,18},{18,2},{3,19},{19,3},{4,20},{20... | collective-permute-start | bytes 196616 | tf_op jit(solution)/shard_map/ppermute | solution.py:371

commit v6 on v5

--- a/solution.py
+++ b/solution.py
@@ -16,6 +16,7 @@
 CHIPS = 64
 PLANE = 16
 BANDS = 5
+COPIES = 8
 GAMMA, DELTA = 4000, 4001
 F32, BF16 = jnp.float32, jnp.bfloat16
 
@@ -59,8 +60,12 @@
     out = lifted
     for place, line in enumerate(lines):
         out = jnp.where(rows == ROWS + place, jnp.broadcast_to(line, out.shape), out)
-    for pair in range(SENT // 2):
-        msg_out[pair] = out[2 * pair : 2 * pair + 2, :].astype(BF16)
+    row = lax.broadcasted_iota(jnp.int32, (COPIES * SENT, PAD), 0)
+    column = lax.broadcasted_iota(jnp.int32, (COPIES * SENT, PAD), 1)
+    again = hot_of(row - SENT * ((row * 2521) >> 16) == column)
+    block = dot_nn(again, out.astype(BF16)).astype(BF16)
+    for start in range(0, CHIPS * SENT, COPIES * SENT):
+        msg_out[start : start + COPIES * SENT, :] = block
 
 
 def column_sum(values):
@@ -95,7 +100,12 @@
     return jnp.concatenate([as_column(idx).astype(jnp.int32), rest], axis=0)
 
 
-def opening_kernel(ids, rhs_hbm, diag_hbm, msg_hbm, rhs, diag, msg, sems):
+def here():
+    vec = lax.axis_index("z") * 4 + lax.axis_index("y")
+    return lax.axis_index("core"), lax.axis_index("x") * PLANE + vec, vec
+
+
+def opening_kernel(rhs_hbm, diag_hbm, msg_hbm, rhs, diag, msg, sems):
     copies = (
         pltpu.make_async_copy(rhs_hbm, rhs, sems.at[0]),
         pltpu.make_async_copy(diag_hbm, diag, sems.at[1]),
@@ -104,7 +114,7 @@
         copy.start()
     for copy in copies:
         copy.wait()
-    mine = pl.ds(pl.multiple_of(ids[0] * HALF, HALF), HALF)
+    mine = pl.ds(pl.multiple_of(here()[0] * HALF, HALF), HALF)
     inverse = 1.0 / diag[mine, :]
     msg[:, 0:WIDTH] = (rhs[mine, :] * inverse).astype(BF16)
     msg[:, WIDTH:] = inverse.astype(BF16)
@@ -203,38 +213,66 @@
         copy.wait()
 
 
-def load_kernel(normal_hbm, rhs_hbm, diag_hbm, idx_hbm, normal, rhs, diag, idx, sems):
-    copies = copy_parts(normal_hbm, normal, sems, 0, 6)
-    for place, pair in enumerate(((rhs_hbm, rhs), (diag_hbm, diag), (idx_hbm, idx))):
-        copies.append(pltpu.make_async_copy(*pair, sems.at[6 + place]))
+def fetched(part, which, want):
+    place = lax.broadcasted_iota(jnp.int32, (1, PLANE * HALF), 1)
+    block = place + HALF * ((place * 1366) >> 16) + HALF * which
+    return dot_nn(hot_of(want[:, 0:1] == block), part[...])
+
+
+def load_kernel(
+    near, normal_hbm, rhs_hbm, diag_hbm, idx_hbm, other_hbm,
+    normal, rhs, diag, targets, labels, selector, found, idx, sems,
+):
+    core, chip, vec = here()
+    index = [
+        pltpu.make_async_copy(hbm, idx.at[k], sems.at[8 + k])
+        for k, hbm in enumerate((idx_hbm, other_hbm))
+    ]
+    copies = [
+        pltpu.make_async_copy(rhs_hbm, rhs, sems.at[6]),
+        pltpu.make_async_copy(diag_hbm, diag, sems.at[7]),
+    ]
+    copies += copy_parts(normal_hbm, normal, sems, 0, 6)
+    for copy in index + copies:
+        copy.start()
+    row = lax.broadcasted_iota(jnp.int32, (2 * CHIPS, CHIPS * SENT), 0)
+    place = lax.broadcasted_iota(jnp.int32, (2 * CHIPS, CHIPS * SENT), 1)
+    line = SENT * (row & (CHIPS - 1)) + ROWS + jnp.where(row < CHIPS, 0, 1)
+    selector[...] = hot_of(place == line)
+    for copy in index:
+        copy.wait()
+    want = scenario_targets(idx[0])
+    targets[0:PAD, :] = want
+    targets[PAD : PAD + OWN, :] = lax.broadcasted_iota(jnp.int32, (OWN, WIDTH), 0) + vec * OWN
+    targets[PAD + OWN :, :] = scenario_targets(idx[1])
+    found[...] = fetched(near, core, want)
+    lane = lax.broadcasted_iota(jnp.int32, (ROWS, WIDTH), 1)
+    rows = lax.broadcasted_iota(jnp.int32, (ROWS, WIDTH), 0)
+    mine = rows == (lane - SENT * chip) & (WIDTH - 1)
+    column = want[0:ROWS, :]
+    for line, values in enumerate((column >> 8, column & 255)):
+        labels[line : line + 1, :] = column_sum(jnp.where(mine, values, 0).astype(F32))
     for copy in copies:
-        copy.start()
-    for copy in copies:
-        copy.wait()
-
-
-def first_kernel(ids, near, far, idx, own, cost, normal, msg_out, us_out, inv_out):
-    want = scenario_targets(idx[...])
-    found = jnp.zeros((PAD, 2 * WIDTH), F32)
-    for part, which in ((near, ids[0]), (far, 1 - ids[0])):
-        place = lax.broadcasted_iota(jnp.int32, (1, PLANE * HALF), 1)
-        block = place + HALF * ((place * 1366) >> 16) + HALF * which
-        found += dot_nn(hot_of(want[:, 0:1] == block), part[...])
-    us = found[:, 0:WIDTH]
-    us_out[...], inv_out[...] = us, found[:, WIDTH:]
+        copy.wait()
+
+
+def first_kernel(
+    far, targets, labels, found, own, cost, normal, msg_out, us_out, inv_out
+):
+    core, chip, _ = here()
+    total = found[...] + fetched(far, 1 - core, targets[0:PAD, :])
+    us = total[:, 0:WIDTH]
+    us_out[...], inv_out[...] = us, total[:, WIDTH:]
     lifted = scenario_lift(us, normal)
     r = own[...]
     ru = r * (r * (1.0 / cost[...]))
     lane = lax.broadcasted_iota(jnp.int32, (1, WIDTH), 1)
-    turned = (lane - SENT * ids[1]) & (WIDTH - 1)
+    turned = (lane - SENT * chip) & (WIDTH - 1)
     parts = []
-    for line in products(us, lifted, ru, ru):
+    for k, line in enumerate(products(us, lifted, ru, ru)):
         high, low = split(jnp.sum(line, axis=1, keepdims=True))
-        parts.append(jnp.where(turned == ROWS, high, jnp.where(turned == ROWS + 1, low, 0.0)))
-    rows = lax.broadcasted_iota(jnp.int32, (ROWS, WIDTH), 0)
-    column = want[0:ROWS, :]
-    for line, values in enumerate((column >> 8, column & 255)):
-        parts[line] += column_sum(jnp.where(rows == turned, values, 0).astype(F32))
+        line = labels[k : k + 1, :]
+        parts.append(jnp.where(turned == ROWS, high, jnp.where(turned == ROWS + 1, low, line)))
     write_message(msg_out, lifted, parts)
 
 
@@ -244,14 +282,9 @@
     give[PAD:, :] = found[PAD : PAD + OWN, :]
 
 
-def label_sum(ids, part, idx, other_idx, hot, keep, give):
-    own = lax.broadcasted_iota(jnp.int32, (OWN, WIDTH), 0) + ids[2] * OWN
-    want = [scenario_targets(idx[...]), own, scenario_targets(other_idx[...])]
-    want = jnp.concatenate(want, axis=0)
-    row = lax.broadcasted_iota(jnp.int32, (2 * CHIPS, CHIPS * SENT), 0)
-    place = lax.broadcasted_iota(jnp.int32, (2 * CHIPS, CHIPS * SENT), 1)
-    line = SENT * (row & (CHIPS - 1)) + ROWS + jnp.where(row < CHIPS, 0, 1)
-    ends = dot_nn(hot_of(place == line), part[...])
+def label_sum(part, targets, selector, hot, keep, give):
+    want = targets[...]
+    ends = dot_nn(selector[...], part[...])
     first, second = ends[0:CHIPS, :], ends[CHIPS:, :]
     message = lax.broadcasted_iota(jnp.int32, (CHIPS, WIDTH), 0) * SENT
     lane = lax.broadcasted_iota(jnp.int32, (CHIPS, WIDTH), 1)
@@ -346,10 +379,9 @@
     x_out[...], r_out[...] = found[6], found[7]
 
 
-def call(kernel, shapes, *args, scalars=0, weights=(), scratch=(), sems=0, hbm_out=False):
+def call(kernel, shapes, *args, weights=(), scratch=(), sems=0, hbm_out=False):
     vmem = pl.BlockSpec(memory_space=pltpu.VMEM)
-    specs = [pl.BlockSpec(memory_space=pltpu.SMEM)] * scalars + [vmem] * (len(args) - scalars)
-    specs += [pl.BlockSpec(memory_space=pltpu.HBM)] * len(weights)
+    specs = [vmem] * len(args) + [pl.BlockSpec(memory_space=pltpu.HBM)] * len(weights)
     scratch = [pltpu.VMEM(s, t) for s, t in scratch]
     if sems:
         scratch.append(pltpu.SemaphoreType.DMA((sems,)))
@@ -372,21 +404,19 @@
 
 
 def to_all(sent):
-    copies = jnp.broadcast_to(sent[None], (CHIPS,) + sent.shape)
-    near = lax.all_to_all(copies, ("x", "z", "y"), 0, 0, tiled=True)
+    sent = sent.reshape(CHIPS, SENT // 2, 2, WIDTH)
+    near = lax.all_to_all(sent, ("x", "z", "y"), 0, 0, tiled=True)
     return near.reshape(CHIPS * SENT, WIDTH)
 
 
 def shards(rhs, diag, couple, couple_idx, factor, pattern):
-    scen, own, msg = ((PAD, WIDTH), F32), ((OWN, WIDTH), F32), ((SENT // 2, 2, WIDTH), BF16)
+    scen, own, msg = ((PAD, WIDTH), F32), ((OWN, WIDTH), F32), ((CHIPS * SENT, WIDTH), BF16)
     scal, sums = ((2, WIDTH), F32), ((PAD + OWN, WIDTH), F32)
     hots = ((PAD + OWN + PAD, CHIPS * SENT), BF16)
-    index = ((1, ROWS), jnp.int32)
-    vec = lax.axis_index("z") * 4 + lax.axis_index("y")
-    ids = [lax.axis_index("core"), lax.axis_index("x") * PLANE + vec, vec]
-    ids = jnp.stack(ids).astype(jnp.int32)
+    aims = ((PAD + OWN + PAD, WIDTH), jnp.int32)
+    selectors = ((2 * CHIPS, CHIPS * SENT), BF16)
     sent = call(
-        opening_kernel, [((PLANE, HALF, 2 * WIDTH), BF16)], ids, scalars=1, hbm_out=True,
+        opening_kernel, [((PLANE, HALF, 2 * WIDTH), BF16)], hbm_out=True,
         weights=in_hbm(rhs, diag), scratch=[own, own, ((HALF, 2 * WIDTH), BF16)], sems=2 + PLANE,
     )[0]
     near = lax.all_to_all(sent, ("z", "y"), 0, 0, tiled=True).reshape(PLANE * HALF, 2 * WIDTH)
@@ -403,18 +433,18 @@
     )[0]
     near, normal, other_idx = lax.optimization_barrier((near, normal, other_idx))
     far = other_core(near)
-    normal, r, cost, idx = call(
-        load_kernel, [bands, own, own, index], sems=9,
-        weights=in_hbm(normal, rhs, diag, couple_idx),
+    normal, r, cost, targets, labels, selector, found = call(
+        load_kernel, [bands, own, own, aims, scal, selectors, ((PAD, 2 * WIDTH), F32)],
+        near, weights=in_hbm(normal, rhs, diag, couple_idx, other_idx),
+        scratch=[((2, 1, ROWS), jnp.int32)], sems=10,
     )
     sent, us, inv_s = call(
-        first_kernel, [msg, scen, scen], ids, near, far, idx, r, cost, normal, scalars=1
+        first_kernel, [msg, scen, scen],
+        far, targets, labels, found, r, cost, normal,
     )
 
     near = to_all(sent)
-    hot, keep, give = call(
-        label_sum, [hots, sums, sums], ids, near, idx, other_idx, scalars=1
-    )
+    hot, keep, give = call(label_sum, [hots, sums, sums], near, targets, selector)
     sent, us, ps, sc, d, q, x, r = call(
         second_kernel, [msg, scen, scen, scal, own, own, own, own],
         keep, other_core(give), us, inv_s, r, cost, normal,

time: 89.1 us -> 87.1 us (0.978)
  Pallas kernels: 16 us -> 14.7 us
    pallas_call x10, Pallas kernels: 16 us -> 14.7 us  [call(): pl.pallas_call(kernel, out_shape=[(pltpu.HBM if hbm_out else jax.ShapeDty...]
where the time goes in v6:
time: 87.1 us; the launch traced here: 86.7 us
  blocking collectives  47.9 us (55%)
  starting transfers between devices  17.9 us (21%)
  Pallas kernels  14.7 us (17%)
  waiting for transfers between devices  5.44 us (6%)
    all_to_all x3, blocking collectives, to_all(): near = lax.all_to_all(sent, ('x', 'z', 'y'), 0, 0, tiled=True)  47.9 us
    pallas_call x10, Pallas kernels, call(): pl.pallas_call(kernel, out_shape=[(pltpu.HBM if hbm_out else jax.ShapeDty...  14.7 us
    ppermute x5, starting transfers between devices, other_core(): return lax.ppermute(values, 'core', [(0, 1), (1, 0)])  9.27 us
    all_to_all x1, starting transfers between devices, shards(): lax.all_to_all(sent, ('z', 'y'), 0, 0, tiled=True)  8.61 us
    all_to_all x1, waiting for transfers between devices, shards(): lax.all_to_all(sent, ('z', 'y'), 0, 0, tiled=True)  2.72 us
    ppermute x5, waiting for transfers between devices, other_core(): return lax.ppermute(values, 'core', [(0, 1), (1, 0)])  2.71 us
  transfers between devices with their start and end apart: 6, of which 4 were waited for; matrix products, arithmetic and copies ran while one was open for 0% of the time, Pallas kernels for 9%

profile of v6, /device:TPU:1, one launch (start us, length us, event | category | flops | bytes accessed | tf_op | source)
XLA Modules:
  0.0 86.7 jit_solution(8708014426050697311)
XLA Ops:
  0.6 1.7 %shard_map.77 = bf16[16,48,256]{2,1,0:T(8,128)(2,1)} custom-call(f32[96,128]{1,0:T(8,128)} %rhs_hbm.3, f32[96,128]{1,0:T(8,128)} %diag_hbm.3), custom_call_target="tpu_custom_call" | custom-call | tf_op jit(solution)/shard_map/pallas_call | solution.py:388
  2.4 8.6 %all-to-all-start = ((bf16[16,48,256]{2,1,0:T(8,128)(2,1)}), bf16[16,48,256]{2,1,0:T(8,128)(2,1)S(1)}, u32[]{:S(2)}, u32[]{:S(2)}) async-start(bf16[16,48,256]{2,1,0:T(8,128)(2,1)} %shard_map.77), calls=%async_computation | async-start | bytes 786432 | tf_op jit(solution)/shard_map/all_to_all | solution.py:422
  11.0 1.0 %collective-permute-start = (s32[1,24]{1,0:T(1,128)}, s32[1,24]{1,0:T(1,128)S(1)}, u32[]{:S(2)}, u32[]{:S(2)}) collective-permute-start(s32[1,24]{1,0:T(1,128)} %idx_hbm.1), channel_id=1, source_target_pairs={{0,16},{16,0},{1,17},{17,1},{2,18},{18,2},{3,19},{19,3},{4,20},{20... | collective-permute-start | bytes 296 | tf_op jit(solution)/shard_map/ppermute | solution.py:403
  12.0 5.4 %shard_map.78.normal_hbm = bf16[24,128,640]{2,1,0:T(8,128)(2,1)} custom-call(s32[2,24]{1,0:T(2,128)} %bitcast.22, bf16[24,128,128]{2,1,0:T(8,128)(2,1)} %bitcast.21, bf16[24,3,128,128]{3,2,1,0:T(8,128)(2,1)} %bitcast.20), custom_call_target="tpu_custom_call" | custom-call | tf_op jit(solution)/shard_map/pallas_call | solution.py:388
  17.4 0.0 copy-start
  17.5 2.7 %all-to-all-done = bf16[16,48,256]{2,1,0:T(8,128)(2,1)S(1)} async-done(((bf16[16,48,256]{2,1,0:T(8,128)(2,1)}), bf16[16,48,256]{2,1,0:T(8,128)(2,1)S(1)}, u32[]{:S(2)}, u32[]{:S(2)}) %all-to-all-start) | async-done | bytes 393248 | tf_op jit(solution)/shard_map/all_to_all | solution.py:422
  20.2 1.9 %collective-permute-start.1 = (bf16[768,256]{1,0:T(8,128)(2,1)S(1)}, bf16[768,256]{1,0:T(8,128)(2,1)S(1)}, u32[]{:S(2)}, u32[]{:S(2)}) collective-permute-start(bf16[768,256]{1,0:T(8,128)(2,1)S(1)} %bitcast.15), channel_id=1, source_target_pairs={{0,16},{16,0},{1,17},{17,1},{2,18},{18,2},{3,19},{19,3},{4,20},{20... | collective-permute-start | bytes 1179656 | tf_op jit(solution)/shard_map/ppermute | solution.py:403
  22.0 2.3 %shard_map.79 = (bf16[24,128,640]{2,1,0:T(8,128)(2,1)S(1)}, f32[96,128]{1,0:T(8,128)S(1)}, f32[96,128]{1,0:T(8,128)S(1)}, s32[160,128]{1,0:T(8,128)S(1)}, f32[2,...) custom-call(bf16[768,256]{1,0:T(8,128)(2,1)S(1)} %bitcast.16, ...), custom_call_target="tpu_custom_call" | custom-call | tf_op jit(solution)/shard_map/pallas_call | solution.py:388
  24.3 1.3 %shard_map.80 = (bf16[1664,128]{1,0:T(8,128)(2,1)S(1)}, f32[32,128]{1,0:T(8,128)S(1)}, f32[32,128]{1,0:T(8,128)S(1)}) custom-call(bf16[768,256]{1,0:T(8,128)(2,1)S(1)} %collective-permute-done.1.far, s32[160,128]{1,0:T(8,128)S(1)} %get-tuple-element.39.targets, f32[2,128]{1,0:T(2,128)S(1)} %get-tuple-element.40.labels, ...), custom_call_target="tpu_custom_call" | custom-call | tf_op jit(solution)/shard_map/pallas_call | solution.py:388
  25.6 17.2 %all_to_all.20 = bf16[64,13,2,128]{3,2,1,0:T(2,128)(2,1)S(1)} all-to-all(bf16[64,13,2,128]{3,2,1,0:T(2,128)(2,1)S(1)} %bitcast.19), channel_id=1, replica_groups=mesh['x'=4,'core'=2,'z'=4,'y'=4] {'x','z','y'}, dimensions={0} | all-to-all | bytes 851968 | tf_op jit(solution)/shard_map/all_to_all | solution.py:408
  42.9 0.6 shard_map.81
  43.5 1.9 %collective-permute-start.2 = (f32[128,128]{1,0:T(8,128)S(1)}, f32[128,128]{1,0:T(8,128)S(1)}, u32[]{:S(2)}, u32[]{:S(2)}) collective-permute-start(f32[128,128]{1,0:T(8,128)S(1)} %get-tuple-element.48), channel_id=1, source_target_pairs={{0,16},{16,0},{1,17},{17,1},{2,18},{18,2},{3,19},{19,3},{4,20},{20... | collective-permute-start | bytes 196616 | tf_op jit(solution)/shard_map/ppermute | solution.py:403
  45.4 0.9 %collective-permute-done.2.got = f32[128,128]{1,0:T(8,128)S(1)} collective-permute-done((f32[128,128]{1,0:T(8,128)S(1)}, f32[128,128]{1,0:T(8,128)S(1)}, u32[]{:S(2)}, u32[]{:S(2)}) %collective-permute-start.2) | collective-permute-done | bytes 65568 | tf_op jit(solution)/shard_map/ppermute | solution.py:403
  46.3 1.0 %shard_map.82 = (bf16[1664,128]{1,0:T(8,128)(2,1)S(1)}, f32[32,128]{1,0:T(8,128)S(1)}, f32[32,128]{1,0:T(8,128)S(1)}, f32[2,128]{1,0:T(2,128)S(1)}, f32[96,128]{...) custom-call(f32[128,128]{1,0:T(8,128)S(1)} %get-tuple-element.47.keep, ...), custom_call_target="tpu_custom_call" | custom-call | tf_op jit(solution)/shard_map/pallas_call | solution.py:388
  47.3 15.4 %all_to_all.21 = bf16[64,13,2,128]{3,2,1,0:T(2,128)(2,1)S(1)} all-to-all(bf16[64,13,2,128]{3,2,1,0:T(2,128)(2,1)S(1)} %bitcast.18), channel_id=1, replica_groups=mesh['x'=4,'core'=2,'z'=4,'y'=4] {'x','z','y'}, dimensions={0} | all-to-all | bytes 851968 | tf_op jit(solution)/shard_map/all_to_all | solution.py:408
  62.7 0.3 shard_map.83
  63.0 2.2 %collective-permute-start.3 = (f32[128,128]{1,0:T(8,128)S(1)}, f32[128,128]{1,0:T(8,128)S(1)}, u32[]{:S(2)}, u32[]{:S(2)}) collective-permute-start(f32[128,128]{1,0:T(8,128)S(1)} %get-tuple-element.54), channel_id=1, source_target_pairs={{0,16},{16,0},{1,17},{17,1},{2,18},{18,2},{3,19},{19,3},{4,20},{20... | collective-permute-start | bytes 196616 | tf_op jit(solution)/shard_map/ppermute | solution.py:403
  65.2 0.9 %collective-permute-done.3.got = f32[128,128]{1,0:T(8,128)S(1)} collective-permute-done((f32[128,128]{1,0:T(8,128)S(1)}, f32[128,128]{1,0:T(8,128)S(1)}, u32[]{:S(2)}, u32[]{:S(2)}) %collective-permute-start.3) | collective-permute-done | bytes 65568 | tf_op jit(solution)/shard_map/ppermute | solution.py:403
  66.1 1.0 %shard_map.84 = (bf16[1664,128]{1,0:T(8,128)(2,1)S(1)}, f32[2,128]{1,0:T(2,128)S(1)}, f32[96,128]{1,0:T(8,128)S(1)}, f32[96,128]{1,0:T(8,128)S(1)}, f32[96,128]{1,0:T(8,128)S(1)}, /*index=5*/f32[96,128]{1,0:T(8,128)S(1)}) custom-call(f32[128,128]{1,0:T(8,128)S(1)} %get-tuple-element.53.keep, f32[128,128]{1,0:T(8,128)S(1)} %collective-permute-done.3.got, ...), custom_call_target="tpu_custom_call" | custom-call | tf_op jit(solution)/shard_map/pallas_call | solution.py:388
  67.2 15.3 %all_to_all.22 = bf16[64,13,2,128]{3,2,1,0:T(2,128)(2,1)S(1)} all-to-all(bf16[64,13,2,128]{3,2,1,0:T(2,128)(2,1)S(1)} %bitcast.17), channel_id=1, replica_groups=mesh['x'=4,'core'=2,'z'=4,'y'=4] {'x','z','y'}, dimensions={0} | all-to-all | bytes 851968 | tf_op jit(solution)/shard_map/all_to_all | solution.py:408
  82.5 0.3 shard_map.85
  82.8 2.2 %collective-permute-start.4 = (f32[128,128]{1,0:T(8,128)S(1)}, f32[128,128]{1,0:T(8,128)S(1)}, u32[]{:S(2)}, u32[]{:S(2)}) collective-permute-start(f32[128,128]{1,0:T(8,128)S(1)} %get-tuple-element.64), channel_id=1, source_target_pairs={{0,16},{16,0},{1,17},{17,1},{2,18},{18,2},{3,19},{19,3},{4,20},{20... | collective-permute-start | bytes 196616 | tf_op jit(solution)/shard_map/ppermute | solution.py:403
  85.0 0.9 %collective-permute-done.4.got = f32[128,128]{1,0:T(8,128)S(1)} collective-permute-done((f32[128,128]{1,0:T(8,128)S(1)}, f32[128,128]{1,0:T(8,128)S(1)}, u32[]{:S(2)}, u32[]{:S(2)}) %collective-permute-start.4) | collective-permute-done | bytes 65568 | tf_op jit(solution)/shard_map/ppermute | solution.py:403
  85.9 0.8 shard_map.86
  (3 shorter events, 0.0 us)
Async XLA Ops:
  2.4 17.8 %all-to-all-start = ((bf16[16,48,256]{2,1,0:T(8,128)(2,1)}), bf16[16,48,256]{2,1,0:T(8,128)(2,1)S(1)}, u32[]{:S(2)}, u32[]{:S(2)}) async-start(bf16[16,48,256]{2,1,0:T(8,128)(2,1)} %shard_map.77), calls=%async_computation | async-start | bytes 786432 | tf_op jit(solution)/shard_map/all_to_all | solution.py:422
  11.0 6.4 %collective-permute-start = (s32[1,24]{1,0:T(1,128)}, s32[1,24]{1,0:T(1,128)S(1)}, u32[]{:S(2)}, u32[]{:S(2)}) collective-permute-start(s32[1,24]{1,0:T(1,128)} %idx_hbm.1), channel_id=1, source_target_pairs={{0,16},{16,0},{1,17},{17,1},{2,18},{18,2},{3,19},{19,3},{4,20},{20... | collective-permute-start | bytes 296 | tf_op jit(solution)/shard_map/ppermute | solution.py:403
  17.4 4.6 %copy-start = (s32[1,24]{1,0:T(1,128)}, s32[1,24]{1,0:T(1,128)S(1)}, u32[]{:S(2)}) copy-start(s32[1,24]{1,0:T(1,128)S(1)} %collective-permute-done.other_hbm) | copy-start | bytes 292
  20.2 4.1 %collective-permute-start.1 = (bf16[768,256]{1,0:T(8,128)(2,1)S(1)}, bf16[768,256]{1,0:T(8,128)(2,1)S(1)}, u32[]{:S(2)}, u32[]{:S(2)}) collective-permute-start(bf16[768,256]{1,0:T(8,128)(2,1)S(1)} %bitcast.15), channel_id=1, source_target_pairs={{0,16},{16,0},{1,17},{17,1},{2,18},{18,2},{3,19},{19,3},{4,20},{20... | collective-permute-start | bytes 1179656 | tf_op jit(solution)/shard_map/ppermute | solution.py:403
  43.5 2.8 %collective-permute-start.2 = (f32[128,128]{1,0:T(8,128)S(1)}, f32[128,128]{1,0:T(8,128)S(1)}, u32[]{:S(2)}, u32[]{:S(2)}) collective-permute-start(f32[128,128]{1,0:T(8,128)S(1)} %get-tuple-element.48), channel_id=1, source_target_pairs={{0,16},{16,0},{1,17},{17,1},{2,18},{18,2},{3,19},{19,3},{4,20},{20... | collective-permute-start | bytes 196616 | tf_op jit(solution)/shard_map/ppermute | solution.py:403
  63.0 3.1 %collective-permute-start.3 = (f32[128,128]{1,0:T(8,128)S(1)}, f32[128,128]{1,0:T(8,128)S(1)}, u32[]{:S(2)}, u32[]{:S(2)}) collective-permute-start(f32[128,128]{1,0:T(8,128)S(1)} %get-tuple-element.54), channel_id=1, source_target_pairs={{0,16},{16,0},{1,17},{17,1},{2,18},{18,2},{3,19},{19,3},{4,20},{20... | collective-permute-start | bytes 196616 | tf_op jit(solution)/shard_map/ppermute | solution.py:403
  82.8 3.1 %collective-permute-start.4 = (f32[128,128]{1,0:T(8,128)S(1)}, f32[128,128]{1,0:T(8,128)S(1)}, u32[]{:S(2)}, u32[]{:S(2)}) collective-permute-start(f32[128,128]{1,0:T(8,128)S(1)} %get-tuple-element.64), channel_id=1, source_target_pairs={{0,16},{16,0},{1,17},{17,1},{2,18},{18,2},{3,19},{19,3},{4,20},{20... | collective-permute-start | bytes 196616 | tf_op jit(solution)/shard_map/ppermute | solution.py:403

commit v7 on v6

--- a/solution.py
+++ b/solution.py
@@ -15,7 +15,7 @@
 WIDTH = 128
 CHIPS = 64
 PLANE = 16
-BANDS = 5
+UPPER, LOWER = 3, 2
 COPIES = 8
 GAMMA, DELTA = 4000, 4001
 F32, BF16 = jnp.float32, jnp.bfloat16
@@ -43,15 +43,16 @@
     return jnp.where(rows == r, values, 0.0).astype(BF16)
 
 
-def scenario_lift(y, normal):
-    spread = jnp.zeros((PAD, BANDS * WIDTH), F32)
+def scenario_lift(y, upper, lower):
+    spread = jnp.zeros((PAD, (LOWER + UPPER) * WIDTH), F32)
     for r in range(0, ROWS, 2):
         pair = jnp.concatenate([only_row(y, r), only_row(y, r + 1)], axis=1)
-        spread += dot_nn(pair, normal[r : r + 2].reshape(2 * WIDTH, BANDS * WIDTH))
-    lifted = spread[:, 2 * WIDTH : 3 * WIDTH]
+        blocks = [m[r : r + 2].reshape(2 * WIDTH, m.shape[2]) for m in (lower, upper)]
+        spread += dot_nn(pair, jnp.concatenate(blocks, axis=1))
+    lifted = spread[:, LOWER * WIDTH : (LOWER + 1) * WIDTH]
     for band in (0, 1, 3, 4):
         part = spread[:, band * WIDTH : (band + 1) * WIDTH]
-        lifted += pltpu.roll(part, (band - 2) % PAD, 0)
+        lifted += pltpu.roll(part, (band - LOWER) % PAD, 0)
     return lifted
 
 
@@ -82,8 +83,8 @@
     return jnp.where(lane < WIDTH // 2, high, low)
 
 
-def next_message(msg_out, us, u, r, cost, normal):
-    lifted = scenario_lift(us, normal)
+def next_message(msg_out, us, u, r, cost, upper, lower):
+    lifted = scenario_lift(us, upper, lower)
     write_message(msg_out, lifted, [folded(v) for v in products(us, lifted, r * u, cost * u * u)])
 
 
@@ -103,28 +104,6 @@
 def here():
     vec = lax.axis_index("z") * 4 + lax.axis_index("y")
     return lax.axis_index("core"), lax.axis_index("x") * PLANE + vec, vec
-
-
-def opening_kernel(rhs_hbm, diag_hbm, msg_hbm, rhs, diag, msg, sems):
-    copies = (
-        pltpu.make_async_copy(rhs_hbm, rhs, sems.at[0]),
-        pltpu.make_async_copy(diag_hbm, diag, sems.at[1]),
-    )
-    for copy in copies:
-        copy.start()
-    for copy in copies:
-        copy.wait()
-    mine = pl.ds(pl.multiple_of(here()[0] * HALF, HALF), HALF)
-    inverse = 1.0 / diag[mine, :]
-    msg[:, 0:WIDTH] = (rhs[mine, :] * inverse).astype(BF16)
-    msg[:, WIDTH:] = inverse.astype(BF16)
-    copies = [
-        pltpu.make_async_copy(msg, msg_hbm.at[place], sems.at[2 + place]) for place in range(PLANE)
-    ]
-    for copy in copies:
-        copy.start()
-    for copy in copies:
-        copy.wait()
 
 
 def copy_parts(source, target, sems, first, parts):
@@ -139,12 +118,12 @@
 
 
 def normal_kernel(
-    pattern_hbm, couple_hbm, factor_hbm, normal_hbm,
-    pattern, couple, factor, prod, flip, normal, sems,
+    pattern_hbm, couple_hbm, factor_hbm, upper_hbm,
+    pattern, couple, factor, prod, flip, upper, sems,
 ):
     couples = copy_parts(couple_hbm, couple, sems, 0, 3)
     factors = copy_parts(factor_hbm, factor, sems, 3, 6)
-    outs = copy_parts(normal, normal_hbm, sems, 9, 6)
+    outs = copy_parts(upper, upper_hbm, sems, 9, 6)
     for part in range(3):
         for copy in (couples[part], factors[2 * part], factors[2 * part + 1]):
             copy.start()
@@ -167,21 +146,17 @@
             flip[c, :, (2 - k) * WIDTH : (3 - k) * WIDTH] = block.T
 
     def normal_row(d):
-        for band in range(BANDS):
-            c = d + band - 2
-            if not 0 <= c < ROWS:
-                normal[d, :, band * WIDTH : (band + 1) * WIDTH] = zeros
-                continue
-            if band < 2:
+        for band in range(UPPER):
+            c = d + band
+            at = slice(band * WIDTH, (band + 1) * WIDTH)
+            if c >= ROWS:
+                upper[d, :, at] = zeros
                 continue
             terms = [r for r in (d - 1, d, d + 1) if 0 <= r < ROWS and abs(r - c) <= 1]
             first = terms[0] - d + 1
             left = flip[d, :, first * WIDTH : (first + len(terms)) * WIDTH]
             right = jnp.concatenate([prod[r, c - r + 1] for r in terms], axis=0)
-            block = dot_nn(left, right).astype(BF16)
-            normal[d, :, band * WIDTH : (band + 1) * WIDTH] = block
-            if c != d:
-                normal[c, :, (4 - band) * WIDTH : (5 - band) * WIDTH] = block.T
+            upper[d, :, at] = dot_nn(left, right).astype(BF16)
 
     for copy in couples[:2] + factors[:2]:
         copy.wait()
@@ -216,12 +191,15 @@
 def fetched(part, which, want):
     place = lax.broadcasted_iota(jnp.int32, (1, PLANE * HALF), 1)
     block = place + HALF * ((place * 1366) >> 16) + HALF * which
-    return dot_nn(hot_of(want[:, 0:1] == block), part[...])
+    starts = range(0, PLANE * OWN, OWN)
+    start = jnp.concatenate([part[k : k + HALF, :] for k in starts], axis=0)
+    inverse = jnp.concatenate([part[k + HALF : k + OWN, :] for k in starts], axis=0)
+    return dot_nn(hot_of(want[:, 0:1] == block), jnp.concatenate([start, inverse], axis=1))
 
 
 def load_kernel(
-    near, normal_hbm, rhs_hbm, diag_hbm, idx_hbm, other_hbm,
-    normal, rhs, diag, targets, labels, selector, found, idx, sems,
+    near, upper_hbm, rhs_hbm, diag_hbm, idx_hbm, other_hbm,
+    upper, lower, rhs, diag, targets, labels, selector, found, idx, sems,
 ):
     core, chip, vec = here()
     index = [
@@ -232,8 +210,8 @@
         pltpu.make_async_copy(rhs_hbm, rhs, sems.at[6]),
         pltpu.make_async_copy(diag_hbm, diag, sems.at[7]),
     ]
-    copies += copy_parts(normal_hbm, normal, sems, 0, 6)
-    for copy in index + copies:
+    parts = copy_parts(upper_hbm, upper, sems, 0, 6)
+    for copy in index + copies + parts:
         copy.start()
     row = lax.broadcasted_iota(jnp.int32, (2 * CHIPS, CHIPS * SENT), 0)
     place = lax.broadcasted_iota(jnp.int32, (2 * CHIPS, CHIPS * SENT), 1)
@@ -252,18 +230,28 @@
     column = want[0:ROWS, :]
     for line, values in enumerate((column >> 8, column & 255)):
         labels[line : line + 1, :] = column_sum(jnp.where(mine, values, 0).astype(F32))
+    lower[0, :, :] = jnp.zeros((WIDTH, LOWER * WIDTH), BF16)
+    lower[1, :, 0:WIDTH] = jnp.zeros((WIDTH, WIDTH), BF16)
+    for d in range(ROWS):
+        if d % 4 == 0:
+            parts[d // 4].wait()
+        for band in range(1, UPPER):
+            if d + band < ROWS:
+                at = (LOWER - band) * WIDTH
+                block = upper[d, :, band * WIDTH : (band + 1) * WIDTH]
+                lower[d + band, :, at : at + WIDTH] = block.T
     for copy in copies:
         copy.wait()
 
 
 def first_kernel(
-    far, targets, labels, found, own, cost, normal, msg_out, us_out, inv_out
+    far, targets, labels, found, own, cost, upper, lower, msg_out, us_out, inv_out
 ):
     core, chip, _ = here()
     total = found[...] + fetched(far, 1 - core, targets[0:PAD, :])
     us = total[:, 0:WIDTH]
     us_out[...], inv_out[...] = us, total[:, WIDTH:]
-    lifted = scenario_lift(us, normal)
+    lifted = scenario_lift(us, upper, lower)
     r = own[...]
     ru = r * (r * (1.0 / cost[...]))
     lane = lax.broadcasted_iota(jnp.int32, (1, WIDTH), 1)
@@ -335,7 +323,7 @@
 
 
 def second_kernel(
-    keep, got, us, inv_s, own, cost, normal,
+    keep, got, us, inv_s, own, cost, upper, lower,
     msg_out, us_out, ps_out, scal_out, d_out, q_out, x_out, r_out,
 ):
     total = keep[...] + got[...]
@@ -349,11 +337,11 @@
     d_out[...], q_out[...], x_out[...], r_out[...] = dn, qn, xn, rn
     scal_out[0:1, :] = jnp.broadcast_to(gamma, (1, WIDTH))
     scal_out[1:2, :] = jnp.broadcast_to(alpha, (1, WIDTH))
-    next_message(msg_out, u_s, inv * rn, rn, d, normal)
+    next_message(msg_out, u_s, inv * rn, rn, d, upper, lower)
 
 
 def third_kernel(
-    keep, got, us, ps, inv_s, scal, d, q, x, r, cost, normal,
+    keep, got, us, ps, inv_s, scal, d, q, x, r, cost, upper, lower,
     msg_out, scal_out, d_out, q_out, x_out, r_out,
 ):
     total = keep[...] + got[...]
@@ -366,7 +354,7 @@
     d_out[...], q_out[...], x_out[...], r_out[...] = dn, qn, xn, rn
     scal_out[0:1, :] = jnp.broadcast_to(gamma, (1, WIDTH))
     scal_out[1:2, :] = jnp.broadcast_to(alpha, (1, WIDTH))
-    next_message(msg_out, u_s, inv * rn, rn, c, normal)
+    next_message(msg_out, u_s, inv * rn, rn, c, upper, lower)
 
 
 def last_kernel(keep, got, scal, d, q, x, r, cost, x_out, r_out):
@@ -415,15 +403,17 @@
     hots = ((PAD + OWN + PAD, CHIPS * SENT), BF16)
     aims = ((PAD + OWN + PAD, WIDTH), jnp.int32)
     selectors = ((2 * CHIPS, CHIPS * SENT), BF16)
-    sent = call(
-        opening_kernel, [((PLANE, HALF, 2 * WIDTH), BF16)], hbm_out=True,
-        weights=in_hbm(rhs, diag), scratch=[own, own, ((HALF, 2 * WIDTH), BF16)], sems=2 + PLANE,
-    )[0]
-    near = lax.all_to_all(sent, ("z", "y"), 0, 0, tiled=True).reshape(PLANE * HALF, 2 * WIDTH)
+    first = lax.axis_index("core") * HALF
+    inverse = 1.0 / lax.dynamic_slice_in_dim(diag, first, HALF, 0)
+    start = lax.dynamic_slice_in_dim(rhs, first, HALF, 0) * inverse
+    sent = jnp.concatenate([start.astype(BF16), inverse.astype(BF16)], axis=0)
+    sent = jnp.broadcast_to(sent[None], (PLANE, OWN, WIDTH))
+    near = lax.all_to_all(sent, ("z", "y"), 0, 0, tiled=True)
+    near = near.reshape(PLANE * OWN, WIDTH)
     other_idx = other_core(couple_idx)
     triple, wide = (ROWS, 3, WIDTH, WIDTH), (ROWS, WIDTH, 3 * WIDTH)
-    bands = ((ROWS, WIDTH, BANDS * WIDTH), BF16)
-    normal = call(
+    bands, below = [((ROWS, WIDTH, n * WIDTH), BF16) for n in (UPPER, LOWER)]
+    upper = call(
         normal_kernel, [bands], hbm_out=True, sems=16,
         weights=in_hbm(pattern[0].T, couple[0], factor[0]),
         scratch=[
@@ -431,29 +421,29 @@
             (triple, BF16), (wide, BF16), bands,
         ],
     )[0]
-    near, normal, other_idx = lax.optimization_barrier((near, normal, other_idx))
+    near, upper, other_idx = lax.optimization_barrier((near, upper, other_idx))
     far = other_core(near)
-    normal, r, cost, targets, labels, selector, found = call(
-        load_kernel, [bands, own, own, aims, scal, selectors, ((PAD, 2 * WIDTH), F32)],
-        near, weights=in_hbm(normal, rhs, diag, couple_idx, other_idx),
+    upper, lower, r, cost, targets, labels, selector, found = call(
+        load_kernel, [bands, below, own, own, aims, scal, selectors, ((PAD, 2 * WIDTH), F32)],
+        near, weights=in_hbm(upper, rhs, diag, couple_idx, other_idx),
         scratch=[((2, 1, ROWS), jnp.int32)], sems=10,
     )
     sent, us, inv_s = call(
         first_kernel, [msg, scen, scen],
-        far, targets, labels, found, r, cost, normal,
+        far, targets, labels, found, r, cost, upper, lower,
     )
 
     near = to_all(sent)
     hot, keep, give = call(label_sum, [hots, sums, sums], near, targets, selector)
     sent, us, ps, sc, d, q, x, r = call(
         second_kernel, [msg, scen, scen, scal, own, own, own, own],
-        keep, other_core(give), us, inv_s, r, cost, normal,
+        keep, other_core(give), us, inv_s, r, cost, upper, lower,
     )
     near = to_all(sent)
     keep, give = call(message_sum, [sums, sums], near, hot)
     sent, sc, d, q, x, r = call(
         third_kernel, [msg, scal, own, own, own, own],
-        keep, other_core(give), us, ps, inv_s, sc, d, q, x, r, cost, normal,
+        keep, other_core(give), us, ps, inv_s, sc, d, q, x, r, cost, upper, lower,
     )
     near = to_all(sent)
     keep, give = call(message_sum, [sums, sums], near, hot)

time: 87.1 us -> 86.6 us (level)
  Pallas kernels: 14.7 us -> 12.3 us
    pallas_call x10 -> x9, Pallas kernels: 14.7 us -> 12.3 us  [call(): pl.pallas_call(kernel, out_shape=[(pltpu.HBM if hbm_out else jax.ShapeDty...]
  transfers between devices with their start and end apart: 6 -> 6, of which waited for: 4 -> 4; matrix products, arithmetic and copies ran while one was open for 0% -> 0% of each run, Pallas kernels for 9% -> 8%
where the time goes in v7:
time: 86.6 us; the launch traced here: 86.2 us
  blocking collectives  48 us (55%)
  starting transfers between devices  17.8 us (21%)
  Pallas kernels  12.3 us (14%)
  waiting for transfers between devices  5.75 us (7%)
    all_to_all x3, blocking collectives, to_all(): near = lax.all_to_all(sent, ('x', 'z', 'y'), 0, 0, tiled=True)  48 us
    pallas_call x9, Pallas kernels, call(): pl.pallas_call(kernel, out_shape=[(pltpu.HBM if hbm_out else jax.ShapeDty...  12.3 us
    ppermute x5, starting transfers between devices, other_core(): return lax.ppermute(values, 'core', [(0, 1), (1, 0)])  9.23 us
    all_to_all x1, starting transfers between devices, shards(): near = lax.all_to_all(sent, ('z', 'y'), 0, 0, tiled=True)  8.6 us
    all_to_all x1, waiting for transfers between devices, shards(): near = lax.all_to_all(sent, ('z', 'y'), 0, 0, tiled=True)  3.04 us
    ppermute x5, waiting for transfers between devices, other_core(): return lax.ppermute(values, 'core', [(0, 1), (1, 0)])  2.71 us
  transfers between devices with their start and end apart: 6, of which 4 were waited for; matrix products, arithmetic and copies ran while one was open for 0% of the time, Pallas kernels for 8%

profile of v7, /device:TPU:1, one launch (start us, length us, event | category | flops | bytes accessed | tf_op | source)
XLA Modules:
  0.0 86.2 jit_solution(7553339609697389075)
XLA Ops:
  0.6 0.8 multiply_convert_fusion
  1.4 0.8 broadcast_in_dim.2
  2.2 8.6 %all-to-all-start = ((bf16[16,96,128]{2,1,0:T(8,128)(2,1)}), bf16[16,96,128]{2,1,0:T(8,128)(2,1)S(1)}, u32[]{:S(2)}, u32[]{:S(2)}) async-start(bf16[16,96,128]{2,1,0:T(8,128)(2,1)} %broadcast_in_dim.2), calls=%async_computation | async-start | bytes 786432 | tf_op jit(solution)/shard_map/all_to_all | solution.py:411
  10.8 1.0 %collective-permute-start = (s32[1,24]{1,0:T(1,128)}, s32[1,24]{1,0:T(1,128)S(1)}, u32[]{:S(2)}, u32[]{:S(2)}) collective-permute-start(s32[1,24]{1,0:T(1,128)} %idx_hbm.1), channel_id=1, source_target_pairs={{0,16},{16,0},{1,17},{17,1},{2,18},{18,2},{3,19},{19,3},{4,20},{20... | collective-permute-start | bytes 296 | tf_op jit(solution)/shard_map/ppermute | solution.py:391
  11.9 5.1 %shard_map.77.upper_hbm = bf16[24,128,384]{2,1,0:T(8,128)(2,1)} custom-call(s32[2,24]{1,0:T(2,128)} %bitcast.22, bf16[24,128,128]{2,1,0:T(8,128)(2,1)} %bitcast.21, bf16[24,3,128,128]{3,2,1,0:T(8,128)(2,1)} %bitcast.20), custom_call_target="tpu_custom_call" | custom-call | tf_op jit(solution)/shard_map/pallas_call | solution.py:376
  17.0 3.0 %all-to-all-done = bf16[16,96,128]{2,1,0:T(8,128)(2,1)S(1)} async-done(((bf16[16,96,128]{2,1,0:T(8,128)(2,1)}), bf16[16,96,128]{2,1,0:T(8,128)(2,1)S(1)}, u32[]{:S(2)}, u32[]{:S(2)}) %all-to-all-start) | async-done | bytes 393248 | tf_op jit(solution)/shard_map/all_to_all | solution.py:411
  20.0 1.9 %collective-permute-start.1 = (bf16[1536,128]{1,0:T(8,128)(2,1)S(1)}, bf16[1536,128]{1,0:T(8,128)(2,1)S(1)}, u32[]{:S(2)}, u32[]{:S(2)}) collective-permute-start(bf16[1536,128]{1,0:T(8,128)(2,1)S(1)} %bitcast.15), channel_id=1, source_target_pairs={{0,16},{16,0},{1,17},{17,1},{2,18},{18,2},{3,19},{19,3},{4,20},{20... | collective-permute-start | bytes 1179656 | tf_op jit(solution)/shard_map/ppermute | solution.py:391
  21.9 1.9 %shard_map.78 = (bf16[24,128,384]{2,1,0:T(8,128)(2,1)S(1)}, bf16[24,128,256]{2,1,0:T(8,128)(2,1)S(1)}, f32[96,128]{1,0:T(8,128)S(1)}, f32[96,128]{1,0:T(8,128)S(...) custom-call(bf16[1536,128]{1,0:T(8,128)(2,1)S(1)} %bitcast.16, ...), custom_call_target="tpu_custom_call" | custom-call | tf_op jit(solution)/shard_map/pallas_call | solution.py:376
  23.8 1.3 %shard_map.79 = (bf16[1664,128]{1,0:T(8,128)(2,1)S(1)}, f32[32,128]{1,0:T(8,128)S(1)}, f32[32,128]{1,0:T(8,128)S(1)}) custom-call(bf16[1536,128]{1,0:T(8,128)(2,1)S(1)} %collective-permute-done.1.far, s32[160,128]{1,0:T(8,128)S(1)} %get-tuple-element.40.targets, f32[2,128]{1,0:T(2,128)S(1)} %get-tuple-element.41.labels, ...), custom_call_target="tpu_custom_call" | custom-call | tf_op jit(solution)/shard_map/pallas_call | solution.py:376
  25.1 17.3 %all_to_all.20 = bf16[64,13,2,128]{3,2,1,0:T(2,128)(2,1)S(1)} all-to-all(bf16[64,13,2,128]{3,2,1,0:T(2,128)(2,1)S(1)} %bitcast.19), channel_id=1, replica_groups=mesh['x'=4,'core'=2,'z'=4,'y'=4] {'x','z','y'}, dimensions={0} | all-to-all | bytes 851968 | tf_op jit(solution)/shard_map/all_to_all | solution.py:396
  42.4 0.6 shard_map.80
  43.0 1.8 %collective-permute-start.2 = (f32[128,128]{1,0:T(8,128)S(1)}, f32[128,128]{1,0:T(8,128)S(1)}, u32[]{:S(2)}, u32[]{:S(2)}) collective-permute-start(f32[128,128]{1,0:T(8,128)S(1)} %get-tuple-element.50), channel_id=1, source_target_pairs={{0,16},{16,0},{1,17},{17,1},{2,18},{18,2},{3,19},{19,3},{4,20},{20... | collective-permute-start | bytes 196616 | tf_op jit(solution)/shard_map/ppermute | solution.py:391
  44.8 0.9 %collective-permute-done.2.got = f32[128,128]{1,0:T(8,128)S(1)} collective-permute-done((f32[128,128]{1,0:T(8,128)S(1)}, f32[128,128]{1,0:T(8,128)S(1)}, u32[]{:S(2)}, u32[]{:S(2)}) %collective-permute-start.2) | collective-permute-done | bytes 65568 | tf_op jit(solution)/shard_map/ppermute | solution.py:391
  45.7 1.0 %shard_map.81 = (bf16[1664,128]{1,0:T(8,128)(2,1)S(1)}, f32[32,128]{1,0:T(8,128)S(1)}, f32[32,128]{1,0:T(8,128)S(1)}, f32[2,128]{1,0:T(2,128)S(1)}, f32[96,128]{...) custom-call(f32[128,128]{1,0:T(8,128)S(1)} %get-tuple-element.49.keep, ...), custom_call_target="tpu_custom_call" | custom-call | tf_op jit(solution)/shard_map/pallas_call | solution.py:376
  46.8 15.4 %all_to_all.21 = bf16[64,13,2,128]{3,2,1,0:T(2,128)(2,1)S(1)} all-to-all(bf16[64,13,2,128]{3,2,1,0:T(2,128)(2,1)S(1)} %bitcast.18), channel_id=1, replica_groups=mesh['x'=4,'core'=2,'z'=4,'y'=4] {'x','z','y'}, dimensions={0} | all-to-all | bytes 851968 | tf_op jit(solution)/shard_map/all_to_all | solution.py:396
  62.1 0.3 shard_map.82
  62.4 2.2 %collective-permute-start.3 = (f32[128,128]{1,0:T(8,128)S(1)}, f32[128,128]{1,0:T(8,128)S(1)}, u32[]{:S(2)}, u32[]{:S(2)}) collective-permute-start(f32[128,128]{1,0:T(8,128)S(1)} %get-tuple-element.56), channel_id=1, source_target_pairs={{0,16},{16,0},{1,17},{17,1},{2,18},{18,2},{3,19},{19,3},{4,20},{20... | collective-permute-start | bytes 196616 | tf_op jit(solution)/shard_map/ppermute | solution.py:391
  64.7 0.9 %collective-permute-done.3.got = f32[128,128]{1,0:T(8,128)S(1)} collective-permute-done((f32[128,128]{1,0:T(8,128)S(1)}, f32[128,128]{1,0:T(8,128)S(1)}, u32[]{:S(2)}, u32[]{:S(2)}) %collective-permute-start.3) | collective-permute-done | bytes 65568 | tf_op jit(solution)/shard_map/ppermute | solution.py:391
  65.6 1.0 %shard_map.83 = (bf16[1664,128]{1,0:T(8,128)(2,1)S(1)}, f32[2,128]{1,0:T(2,128)S(1)}, f32[96,128]{1,0:T(8,128)S(1)}, f32[96,128]{1,0:T(8,128)S(1)}, f32[96,128]{1,0:T(8,128)S(1)}, /*index=5*/f32[96,128]{1,0:T(8,128)S(1)}) custom-call(f32[128,128]{1,0:T(8,128)S(1)} %get-tuple-element.55.keep, f32[128,128]{1,0:T(8,128)S(1)} %collective-permute-done.3.got, ...), custom_call_target="tpu_custom_call" | custom-call | tf_op jit(solution)/shard_map/pallas_call | solution.py:376
  66.6 15.3 %all_to_all.22 = bf16[64,13,2,128]{3,2,1,0:T(2,128)(2,1)S(1)} all-to-all(bf16[64,13,2,128]{3,2,1,0:T(2,128)(2,1)S(1)} %bitcast.17), channel_id=1, replica_groups=mesh['x'=4,'core'=2,'z'=4,'y'=4] {'x','z','y'}, dimensions={0} | all-to-all | bytes 851968 | tf_op jit(solution)/shard_map/all_to_all | solution.py:396
  82.0 0.3 shard_map.84
  82.3 2.2 %collective-permute-start.4 = (f32[128,128]{1,0:T(8,128)S(1)}, f32[128,128]{1,0:T(8,128)S(1)}, u32[]{:S(2)}, u32[]{:S(2)}) collective-permute-start(f32[128,128]{1,0:T(8,128)S(1)} %get-tuple-element.66), channel_id=1, source_target_pairs={{0,16},{16,0},{1,17},{17,1},{2,18},{18,2},{3,19},{19,3},{4,20},{20... | collective-permute-start | bytes 196616 | tf_op jit(solution)/shard_map/ppermute | solution.py:391
  84.5 0.9 %collective-permute-done.4.got = f32[128,128]{1,0:T(8,128)S(1)} collective-permute-done((f32[128,128]{1,0:T(8,128)S(1)}, f32[128,128]{1,0:T(8,128)S(1)}, u32[]{:S(2)}, u32[]{:S(2)}) %collective-permute-start.4) | collective-permute-done | bytes 65568 | tf_op jit(solution)/shard_map/ppermute | solution.py:391
  85.4 0.8 shard_map.85
  (5 shorter events, 0.0 us)
Async XLA Ops:
  2.2 17.8 %all-to-all-start = ((bf16[16,96,128]{2,1,0:T(8,128)(2,1)}), bf16[16,96,128]{2,1,0:T(8,128)(2,1)S(1)}, u32[]{:S(2)}, u32[]{:S(2)}) async-start(bf16[16,96,128]{2,1,0:T(8,128)(2,1)} %broadcast_in_dim.2), calls=%async_computation | async-start | bytes 786432 | tf_op jit(solution)/shard_map/all_to_all | solution.py:411
  10.8 6.1 %collective-permute-start = (s32[1,24]{1,0:T(1,128)}, s32[1,24]{1,0:T(1,128)S(1)}, u32[]{:S(2)}, u32[]{:S(2)}) collective-permute-start(s32[1,24]{1,0:T(1,128)} %idx_hbm.1), channel_id=1, source_target_pairs={{0,16},{16,0},{1,17},{17,1},{2,18},{18,2},{3,19},{19,3},{4,20},{20... | collective-permute-start | bytes 296 | tf_op jit(solution)/shard_map/ppermute | solution.py:391
  16.9 4.9 %copy-start = (s32[1,24]{1,0:T(1,128)}, s32[1,24]{1,0:T(1,128)S(1)}, u32[]{:S(2)}) copy-start(s32[1,24]{1,0:T(1,128)S(1)} %collective-permute-done.other_hbm) | copy-start | bytes 292
  20.0 3.8 %collective-permute-start.1 = (bf16[1536,128]{1,0:T(8,128)(2,1)S(1)}, bf16[1536,128]{1,0:T(8,128)(2,1)S(1)}, u32[]{:S(2)}, u32[]{:S(2)}) collective-permute-start(bf16[1536,128]{1,0:T(8,128)(2,1)S(1)} %bitcast.15), channel_id=1, source_target_pairs={{0,16},{16,0},{1,17},{17,1},{2,18},{18,2},{3,19},{19,3},{4,20},{20... | collective-permute-start | bytes 1179656 | tf_op jit(solution)/shard_map/ppermute | solution.py:391
  43.0 2.7 %collective-permute-start.2 = (f32[128,128]{1,0:T(8,128)S(1)}, f32[128,128]{1,0:T(8,128)S(1)}, u32[]{:S(2)}, u32[]{:S(2)}) collective-permute-start(f32[128,128]{1,0:T(8,128)S(1)} %get-tuple-element.50), channel_id=1, source_target_pairs={{0,16},{16,0},{1,17},{17,1},{2,18},{18,2},{3,19},{19,3},{4,20},{20... | collective-permute-start | bytes 196616 | tf_op jit(solution)/shard_map/ppermute | solution.py:391
  62.4 3.1 %collective-permute-start.3 = (f32[128,128]{1,0:T(8,128)S(1)}, f32[128,128]{1,0:T(8,128)S(1)}, u32[]{:S(2)}, u32[]{:S(2)}) collective-permute-start(f32[128,128]{1,0:T(8,128)S(1)} %get-tuple-element.56), channel_id=1, source_target_pairs={{0,16},{16,0},{1,17},{17,1},{2,18},{18,2},{3,19},{19,3},{4,20},{20... | collective-permute-start | bytes 196616 | tf_op jit(solution)/shard_map/ppermute | solution.py:391
  82.3 3.1 %collective-permute-start.4 = (f32[128,128]{1,0:T(8,128)S(1)}, f32[128,128]{1,0:T(8,128)S(1)}, u32[]{:S(2)}, u32[]{:S(2)}) collective-permute-start(f32[128,128]{1,0:T(8,128)S(1)} %get-tuple-element.66), channel_id=1, source_target_pairs={{0,16},{16,0},{1,17},{17,1},{2,18},{18,2},{3,19},{19,3},{4,20},{20... | collective-permute-start | bytes 196616 | tf_op jit(solution)/shard_map/ppermute | solution.py:391

commit v8 on v7

--- a/solution.py
+++ b/solution.py
@@ -118,16 +118,14 @@
 
 
 def normal_kernel(
-    pattern_hbm, couple_hbm, factor_hbm, upper_hbm,
-    pattern, couple, factor, prod, flip, upper, sems,
+    pattern_hbm, couple_hbm, factor_hbm, upper, pattern, couple, factor, prod, flip, sems
 ):
     couples = copy_parts(couple_hbm, couple, sems, 0, 3)
     factors = copy_parts(factor_hbm, factor, sems, 3, 6)
-    outs = copy_parts(upper, upper_hbm, sems, 9, 6)
     for part in range(3):
         for copy in (couples[part], factors[2 * part], factors[2 * part + 1]):
             copy.start()
-    copy = pltpu.make_async_copy(pattern_hbm, pattern, sems.at[15])
+    copy = pltpu.make_async_copy(pattern_hbm, pattern, sems.at[9])
     copy.start()
     copy.wait()
     side = [as_column(pattern[k : k + 1, :]) for k in range(2)]
@@ -168,24 +166,16 @@
         product_row(r)
     for d in range(7):
         normal_row(d)
-    outs[0].start()
     for copy in factors[4:]:
         copy.wait()
     for r in range(16, 24):
         product_row(r)
     for d in range(7, 12):
         normal_row(d)
-    outs[1].start()
-    outs[2].start()
     for d in range(12, 18):
         normal_row(d)
-    outs[3].start()
     for d in range(18, 24):
         normal_row(d)
-    outs[4].start()
-    outs[5].start()
-    for copy in outs:
-        copy.wait()
 
 
 def fetched(part, which, want):
@@ -198,20 +188,19 @@
 
 
 def load_kernel(
-    near, upper_hbm, rhs_hbm, diag_hbm, idx_hbm, other_hbm,
-    upper, lower, rhs, diag, targets, labels, selector, found, idx, sems,
+    near, upper, rhs_hbm, diag_hbm, idx_hbm, other_hbm,
+    lower, rhs, diag, targets, labels, selector, found, idx, sems,
 ):
     core, chip, vec = here()
     index = [
-        pltpu.make_async_copy(hbm, idx.at[k], sems.at[8 + k])
+        pltpu.make_async_copy(hbm, idx.at[k], sems.at[2 + k])
         for k, hbm in enumerate((idx_hbm, other_hbm))
     ]
     copies = [
-        pltpu.make_async_copy(rhs_hbm, rhs, sems.at[6]),
-        pltpu.make_async_copy(diag_hbm, diag, sems.at[7]),
+        pltpu.make_async_copy(rhs_hbm, rhs, sems.at[0]),
+        pltpu.make_async_copy(diag_hbm, diag, sems.at[1]),
     ]
-    parts = copy_parts(upper_hbm, upper, sems, 0, 6)
-    for copy in index + copies + parts:
+    for copy in index + copies:
         copy.start()
     row = lax.broadcasted_iota(jnp.int32, (2 * CHIPS, CHIPS * SENT), 0)
     place = lax.broadcasted_iota(jnp.int32, (2 * CHIPS, CHIPS * SENT), 1)
@@ -233,8 +222,6 @@
     lower[0, :, :] = jnp.zeros((WIDTH, LOWER * WIDTH), BF16)
     lower[1, :, 0:WIDTH] = jnp.zeros((WIDTH, WIDTH), BF16)
     for d in range(ROWS):
-        if d % 4 == 0:
-            parts[d // 4].wait()
         for band in range(1, UPPER):
             if d + band < ROWS:
                 at = (LOWER - band) * WIDTH
@@ -414,19 +401,19 @@
     triple, wide = (ROWS, 3, WIDTH, WIDTH), (ROWS, WIDTH, 3 * WIDTH)
     bands, below = [((ROWS, WIDTH, n * WIDTH), BF16) for n in (UPPER, LOWER)]
     upper = call(
-        normal_kernel, [bands], hbm_out=True, sems=16,
+        normal_kernel, [bands], sems=10,
         weights=in_hbm(pattern[0].T, couple[0], factor[0]),
         scratch=[
             ((2, ROWS), jnp.int32), ((ROWS, WIDTH, WIDTH), BF16), (triple, BF16),
-            (triple, BF16), (wide, BF16), bands,
+            (triple, BF16), (wide, BF16),
         ],
     )[0]
     near, upper, other_idx = lax.optimization_barrier((near, upper, other_idx))
     far = other_core(near)
-    upper, lower, r, cost, targets, labels, selector, found = call(
-        load_kernel, [bands, below, own, own, aims, scal, selectors, ((PAD, 2 * WIDTH), F32)],
-        near, weights=in_hbm(upper, rhs, diag, couple_idx, other_idx),
-        scratch=[((2, 1, ROWS), jnp.int32)], sems=10,
+    lower, r, cost, targets, labels, selector, found = call(
+        load_kernel, [below, own, own, aims, scal, selectors, ((PAD, 2 * WIDTH), F32)],
+        near, upper, weights=in_hbm(rhs, diag, couple_idx, other_idx),
+        scratch=[((2, 1, ROWS), jnp.int32)], sems=4,
     )
     sent, us, inv_s = call(
         first_kernel, [msg, scen, scen],

time: 86.6 us -> 86.1 us (level)
  Pallas kernels: 12.3 us -> 10.8 us
  waiting for transfers between devices: 5.75 us -> 6.76 us
    pallas_call x9, Pallas kernels: 12.3 us -> 10.8 us  [call(): pl.pallas_call(kernel, out_shape=[(pltpu.HBM if hbm_out else jax.ShapeDty...]
    all_to_all x1, waiting for transfers between devices: 3.04 us -> 3.98 us  [shards(): near = lax.all_to_all(sent, ('z', 'y'), 0, 0, tiled=True)]
  transfers between devices with their start and end apart: 6 -> 6, of which waited for: 4 -> 5; matrix products, arithmetic and copies ran while one was open for 0% -> 0% of each run, Pallas kernels for 8% -> 6%
where the time goes in v8:
time: 86.1 us; the launch traced here: 85.6 us
  blocking collectives  47.6 us (55%)
  starting transfers between devices  18.2 us (21%)
  Pallas kernels  10.8 us (13%)
  waiting for transfers between devices  6.76 us (8%)
    all_to_all x3, blocking collectives, to_all(): near = lax.all_to_all(sent, ('x', 'z', 'y'), 0, 0, tiled=True)  47.6 us
    pallas_call x9, Pallas kernels, call(): pl.pallas_call(kernel, out_shape=[(pltpu.HBM if hbm_out else jax.ShapeDty...  10.8 us
    ppermute x5, starting transfers between devices, other_core(): return lax.ppermute(values, 'core', [(0, 1), (1, 0)])  9.65 us
    all_to_all x1, starting transfers between devices, shards(): near = lax.all_to_all(sent, ('z', 'y'), 0, 0, tiled=True)  8.6 us
    all_to_all x1, waiting for transfers between devices, shards(): near = lax.all_to_all(sent, ('z', 'y'), 0, 0, tiled=True)  3.98 us
    ppermute x5, waiting for transfers between devices, other_core(): return lax.ppermute(values, 'core', [(0, 1), (1, 0)])  2.78 us
  transfers between devices with their start and end apart: 6, of which 5 were waited for; matrix products, arithmetic and copies ran while one was open for 0% of the time, Pallas kernels for 6%

profile of v8, /device:TPU:1, one launch (start us, length us, event | category | flops | bytes accessed | tf_op | source)
XLA Modules:
  0.0 85.6 jit_solution(9614299261684399649)
XLA Ops:
  0.6 0.8 multiply_convert_fusion
  1.4 0.8 broadcast_in_dim.2
  2.2 8.6 %all-to-all-start = ((bf16[16,96,128]{2,1,0:T(8,128)(2,1)}), bf16[16,96,128]{2,1,0:T(8,128)(2,1)S(1)}, u32[]{:S(2)}, u32[]{:S(2)}) async-start(bf16[16,96,128]{2,1,0:T(8,128)(2,1)} %broadcast_in_dim.2), calls=%async_computation | async-start | bytes 786432 | tf_op jit(solution)/shard_map/all_to_all | solution.py:398
  10.8 1.0 %collective-permute-start = (s32[1,24]{1,0:T(1,128)}, s32[1,24]{1,0:T(1,128)S(1)}, u32[]{:S(2)}, u32[]{:S(2)}) collective-permute-start(s32[1,24]{1,0:T(1,128)} %idx_hbm.1), channel_id=1, source_target_pairs={{0,16},{16,0},{1,17},{17,1},{2,18},{18,2},{3,19},{19,3},{4,20},{20... | collective-permute-start | bytes 296 | tf_op jit(solution)/shard_map/ppermute | solution.py:378
  11.9 4.1 %shard_map.77.upper = bf16[24,128,384]{2,1,0:T(8,128)(2,1)S(1)} custom-call(s32[2,24]{1,0:T(2,128)} %bitcast.22, bf16[24,128,128]{2,1,0:T(8,128)(2,1)} %bitcast.21, bf16[24,3,128,128]{3,2,1,0:T(8,128)(2,1)} %bitcast.20), custom_call_target="tpu_custom_call" | custom-call | tf_op jit(solution)/shard_map/pallas_call | solution.py:363
  16.0 4.0 %all-to-all-done = bf16[16,96,128]{2,1,0:T(8,128)(2,1)S(1)} async-done(((bf16[16,96,128]{2,1,0:T(8,128)(2,1)}), bf16[16,96,128]{2,1,0:T(8,128)(2,1)S(1)}, u32[]{:S(2)}, u32[]{:S(2)}) %all-to-all-start) | async-done | bytes 393248 | tf_op jit(solution)/shard_map/all_to_all | solution.py:398
  20.0 1.9 %collective-permute-start.1 = (bf16[1536,128]{1,0:T(8,128)(2,1)S(1)}, bf16[1536,128]{1,0:T(8,128)(2,1)S(1)}, u32[]{:S(2)}, u32[]{:S(2)}) collective-permute-start(bf16[1536,128]{1,0:T(8,128)(2,1)S(1)} %bitcast.15), channel_id=1, source_target_pairs={{0,16},{16,0},{1,17},{17,1},{2,18},{18,2},{3,19},{19,3},{4,20},{20... | collective-permute-start | bytes 1179656 | tf_op jit(solution)/shard_map/ppermute | solution.py:378
  21.9 1.3 %shard_map.78 = (bf16[24,128,256]{2,1,0:T(8,128)(2,1)S(1)}, f32[96,128]{1,0:T(8,128)S(1)}, f32[96,128]{1,0:T(8,128)S(1)}, s32[160,128]{1,0:T(8,128)S(1)}, f32[2,...) custom-call(bf16[1536,128]{1,0:T(8,128)(2,1)S(1)} %bitcast.16, ...), custom_call_target="tpu_custom_call" | custom-call | tf_op jit(solution)/shard_map/pallas_call | solution.py:363
  23.2 1.3 %shard_map.79 = (bf16[1664,128]{1,0:T(8,128)(2,1)S(1)}, f32[32,128]{1,0:T(8,128)S(1)}, f32[32,128]{1,0:T(8,128)S(1)}) custom-call(bf16[1536,128]{1,0:T(8,128)(2,1)S(1)} %collective-permute-done.1.far, s32[160,128]{1,0:T(8,128)S(1)} %get-tuple-element.39.targets, f32[2,128]{1,0:T(2,128)S(1)} %get-tuple-element.40.labels, ...), custom_call_target="tpu_custom_call" | custom-call | tf_op jit(solution)/shard_map/pallas_call | solution.py:363
  24.5 16.9 %all_to_all.20 = bf16[64,13,2,128]{3,2,1,0:T(2,128)(2,1)S(1)} all-to-all(bf16[64,13,2,128]{3,2,1,0:T(2,128)(2,1)S(1)} %bitcast.19), channel_id=1, replica_groups=mesh['x'=4,'core'=2,'z'=4,'y'=4] {'x','z','y'}, dimensions={0} | all-to-all | bytes 851968 | tf_op jit(solution)/shard_map/all_to_all | solution.py:383
  41.4 0.6 shard_map.80
  42.0 2.3 %collective-permute-start.2 = (f32[128,128]{1,0:T(8,128)S(1)}, f32[128,128]{1,0:T(8,128)S(1)}, u32[]{:S(2)}, u32[]{:S(2)}) collective-permute-start(f32[128,128]{1,0:T(8,128)S(1)} %get-tuple-element.48), channel_id=1, source_target_pairs={{0,16},{16,0},{1,17},{17,1},{2,18},{18,2},{3,19},{19,3},{4,20},{20... | collective-permute-start | bytes 196616 | tf_op jit(solution)/shard_map/ppermute | solution.py:378
  44.3 0.9 %collective-permute-done.2.got = f32[128,128]{1,0:T(8,128)S(1)} collective-permute-done((f32[128,128]{1,0:T(8,128)S(1)}, f32[128,128]{1,0:T(8,128)S(1)}, u32[]{:S(2)}, u32[]{:S(2)}) %collective-permute-start.2) | collective-permute-done | bytes 65568 | tf_op jit(solution)/shard_map/ppermute | solution.py:378
  45.2 1.1 %shard_map.81 = (bf16[1664,128]{1,0:T(8,128)(2,1)S(1)}, f32[32,128]{1,0:T(8,128)S(1)}, f32[32,128]{1,0:T(8,128)S(1)}, f32[2,128]{1,0:T(2,128)S(1)}, f32[96,128]{...) custom-call(f32[128,128]{1,0:T(8,128)S(1)} %get-tuple-element.47.keep, ...), custom_call_target="tpu_custom_call" | custom-call | tf_op jit(solution)/shard_map/pallas_call | solution.py:363
  46.2 15.3 %all_to_all.21 = bf16[64,13,2,128]{3,2,1,0:T(2,128)(2,1)S(1)} all-to-all(bf16[64,13,2,128]{3,2,1,0:T(2,128)(2,1)S(1)} %bitcast.18), channel_id=1, replica_groups=mesh['x'=4,'core'=2,'z'=4,'y'=4] {'x','z','y'}, dimensions={0} | all-to-all | bytes 851968 | tf_op jit(solution)/shard_map/all_to_all | solution.py:383
  61.6 0.3 shard_map.82
  61.9 2.2 %collective-permute-start.3 = (f32[128,128]{1,0:T(8,128)S(1)}, f32[128,128]{1,0:T(8,128)S(1)}, u32[]{:S(2)}, u32[]{:S(2)}) collective-permute-start(f32[128,128]{1,0:T(8,128)S(1)} %get-tuple-element.54), channel_id=1, source_target_pairs={{0,16},{16,0},{1,17},{17,1},{2,18},{18,2},{3,19},{19,3},{4,20},{20... | collective-permute-start | bytes 196616 | tf_op jit(solution)/shard_map/ppermute | solution.py:378
  64.1 0.9 %collective-permute-done.3.got = f32[128,128]{1,0:T(8,128)S(1)} collective-permute-done((f32[128,128]{1,0:T(8,128)S(1)}, f32[128,128]{1,0:T(8,128)S(1)}, u32[]{:S(2)}, u32[]{:S(2)}) %collective-permute-start.3) | collective-permute-done | bytes 65568 | tf_op jit(solution)/shard_map/ppermute | solution.py:378
  65.0 1.1 %shard_map.83 = (bf16[1664,128]{1,0:T(8,128)(2,1)S(1)}, f32[2,128]{1,0:T(2,128)S(1)}, f32[96,128]{1,0:T(8,128)S(1)}, f32[96,128]{1,0:T(8,128)S(1)}, f32[96,128]{1,0:T(8,128)S(1)}, /*index=5*/f32[96,128]{1,0:T(8,128)S(1)}) custom-call(f32[128,128]{1,0:T(8,128)S(1)} %get-tuple-element.53.keep, f32[128,128]{1,0:T(8,128)S(1)} %collective-permute-done.3.got, ...), custom_call_target="tpu_custom_call" | custom-call | tf_op jit(solution)/shard_map/pallas_call | solution.py:363
  66.1 15.3 %all_to_all.22 = bf16[64,13,2,128]{3,2,1,0:T(2,128)(2,1)S(1)} all-to-all(bf16[64,13,2,128]{3,2,1,0:T(2,128)(2,1)S(1)} %bitcast.17), channel_id=1, replica_groups=mesh['x'=4,'core'=2,'z'=4,'y'=4] {'x','z','y'}, dimensions={0} | all-to-all | bytes 851968 | tf_op jit(solution)/shard_map/all_to_all | solution.py:383
  81.4 0.3 shard_map.84
  81.7 2.2 %collective-permute-start.4 = (f32[128,128]{1,0:T(8,128)S(1)}, f32[128,128]{1,0:T(8,128)S(1)}, u32[]{:S(2)}, u32[]{:S(2)}) collective-permute-start(f32[128,128]{1,0:T(8,128)S(1)} %get-tuple-element.64), channel_id=1, source_target_pairs={{0,16},{16,0},{1,17},{17,1},{2,18},{18,2},{3,19},{19,3},{4,20},{20... | collective-permute-start | bytes 196616 | tf_op jit(solution)/shard_map/ppermute | solution.py:378
  84.0 0.9 %collective-permute-done.4.got = f32[128,128]{1,0:T(8,128)S(1)} collective-permute-done((f32[128,128]{1,0:T(8,128)S(1)}, f32[128,128]{1,0:T(8,128)S(1)}, u32[]{:S(2)}, u32[]{:S(2)}) %collective-permute-start.4) | collective-permute-done | bytes 65568 | tf_op jit(solution)/shard_map/ppermute | solution.py:378
  84.9 0.8 shard_map.85
  (5 shorter events, 0.1 us)
Async XLA Ops:
  2.2 17.8 %all-to-all-start = ((bf16[16,96,128]{2,1,0:T(8,128)(2,1)}), bf16[16,96,128]{2,1,0:T(8,128)(2,1)S(1)}, u32[]{:S(2)}, u32[]{:S(2)}) async-start(bf16[16,96,128]{2,1,0:T(8,128)(2,1)} %broadcast_in_dim.2), calls=%async_computation | async-start | bytes 786432 | tf_op jit(solution)/shard_map/all_to_all | solution.py:398
  10.8 5.2 %collective-permute-start = (s32[1,24]{1,0:T(1,128)}, s32[1,24]{1,0:T(1,128)S(1)}, u32[]{:S(2)}, u32[]{:S(2)}) collective-permute-start(s32[1,24]{1,0:T(1,128)} %idx_hbm.1), channel_id=1, source_target_pairs={{0,16},{16,0},{1,17},{17,1},{2,18},{18,2},{3,19},{19,3},{4,20},{20... | collective-permute-start | bytes 296 | tf_op jit(solution)/shard_map/ppermute | solution.py:378
  16.0 5.9 %copy-start = (s32[1,24]{1,0:T(1,128)}, s32[1,24]{1,0:T(1,128)S(1)}, u32[]{:S(2)}) copy-start(s32[1,24]{1,0:T(1,128)S(1)} %collective-permute-done.other_hbm) | copy-start | bytes 292
  20.0 3.2 %collective-permute-start.1 = (bf16[1536,128]{1,0:T(8,128)(2,1)S(1)}, bf16[1536,128]{1,0:T(8,128)(2,1)S(1)}, u32[]{:S(2)}, u32[]{:S(2)}) collective-permute-start(bf16[1536,128]{1,0:T(8,128)(2,1)S(1)} %bitcast.15), channel_id=1, source_target_pairs={{0,16},{16,0},{1,17},{17,1},{2,18},{18,2},{3,19},{19,3},{4,20},{20... | collective-permute-start | bytes 1179656 | tf_op jit(solution)/shard_map/ppermute | solution.py:378
  42.0 3.2 %collective-permute-start.2 = (f32[128,128]{1,0:T(8,128)S(1)}, f32[128,128]{1,0:T(8,128)S(1)}, u32[]{:S(2)}, u32[]{:S(2)}) collective-permute-start(f32[128,128]{1,0:T(8,128)S(1)} %get-tuple-element.48), channel_id=1, source_target_pairs={{0,16},{16,0},{1,17},{17,1},{2,18},{18,2},{3,19},{19,3},{4,20},{20... | collective-permute-start | bytes 196616 | tf_op jit(solution)/shard_map/ppermute | solution.py:378
  61.9 3.1 %collective-permute-start.3 = (f32[128,128]{1,0:T(8,128)S(1)}, f32[128,128]{1,0:T(8,128)S(1)}, u32[]{:S(2)}, u32[]{:S(2)}) collective-permute-start(f32[128,128]{1,0:T(8,128)S(1)} %get-tuple-element.54), channel_id=1, source_target_pairs={{0,16},{16,0},{1,17},{17,1},{2,18},{18,2},{3,19},{19,3},{4,20},{20... | collective-permute-start | bytes 196616 | tf_op jit(solution)/shard_map/ppermute | solution.py:378
  81.7 3.1 %collective-permute-start.4 = (f32[128,128]{1,0:T(8,128)S(1)}, f32[128,128]{1,0:T(8,128)S(1)}, u32[]{:S(2)}, u32[]{:S(2)}) collective-permute-start(f32[128,128]{1,0:T(8,128)S(1)} %get-tuple-element.64), channel_id=1, source_target_pairs={{0,16},{16,0},{1,17},{17,1},{2,18},{18,2},{3,19},{19,3},{4,20},{20... | collective-permute-start | bytes 196616 | tf_op jit(solution)/shard_map/ppermute | solution.py:378

commit v9 on v8

--- a/solution.py
+++ b/solution.py
@@ -187,38 +187,50 @@
     return dot_nn(hot_of(want[:, 0:1] == block), jnp.concatenate([start, inverse], axis=1))
 
 
-def load_kernel(
-    near, upper, rhs_hbm, diag_hbm, idx_hbm, other_hbm,
-    lower, rhs, diag, targets, labels, selector, found, idx, sems,
+def index_kernel(
+    other_idx, rhs_hbm, diag_hbm, idx_hbm, rhs, diag, targets, labels, selector, idx, sems
 ):
-    core, chip, vec = here()
-    index = [
-        pltpu.make_async_copy(hbm, idx.at[k], sems.at[2 + k])
-        for k, hbm in enumerate((idx_hbm, other_hbm))
-    ]
+    _, chip, vec = here()
+    index = pltpu.make_async_copy(idx_hbm, idx, sems.at[2])
+    index.start()
     copies = [
         pltpu.make_async_copy(rhs_hbm, rhs, sems.at[0]),
         pltpu.make_async_copy(diag_hbm, diag, sems.at[1]),
     ]
-    for copy in index + copies:
+    for copy in copies:
         copy.start()
     row = lax.broadcasted_iota(jnp.int32, (2 * CHIPS, CHIPS * SENT), 0)
     place = lax.broadcasted_iota(jnp.int32, (2 * CHIPS, CHIPS * SENT), 1)
     line = SENT * (row & (CHIPS - 1)) + ROWS + jnp.where(row < CHIPS, 0, 1)
     selector[...] = hot_of(place == line)
-    for copy in index:
-        copy.wait()
-    want = scenario_targets(idx[0])
+    targets[PAD + OWN :, :] = scenario_targets(other_idx[...])
+    index.wait()
+    want = scenario_targets(idx[...])
     targets[0:PAD, :] = want
     targets[PAD : PAD + OWN, :] = lax.broadcasted_iota(jnp.int32, (OWN, WIDTH), 0) + vec * OWN
-    targets[PAD + OWN :, :] = scenario_targets(idx[1])
-    found[...] = fetched(near, core, want)
     lane = lax.broadcasted_iota(jnp.int32, (ROWS, WIDTH), 1)
     rows = lax.broadcasted_iota(jnp.int32, (ROWS, WIDTH), 0)
     mine = rows == (lane - SENT * chip) & (WIDTH - 1)
     column = want[0:ROWS, :]
     for line, values in enumerate((column >> 8, column & 255)):
         labels[line : line + 1, :] = column_sum(jnp.where(mine, values, 0).astype(F32))
+    for copy in copies:
+        copy.wait()
+
+
+def fetch_kernel(near, targets, keep, give):
+    want = jnp.concatenate([targets[0:PAD, 0:1], targets[PAD + OWN :, 0:1]], axis=0)
+    place = lax.broadcasted_iota(jnp.int32, (1, PLANE * HALF), 1)
+    block = place + HALF * ((place * 1366) >> 16) + HALF * lax.axis_index("core")
+    starts = range(0, PLANE * OWN, OWN)
+    start = jnp.concatenate([near[k : k + HALF, :] for k in starts], axis=0)
+    inverse = jnp.concatenate([near[k + HALF : k + OWN, :] for k in starts], axis=0)
+    found = dot_nn(hot_of(want == block), jnp.concatenate([start, inverse], axis=1))
+    keep[...] = found[0:PAD, :]
+    give[...] = found[PAD:, :].astype(BF16)
+
+
+def lower_kernel(upper, lower):
     lower[0, :, :] = jnp.zeros((WIDTH, LOWER * WIDTH), BF16)
     lower[1, :, 0:WIDTH] = jnp.zeros((WIDTH, WIDTH), BF16)
     for d in range(ROWS):
@@ -227,15 +239,11 @@
                 at = (LOWER - band) * WIDTH
                 block = upper[d, :, band * WIDTH : (band + 1) * WIDTH]
                 lower[d + band, :, at : at + WIDTH] = block.T
-    for copy in copies:
-        copy.wait()
-
-
-def first_kernel(
-    far, targets, labels, found, own, cost, upper, lower, msg_out, us_out, inv_out
-):
-    core, chip, _ = here()
-    total = found[...] + fetched(far, 1 - core, targets[0:PAD, :])
+
+
+def first_kernel(keep, got, labels, own, cost, upper, lower, msg_out, us_out, inv_out):
+    chip = here()[1]
+    total = keep[...] + got[...].astype(F32)
     us = total[:, 0:WIDTH]
     us_out[...], inv_out[...] = us, total[:, WIDTH:]
     lifted = scenario_lift(us, upper, lower)
@@ -408,16 +416,19 @@
             (triple, BF16), (wide, BF16),
         ],
     )[0]
-    near, upper, other_idx = lax.optimization_barrier((near, upper, other_idx))
-    far = other_core(near)
-    lower, r, cost, targets, labels, selector, found = call(
-        load_kernel, [below, own, own, aims, scal, selectors, ((PAD, 2 * WIDTH), F32)],
-        near, upper, weights=in_hbm(rhs, diag, couple_idx, other_idx),
-        scratch=[((2, 1, ROWS), jnp.int32)], sems=4,
-    )
+    r, cost, targets, labels, selector = call(
+        index_kernel, [own, own, aims, scal, selectors],
+        other_idx, weights=in_hbm(rhs, diag, couple_idx),
+        scratch=[((1, ROWS), jnp.int32)], sems=3,
+    )
+    near, upper, r, cost, targets, labels, selector = lax.optimization_barrier(
+        (near, upper, r, cost, targets, labels, selector)
+    )
+    pair = (PAD, 2 * WIDTH)
+    keep, give = call(fetch_kernel, [(pair, F32), (pair, BF16)], near, targets)
+    lower = call(lower_kernel, [below], upper)[0]
     sent, us, inv_s = call(
-        first_kernel, [msg, scen, scen],
-        far, targets, labels, found, r, cost, upper, lower,
+        first_kernel, [msg, scen, scen], keep, other_core(give), labels, r, cost, upper, lower
     )
 
     near = to_all(sent)

time: 86.1 us -> 85.6 us (level)
    all_to_all x1, waiting for transfers between devices: 3.98 us -> 3.11 us  [shards(): near = lax.all_to_all(sent, ('z', 'y'), 0, 0, tiled=True)]
    pallas_call x9 -> x11, Pallas kernels: 10.8 us -> 10.7 us  [call(): pl.pallas_call(kernel, out_shape=[(pltpu.HBM if hbm_out else jax.ShapeDty...]
where the time goes in v9:
time: 85.6 us; the launch traced here: 85.2 us
  blocking collectives  47.6 us (56%)
  starting transfers between devices  18.3 us (21%)
  Pallas kernels  10.7 us (12%)
  waiting for transfers between devices  6.22 us (7%)
    all_to_all x3, blocking collectives, to_all(): near = lax.all_to_all(sent, ('x', 'z', 'y'), 0, 0, tiled=True)  47.6 us
    pallas_call x11, Pallas kernels, call(): pl.pallas_call(kernel, out_shape=[(pltpu.HBM if hbm_out else jax.ShapeDty...  10.7 us
    ppermute x5, starting transfers between devices, other_core(): return lax.ppermute(values, 'core', [(0, 1), (1, 0)])  9.7 us
    all_to_all x1, starting transfers between devices, shards(): near = lax.all_to_all(sent, ('z', 'y'), 0, 0, tiled=True)  8.6 us
    all_to_all x1, waiting for transfers between devices, shards(): near = lax.all_to_all(sent, ('z', 'y'), 0, 0, tiled=True)  3.11 us
    ppermute x5, waiting for transfers between devices, other_core(): return lax.ppermute(values, 'core', [(0, 1), (1, 0)])  3.11 us
  transfers between devices with their start and end apart: 6, of which 5 were waited for; matrix products, arithmetic and copies ran while one was open for 0% of the time, Pallas kernels for 6%

profile of v9, /device:TPU:1, one launch (start us, length us, event | category | flops | bytes accessed | tf_op | source)
XLA Modules:
  0.0 85.2 jit_solution(7805263110649120614)
XLA Ops:
  0.6 0.8 multiply_convert_fusion
  1.4 0.8 broadcast_in_dim.2
  2.2 8.6 %all-to-all-start = ((bf16[16,96,128]{2,1,0:T(8,128)(2,1)}), bf16[16,96,128]{2,1,0:T(8,128)(2,1)S(1)}, u32[]{:S(2)}, u32[]{:S(2)}) async-start(bf16[16,96,128]{2,1,0:T(8,128)(2,1)} %broadcast_in_dim.2), calls=%async_computation | async-start | bytes 786432 | tf_op jit(solution)/shard_map/all_to_all | solution.py:406
  10.8 1.0 %collective-permute-start = (s32[1,24]{1,0:T(1,128)}, s32[1,24]{1,0:T(1,128)S(1)}, u32[]{:S(2)}, u32[]{:S(2)}) collective-permute-start(s32[1,24]{1,0:T(1,128)} %idx_hbm.1), channel_id=1, source_target_pairs={{0,16},{16,0},{1,17},{17,1},{2,18},{18,2},{3,19},{19,3},{4,20},{20... | collective-permute-start | bytes 296 | tf_op jit(solution)/shard_map/ppermute | solution.py:386
  11.9 4.1 %shard_map.77.upper = bf16[24,128,384]{2,1,0:T(8,128)(2,1)S(1)} custom-call(s32[2,24]{1,0:T(2,128)} %bitcast.21, bf16[24,128,128]{2,1,0:T(8,128)(2,1)} %bitcast.20, bf16[24,3,128,128]{3,2,1,0:T(8,128)(2,1)} %bitcast.19), custom_call_target="tpu_custom_call" | custom-call | tf_op jit(solution)/shard_map/pallas_call | solution.py:371
  16.0 0.9 %shard_map.78 = (f32[96,128]{1,0:T(8,128)S(1)}, f32[96,128]{1,0:T(8,128)S(1)}, s32[160,128]{1,0:T(8,128)S(1)}, f32[2,128]{1,0:T(2,128)S(1)}, bf16[128,1664]{1,0:T(8,128)(2,1)S(1)}) custom-call(s32[1,24]{1,0:T(1,128)S(1)} %collective-permute-done.other_idx, f32[96,128]{1,0:T(8,128)} %rhs_hbm.1, f32[96,128]{1,0:T(8,128)} %diag_hbm.1, s32[1,24]{1,0:T(1,128)} %idx_hbm.1), custom_call_target="tpu_custom_call" | custom-call | tf_op jit(solution)/shard_map/pallas_call | solution.py:371
  16.9 3.1 %all-to-all-done = bf16[16,96,128]{2,1,0:T(8,128)(2,1)S(1)} async-done(((bf16[16,96,128]{2,1,0:T(8,128)(2,1)}), bf16[16,96,128]{2,1,0:T(8,128)(2,1)S(1)}, u32[]{:S(2)}, u32[]{:S(2)}) %all-to-all-start) | async-done | bytes 393248 | tf_op jit(solution)/shard_map/all_to_all | solution.py:406
  20.2 1.9 %collective-permute-start.1 = (bf16[32,256]{1,0:T(8,128)(2,1)S(1)}, bf16[32,256]{1,0:T(8,128)(2,1)S(1)}, u32[]{:S(2)}, u32[]{:S(2)}) collective-permute-start(bf16[32,256]{1,0:T(8,128)(2,1)S(1)} %get-tuple-element.48), channel_id=1, source_target_pairs={{0,16},{16,0},{1,17},{17,1},{2,18},{18,2},{3,19},{19,3},{4,20},{20... | collective-permute-start | bytes 49160 | tf_op jit(solution)/shard_map/ppermute | solution.py:386
  22.2 0.4 shard_map.80.lower
  22.6 0.4 collective-permute-done.1.got
  23.0 1.0 %shard_map.81 = (bf16[1664,128]{1,0:T(8,128)(2,1)S(1)}, f32[32,128]{1,0:T(8,128)S(1)}, f32[32,128]{1,0:T(8,128)S(1)}) custom-call(f32[32,256]{1,0:T(8,128)S(1)} %get-tuple-element.47.keep, bf16[32,256]{1,0:T(8,128)(2,1)S(1)} %collective-permute-done.1.got, f32[2,128]{1,0:T(2,128)S(1)} %get-tuple-element.49.labels, f32[96,128]{1,0:T(8,128)S(1)} %get-tuple-element.50.own, ...), custom_call_target="tpu_custom_call" | custom-call | tf_op jit(solution)/shard_map/pallas_call | solution.py:371
  24.0 16.9 %all_to_all.20 = bf16[64,13,2,128]{3,2,1,0:T(2,128)(2,1)S(1)} all-to-all(bf16[64,13,2,128]{3,2,1,0:T(2,128)(2,1)S(1)} %bitcast.18), channel_id=1, replica_groups=mesh['x'=4,'core'=2,'z'=4,'y'=4] {'x','z','y'}, dimensions={0} | all-to-all | bytes 851968 | tf_op jit(solution)/shard_map/all_to_all | solution.py:391
  40.9 0.6 shard_map.82
  41.5 2.2 %collective-permute-start.2 = (f32[128,128]{1,0:T(8,128)S(1)}, f32[128,128]{1,0:T(8,128)S(1)}, u32[]{:S(2)}, u32[]{:S(2)}) collective-permute-start(f32[128,128]{1,0:T(8,128)S(1)} %get-tuple-element.56), channel_id=1, source_target_pairs={{0,16},{16,0},{1,17},{17,1},{2,18},{18,2},{3,19},{19,3},{4,20},{20... | collective-permute-start | bytes 196616 | tf_op jit(solution)/shard_map/ppermute | solution.py:386
  43.8 0.9 %collective-permute-done.2.got = f32[128,128]{1,0:T(8,128)S(1)} collective-permute-done((f32[128,128]{1,0:T(8,128)S(1)}, f32[128,128]{1,0:T(8,128)S(1)}, u32[]{:S(2)}, u32[]{:S(2)}) %collective-permute-start.2) | collective-permute-done | bytes 65568 | tf_op jit(solution)/shard_map/ppermute | solution.py:386
  44.7 1.1 %shard_map.83 = (bf16[1664,128]{1,0:T(8,128)(2,1)S(1)}, f32[32,128]{1,0:T(8,128)S(1)}, f32[32,128]{1,0:T(8,128)S(1)}, f32[2,128]{1,0:T(2,128)S(1)}, f32[96,128]{...) custom-call(f32[128,128]{1,0:T(8,128)S(1)} %get-tuple-element.55.keep, ...), custom_call_target="tpu_custom_call" | custom-call | tf_op jit(solution)/shard_map/pallas_call | solution.py:371
  45.7 15.3 %all_to_all.21 = bf16[64,13,2,128]{3,2,1,0:T(2,128)(2,1)S(1)} all-to-all(bf16[64,13,2,128]{3,2,1,0:T(2,128)(2,1)S(1)} %bitcast.17), channel_id=1, replica_groups=mesh['x'=4,'core'=2,'z'=4,'y'=4] {'x','z','y'}, dimensions={0} | all-to-all | bytes 851968 | tf_op jit(solution)/shard_map/all_to_all | solution.py:391
  61.4 2.2 %collective-permute-start.3 = (f32[128,128]{1,0:T(8,128)S(1)}, f32[128,128]{1,0:T(8,128)S(1)}, u32[]{:S(2)}, u32[]{:S(2)}) collective-permute-start(f32[128,128]{1,0:T(8,128)S(1)} %get-tuple-element.62), channel_id=1, source_target_pairs={{0,16},{16,0},{1,17},{17,1},{2,18},{18,2},{3,19},{19,3},{4,20},{20... | collective-permute-start | bytes 196616 | tf_op jit(solution)/shard_map/ppermute | solution.py:386
  63.6 0.9 %collective-permute-done.3.got = f32[128,128]{1,0:T(8,128)S(1)} collective-permute-done((f32[128,128]{1,0:T(8,128)S(1)}, f32[128,128]{1,0:T(8,128)S(1)}, u32[]{:S(2)}, u32[]{:S(2)}) %collective-permute-start.3) | collective-permute-done | bytes 65568 | tf_op jit(solution)/shard_map/ppermute | solution.py:386
  64.5 1.1 %shard_map.85 = (bf16[1664,128]{1,0:T(8,128)(2,1)S(1)}, f32[2,128]{1,0:T(2,128)S(1)}, f32[96,128]{1,0:T(8,128)S(1)}, f32[96,128]{1,0:T(8,128)S(1)}, f32[96,128]{1,0:T(8,128)S(1)}, /*index=5*/f32[96,128]{1,0:T(8,128)S(1)}) custom-call(f32[128,128]{1,0:T(8,128)S(1)} %get-tuple-element.61.keep, f32[128,128]{1,0:T(8,128)S(1)} %collective-permute-done.3.got, ...), custom_call_target="tpu_custom_call" | custom-call | tf_op jit(solution)/shard_map/pallas_call | solution.py:371
  65.6 15.3 %all_to_all.22 = bf16[64,13,2,128]{3,2,1,0:T(2,128)(2,1)S(1)} all-to-all(bf16[64,13,2,128]{3,2,1,0:T(2,128)(2,1)S(1)} %bitcast.16), channel_id=1, replica_groups=mesh['x'=4,'core'=2,'z'=4,'y'=4] {'x','z','y'}, dimensions={0} | all-to-all | bytes 851968 | tf_op jit(solution)/shard_map/all_to_all | solution.py:391
  81.2 2.2 %collective-permute-start.4 = (f32[128,128]{1,0:T(8,128)S(1)}, f32[128,128]{1,0:T(8,128)S(1)}, u32[]{:S(2)}, u32[]{:S(2)}) collective-permute-start(f32[128,128]{1,0:T(8,128)S(1)} %get-tuple-element.72), channel_id=1, source_target_pairs={{0,16},{16,0},{1,17},{17,1},{2,18},{18,2},{3,19},{19,3},{4,20},{20... | collective-permute-start | bytes 196616 | tf_op jit(solution)/shard_map/ppermute | solution.py:386
  83.5 0.9 %collective-permute-done.4.got = f32[128,128]{1,0:T(8,128)S(1)} collective-permute-done((f32[128,128]{1,0:T(8,128)S(1)}, f32[128,128]{1,0:T(8,128)S(1)}, u32[]{:S(2)}, u32[]{:S(2)}) %collective-permute-start.4) | collective-permute-done | bytes 65568 | tf_op jit(solution)/shard_map/ppermute | solution.py:386
  84.4 0.8 shard_map.87
  (5 shorter events, 0.8 us)
Async XLA Ops:
  2.2 17.8 %all-to-all-start = ((bf16[16,96,128]{2,1,0:T(8,128)(2,1)}), bf16[16,96,128]{2,1,0:T(8,128)(2,1)S(1)}, u32[]{:S(2)}, u32[]{:S(2)}) async-start(bf16[16,96,128]{2,1,0:T(8,128)(2,1)} %broadcast_in_dim.2), calls=%async_computation | async-start | bytes 786432 | tf_op jit(solution)/shard_map/all_to_all | solution.py:406
  10.8 5.2 %collective-permute-start = (s32[1,24]{1,0:T(1,128)}, s32[1,24]{1,0:T(1,128)S(1)}, u32[]{:S(2)}, u32[]{:S(2)}) collective-permute-start(s32[1,24]{1,0:T(1,128)} %idx_hbm.1), channel_id=1, source_target_pairs={{0,16},{16,0},{1,17},{17,1},{2,18},{18,2},{3,19},{19,3},{4,20},{20... | collective-permute-start | bytes 296 | tf_op jit(solution)/shard_map/ppermute | solution.py:386
  20.2 2.8 %collective-permute-start.1 = (bf16[32,256]{1,0:T(8,128)(2,1)S(1)}, bf16[32,256]{1,0:T(8,128)(2,1)S(1)}, u32[]{:S(2)}, u32[]{:S(2)}) collective-permute-start(bf16[32,256]{1,0:T(8,128)(2,1)S(1)} %get-tuple-element.48), channel_id=1, source_target_pairs={{0,16},{16,0},{1,17},{17,1},{2,18},{18,2},{3,19},{19,3},{4,20},{20... | collective-permute-start | bytes 49160 | tf_op jit(solution)/shard_map/ppermute | solution.py:386
  41.5 3.1 %collective-permute-start.2 = (f32[128,128]{1,0:T(8,128)S(1)}, f32[128,128]{1,0:T(8,128)S(1)}, u32[]{:S(2)}, u32[]{:S(2)}) collective-permute-start(f32[128,128]{1,0:T(8,128)S(1)} %get-tuple-element.56), channel_id=1, source_target_pairs={{0,16},{16,0},{1,17},{17,1},{2,18},{18,2},{3,19},{19,3},{4,20},{20... | collective-permute-start | bytes 196616 | tf_op jit(solution)/shard_map/ppermute | solution.py:386
  61.4 3.1 %collective-permute-start.3 = (f32[128,128]{1,0:T(8,128)S(1)}, f32[128,128]{1,0:T(8,128)S(1)}, u32[]{:S(2)}, u32[]{:S(2)}) collective-permute-start(f32[128,128]{1,0:T(8,128)S(1)} %get-tuple-element.62), channel_id=1, source_target_pairs={{0,16},{16,0},{1,17},{17,1},{2,18},{18,2},{3,19},{19,3},{4,20},{20... | collective-permute-start | bytes 196616 | tf_op jit(solution)/shard_map/ppermute | solution.py:386
  81.2 3.1 %collective-permute-start.4 = (f32[128,128]{1,0:T(8,128)S(1)}, f32[128,128]{1,0:T(8,128)S(1)}, u32[]{:S(2)}, u32[]{:S(2)}) collective-permute-start(f32[128,128]{1,0:T(8,128)S(1)} %get-tuple-element.72), channel_id=1, source_target_pairs={{0,16},{16,0},{1,17},{17,1},{2,18},{18,2},{3,19},{19,3},{4,20},{20... | collective-permute-start | bytes 196616 | tf_op jit(solution)/shard_map/ppermute | solution.py:386

commit v10 on v9

--- a/solution.py
+++ b/solution.py
@@ -44,15 +44,24 @@
 
 
 def scenario_lift(y, upper, lower):
-    spread = jnp.zeros((PAD, (LOWER + UPPER) * WIDTH), F32)
+    rows = lax.broadcasted_iota(jnp.int32, (PAD, WIDTH), 0)
+    exact = y.astype(BF16).astype(F32)
+    columns = jnp.concatenate([exact] * (WIDTH // PAD), axis=0).T
+    spread = jnp.zeros((PAD, UPPER * WIDTH), F32)
+    below = [jnp.zeros((PAD, WIDTH), F32) for band in range(LOWER)]
     for r in range(0, ROWS, 2):
         pair = jnp.concatenate([only_row(y, r), only_row(y, r + 1)], axis=1)
-        blocks = [m[r : r + 2].reshape(2 * WIDTH, m.shape[2]) for m in (lower, upper)]
-        spread += dot_nn(pair, jnp.concatenate(blocks, axis=1))
-    lifted = spread[:, LOWER * WIDTH : (LOWER + 1) * WIDTH]
-    for band in (0, 1, 3, 4):
-        part = spread[:, band * WIDTH : (band + 1) * WIDTH]
-        lifted += pltpu.roll(part, (band - LOWER) % PAD, 0)
+        spread += dot_nn(pair, upper[r : r + 2].reshape(2 * WIDTH, UPPER * WIDTH))
+        for d in (r, r + 1):
+            for band in range(LOWER):
+                c = d + band - LOWER
+                if c >= 0:
+                    block = lower[d, :, band * WIDTH : (band + 1) * WIDTH].astype(F32)
+                    line = column_sum(block * columns[:, d : d + 1])
+                    below[band] = jnp.where(rows == c, line, below[band])
+    lifted = spread[:, 0:WIDTH] + below[0] + below[1]
+    for band in range(1, UPPER):
+        lifted += pltpu.roll(spread[:, band * WIDTH : (band + 1) * WIDTH], band, 0)
     return lifted
 
 

time: 85.6 us -> 85.4 us (level)
  no operation moved by 1% of the time
where the time goes in v10:
time: 85.4 us; the launch traced here: 85 us
  blocking collectives  47.6 us (56%)
  starting transfers between devices  18.3 us (21%)
  Pallas kernels  10.6 us (12%)
  waiting for transfers between devices  6.22 us (7%)
    all_to_all x3, blocking collectives, to_all(): near = lax.all_to_all(sent, ('x', 'z', 'y'), 0, 0, tiled=True)  47.6 us
    pallas_call x11, Pallas kernels, call(): pl.pallas_call(kernel, out_shape=[(pltpu.HBM if hbm_out else jax.ShapeDty...  10.6 us
    ppermute x5, starting transfers between devices, other_core(): return lax.ppermute(values, 'core', [(0, 1), (1, 0)])  9.7 us
    all_to_all x1, starting transfers between devices, shards(): near = lax.all_to_all(sent, ('z', 'y'), 0, 0, tiled=True)  8.6 us
    all_to_all x1, waiting for transfers between devices, shards(): near = lax.all_to_all(sent, ('z', 'y'), 0, 0, tiled=True)  3.11 us
    ppermute x5, waiting for transfers between devices, other_core(): return lax.ppermute(values, 'core', [(0, 1), (1, 0)])  3.11 us
  transfers between devices with their start and end apart: 6, of which 5 were waited for; matrix products, arithmetic and copies ran while one was open for 0% of the time, Pallas kernels for 6%

profile of v10, /device:TPU:1, one launch (start us, length us, event | category | flops | bytes accessed | tf_op | source)
XLA Modules:
  0.0 85.0 jit_solution(13085596303323031675)
XLA Ops:
  0.6 0.8 multiply_convert_fusion
  1.4 0.8 broadcast_in_dim.2
  2.2 8.6 %all-to-all-start = ((bf16[16,96,128]{2,1,0:T(8,128)(2,1)}), bf16[16,96,128]{2,1,0:T(8,128)(2,1)S(1)}, u32[]{:S(2)}, u32[]{:S(2)}) async-start(bf16[16,96,128]{2,1,0:T(8,128)(2,1)} %broadcast_in_dim.2), calls=%async_computation | async-start | bytes 786432 | tf_op jit(solution)/shard_map/all_to_all | solution.py:415
  10.8 1.0 %collective-permute-start = (s32[1,24]{1,0:T(1,128)}, s32[1,24]{1,0:T(1,128)S(1)}, u32[]{:S(2)}, u32[]{:S(2)}) collective-permute-start(s32[1,24]{1,0:T(1,128)} %idx_hbm.1), channel_id=1, source_target_pairs={{0,16},{16,0},{1,17},{17,1},{2,18},{18,2},{3,19},{19,3},{4,20},{20... | collective-permute-start | bytes 296 | tf_op jit(solution)/shard_map/ppermute | solution.py:395
  11.9 4.1 %shard_map.77.upper = bf16[24,128,384]{2,1,0:T(8,128)(2,1)S(1)} custom-call(s32[2,24]{1,0:T(2,128)} %bitcast.21, bf16[24,128,128]{2,1,0:T(8,128)(2,1)} %bitcast.20, bf16[24,3,128,128]{3,2,1,0:T(8,128)(2,1)} %bitcast.19), custom_call_target="tpu_custom_call" | custom-call | tf_op jit(solution)/shard_map/pallas_call | solution.py:380
  16.0 0.9 %shard_map.78 = (f32[96,128]{1,0:T(8,128)S(1)}, f32[96,128]{1,0:T(8,128)S(1)}, s32[160,128]{1,0:T(8,128)S(1)}, f32[2,128]{1,0:T(2,128)S(1)}, bf16[128,1664]{1,0:T(8,128)(2,1)S(1)}) custom-call(s32[1,24]{1,0:T(1,128)S(1)} %collective-permute-done.other_idx, f32[96,128]{1,0:T(8,128)} %rhs_hbm.1, f32[96,128]{1,0:T(8,128)} %diag_hbm.1, s32[1,24]{1,0:T(1,128)} %idx_hbm.1), custom_call_target="tpu_custom_call" | custom-call | tf_op jit(solution)/shard_map/pallas_call | solution.py:380
  16.9 3.1 %all-to-all-done = bf16[16,96,128]{2,1,0:T(8,128)(2,1)S(1)} async-done(((bf16[16,96,128]{2,1,0:T(8,128)(2,1)}), bf16[16,96,128]{2,1,0:T(8,128)(2,1)S(1)}, u32[]{:S(2)}, u32[]{:S(2)}) %all-to-all-start) | async-done | bytes 393248 | tf_op jit(solution)/shard_map/all_to_all | solution.py:415
  20.2 1.9 %collective-permute-start.1 = (bf16[32,256]{1,0:T(8,128)(2,1)S(1)}, bf16[32,256]{1,0:T(8,128)(2,1)S(1)}, u32[]{:S(2)}, u32[]{:S(2)}) collective-permute-start(bf16[32,256]{1,0:T(8,128)(2,1)S(1)} %get-tuple-element.48), channel_id=1, source_target_pairs={{0,16},{16,0},{1,17},{17,1},{2,18},{18,2},{3,19},{19,3},{4,20},{20... | collective-permute-start | bytes 49160 | tf_op jit(solution)/shard_map/ppermute | solution.py:395
  22.2 0.4 shard_map.80.lower
  22.6 0.4 collective-permute-done.1.got
  23.0 0.9 %shard_map.81 = (bf16[1664,128]{1,0:T(8,128)(2,1)S(1)}, f32[32,128]{1,0:T(8,128)S(1)}, f32[32,128]{1,0:T(8,128)S(1)}) custom-call(f32[32,256]{1,0:T(8,128)S(1)} %get-tuple-element.47.keep, bf16[32,256]{1,0:T(8,128)(2,1)S(1)} %collective-permute-done.1.got, f32[2,128]{1,0:T(2,128)S(1)} %get-tuple-element.49.labels, f32[96,128]{1,0:T(8,128)S(1)} %get-tuple-element.50.own, ...), custom_call_target="tpu_custom_call" | custom-call | tf_op jit(solution)/shard_map/pallas_call | solution.py:380
  23.9 16.9 %all_to_all.20 = bf16[64,13,2,128]{3,2,1,0:T(2,128)(2,1)S(1)} all-to-all(bf16[64,13,2,128]{3,2,1,0:T(2,128)(2,1)S(1)} %bitcast.18), channel_id=1, replica_groups=mesh['x'=4,'core'=2,'z'=4,'y'=4] {'x','z','y'}, dimensions={0} | all-to-all | bytes 851968 | tf_op jit(solution)/shard_map/all_to_all | solution.py:400
  40.8 0.6 shard_map.82
  41.4 2.2 %collective-permute-start.2 = (f32[128,128]{1,0:T(8,128)S(1)}, f32[128,128]{1,0:T(8,128)S(1)}, u32[]{:S(2)}, u32[]{:S(2)}) collective-permute-start(f32[128,128]{1,0:T(8,128)S(1)} %get-tuple-element.56), channel_id=1, source_target_pairs={{0,16},{16,0},{1,17},{17,1},{2,18},{18,2},{3,19},{19,3},{4,20},{20... | collective-permute-start | bytes 196616 | tf_op jit(solution)/shard_map/ppermute | solution.py:395
  43.7 0.9 %collective-permute-done.2.got = f32[128,128]{1,0:T(8,128)S(1)} collective-permute-done((f32[128,128]{1,0:T(8,128)S(1)}, f32[128,128]{1,0:T(8,128)S(1)}, u32[]{:S(2)}, u32[]{:S(2)}) %collective-permute-start.2) | collective-permute-done | bytes 65568 | tf_op jit(solution)/shard_map/ppermute | solution.py:395
  44.6 1.0 %shard_map.83 = (bf16[1664,128]{1,0:T(8,128)(2,1)S(1)}, f32[32,128]{1,0:T(8,128)S(1)}, f32[32,128]{1,0:T(8,128)S(1)}, f32[2,128]{1,0:T(2,128)S(1)}, f32[96,128]{...) custom-call(f32[128,128]{1,0:T(8,128)S(1)} %get-tuple-element.55.keep, ...), custom_call_target="tpu_custom_call" | custom-call | tf_op jit(solution)/shard_map/pallas_call | solution.py:380
  45.6 15.3 %all_to_all.21 = bf16[64,13,2,128]{3,2,1,0:T(2,128)(2,1)S(1)} all-to-all(bf16[64,13,2,128]{3,2,1,0:T(2,128)(2,1)S(1)} %bitcast.17), channel_id=1, replica_groups=mesh['x'=4,'core'=2,'z'=4,'y'=4] {'x','z','y'}, dimensions={0} | all-to-all | bytes 851968 | tf_op jit(solution)/shard_map/all_to_all | solution.py:400
  61.3 2.2 %collective-permute-start.3 = (f32[128,128]{1,0:T(8,128)S(1)}, f32[128,128]{1,0:T(8,128)S(1)}, u32[]{:S(2)}, u32[]{:S(2)}) collective-permute-start(f32[128,128]{1,0:T(8,128)S(1)} %get-tuple-element.62), channel_id=1, source_target_pairs={{0,16},{16,0},{1,17},{17,1},{2,18},{18,2},{3,19},{19,3},{4,20},{20... | collective-permute-start | bytes 196616 | tf_op jit(solution)/shard_map/ppermute | solution.py:395
  63.5 0.9 %collective-permute-done.3.got = f32[128,128]{1,0:T(8,128)S(1)} collective-permute-done((f32[128,128]{1,0:T(8,128)S(1)}, f32[128,128]{1,0:T(8,128)S(1)}, u32[]{:S(2)}, u32[]{:S(2)}) %collective-permute-start.3) | collective-permute-done | bytes 65568 | tf_op jit(solution)/shard_map/ppermute | solution.py:395
  64.4 1.0 %shard_map.85 = (bf16[1664,128]{1,0:T(8,128)(2,1)S(1)}, f32[2,128]{1,0:T(2,128)S(1)}, f32[96,128]{1,0:T(8,128)S(1)}, f32[96,128]{1,0:T(8,128)S(1)}, f32[96,128]{1,0:T(8,128)S(1)}, /*index=5*/f32[96,128]{1,0:T(8,128)S(1)}) custom-call(f32[128,128]{1,0:T(8,128)S(1)} %get-tuple-element.61.keep, f32[128,128]{1,0:T(8,128)S(1)} %collective-permute-done.3.got, ...), custom_call_target="tpu_custom_call" | custom-call | tf_op jit(solution)/shard_map/pallas_call | solution.py:380
  65.4 15.4 %all_to_all.22 = bf16[64,13,2,128]{3,2,1,0:T(2,128)(2,1)S(1)} all-to-all(bf16[64,13,2,128]{3,2,1,0:T(2,128)(2,1)S(1)} %bitcast.16), channel_id=1, replica_groups=mesh['x'=4,'core'=2,'z'=4,'y'=4] {'x','z','y'}, dimensions={0} | all-to-all | bytes 851968 | tf_op jit(solution)/shard_map/all_to_all | solution.py:400
  81.1 2.2 %collective-permute-start.4 = (f32[128,128]{1,0:T(8,128)S(1)}, f32[128,128]{1,0:T(8,128)S(1)}, u32[]{:S(2)}, u32[]{:S(2)}) collective-permute-start(f32[128,128]{1,0:T(8,128)S(1)} %get-tuple-element.72), channel_id=1, source_target_pairs={{0,16},{16,0},{1,17},{17,1},{2,18},{18,2},{3,19},{19,3},{4,20},{20... | collective-permute-start | bytes 196616 | tf_op jit(solution)/shard_map/ppermute | solution.py:395
  83.3 0.9 %collective-permute-done.4.got = f32[128,128]{1,0:T(8,128)S(1)} collective-permute-done((f32[128,128]{1,0:T(8,128)S(1)}, f32[128,128]{1,0:T(8,128)S(1)}, u32[]{:S(2)}, u32[]{:S(2)}) %collective-permute-start.4) | collective-permute-done | bytes 65568 | tf_op jit(solution)/shard_map/ppermute | solution.py:395
  84.2 0.8 shard_map.87
  (5 shorter events, 0.8 us)
Async XLA Ops:
  2.2 17.8 %all-to-all-start = ((bf16[16,96,128]{2,1,0:T(8,128)(2,1)}), bf16[16,96,128]{2,1,0:T(8,128)(2,1)S(1)}, u32[]{:S(2)}, u32[]{:S(2)}) async-start(bf16[16,96,128]{2,1,0:T(8,128)(2,1)} %broadcast_in_dim.2), calls=%async_computation | async-start | bytes 786432 | tf_op jit(solution)/shard_map/all_to_all | solution.py:415
  10.8 5.2 %collective-permute-start = (s32[1,24]{1,0:T(1,128)}, s32[1,24]{1,0:T(1,128)S(1)}, u32[]{:S(2)}, u32[]{:S(2)}) collective-permute-start(s32[1,24]{1,0:T(1,128)} %idx_hbm.1), channel_id=1, source_target_pairs={{0,16},{16,0},{1,17},{17,1},{2,18},{18,2},{3,19},{19,3},{4,20},{20... | collective-permute-start | bytes 296 | tf_op jit(solution)/shard_map/ppermute | solution.py:395
  20.2 2.8 %collective-permute-start.1 = (bf16[32,256]{1,0:T(8,128)(2,1)S(1)}, bf16[32,256]{1,0:T(8,128)(2,1)S(1)}, u32[]{:S(2)}, u32[]{:S(2)}) collective-permute-start(bf16[32,256]{1,0:T(8,128)(2,1)S(1)} %get-tuple-element.48), channel_id=1, source_target_pairs={{0,16},{16,0},{1,17},{17,1},{2,18},{18,2},{3,19},{19,3},{4,20},{20... | collective-permute-start | bytes 49160 | tf_op jit(solution)/shard_map/ppermute | solution.py:395
  41.4 3.1 %collective-permute-start.2 = (f32[128,128]{1,0:T(8,128)S(1)}, f32[128,128]{1,0:T(8,128)S(1)}, u32[]{:S(2)}, u32[]{:S(2)}) collective-permute-start(f32[128,128]{1,0:T(8,128)S(1)} %get-tuple-element.56), channel_id=1, source_target_pairs={{0,16},{16,0},{1,17},{17,1},{2,18},{18,2},{3,19},{19,3},{4,20},{20... | collective-permute-start | bytes 196616 | tf_op jit(solution)/shard_map/ppermute | solution.py:395
  61.3 3.1 %collective-permute-start.3 = (f32[128,128]{1,0:T(8,128)S(1)}, f32[128,128]{1,0:T(8,128)S(1)}, u32[]{:S(2)}, u32[]{:S(2)}) collective-permute-start(f32[128,128]{1,0:T(8,128)S(1)} %get-tuple-element.62), channel_id=1, source_target_pairs={{0,16},{16,0},{1,17},{17,1},{2,18},{18,2},{3,19},{19,3},{4,20},{20... | collective-permute-start | bytes 196616 | tf_op jit(solution)/shard_map/ppermute | solution.py:395
  81.1 3.1 %collective-permute-start.4 = (f32[128,128]{1,0:T(8,128)S(1)}, f32[128,128]{1,0:T(8,128)S(1)}, u32[]{:S(2)}, u32[]{:S(2)}) collective-permute-start(f32[128,128]{1,0:T(8,128)S(1)} %get-tuple-element.72), channel_id=1, source_target_pairs={{0,16},{16,0},{1,17},{17,1},{2,18},{18,2},{3,19},{19,3},{4,20},{20... | collective-permute-start | bytes 196616 | tf_op jit(solution)/shard_map/ppermute | solution.py:395

commit v11 on v10

--- a/solution.py
+++ b/solution.py
@@ -66,14 +66,15 @@
 
 
 def write_message(msg_out, lifted, lines):
-    rows = lax.broadcasted_iota(jnp.int32, (PAD, WIDTH), 0)
-    out = lifted
-    for place, line in enumerate(lines):
-        out = jnp.where(rows == ROWS + place, jnp.broadcast_to(line, out.shape), out)
     row = lax.broadcasted_iota(jnp.int32, (COPIES * SENT, PAD), 0)
     column = lax.broadcasted_iota(jnp.int32, (COPIES * SENT, PAD), 1)
     again = hot_of(row - SENT * ((row * 2521) >> 16) == column)
-    block = dot_nn(again, out.astype(BF16)).astype(BF16)
+    block = dot_nn(again, lifted.astype(BF16))
+    row = lax.broadcasted_iota(jnp.int32, (COPIES * SENT, WIDTH), 0)
+    row = row - SENT * ((row * 2521) >> 16)
+    for place, line in enumerate(lines):
+        block = jnp.where(row == ROWS + place, line, block)
+    block = block.astype(BF16)
     for start in range(0, CHIPS * SENT, COPIES * SENT):
         msg_out[start : start + COPIES * SENT, :] = block
 
@@ -303,16 +304,16 @@
     give_and_keep(dot_nn(hot[...], part[...]), keep, give)
 
 
-def advance(total, us, inv_s, ps, u, cost, q, d, x, r, gamma_old, alpha_old):
+def advance(total, us, inv_s, ps, u, cost, q, d, x, r, per_gamma, per_alpha):
     gamma = jnp.sum(total[ROWS : ROWS + 1, :], axis=1, keepdims=True)
     delta = jnp.sum(total[ROWS + 1 : ROWS + 2, :], axis=1, keepdims=True)
-    if gamma_old is None:
+    if per_gamma is None:
         alpha = gamma / delta
     else:
-        beta = gamma / gamma_old
-        alpha = gamma / (delta - beta * gamma / alpha_old)
+        beta = gamma * per_gamma
+        alpha = gamma / (delta - beta * (gamma * per_alpha))
     s = cost * u + total[PAD:, :]
-    if gamma_old is None:
+    if per_gamma is None:
         d, q = u, s
     else:
         d, q = u + beta * d, s + beta * q
@@ -339,8 +340,8 @@
     )
     us_out[...], ps_out[...] = u_s, p_s
     d_out[...], q_out[...], x_out[...], r_out[...] = dn, qn, xn, rn
-    scal_out[0:1, :] = jnp.broadcast_to(gamma, (1, WIDTH))
-    scal_out[1:2, :] = jnp.broadcast_to(alpha, (1, WIDTH))
+    scal_out[0:1, :] = jnp.broadcast_to(1.0 / gamma, (1, WIDTH))
+    scal_out[1:2, :] = jnp.broadcast_to(1.0 / alpha, (1, WIDTH))
     next_message(msg_out, u_s, inv * rn, rn, d, upper, lower)
 
 
@@ -356,8 +357,8 @@
         scal[0:1, 0:1], scal[1:2, 0:1],
     )
     d_out[...], q_out[...], x_out[...], r_out[...] = dn, qn, xn, rn
-    scal_out[0:1, :] = jnp.broadcast_to(gamma, (1, WIDTH))
-    scal_out[1:2, :] = jnp.broadcast_to(alpha, (1, WIDTH))
+    scal_out[0:1, :] = jnp.broadcast_to(1.0 / gamma, (1, WIDTH))
+    scal_out[1:2, :] = jnp.broadcast_to(1.0 / alpha, (1, WIDTH))
     next_message(msg_out, u_s, inv * rn, rn, c, upper, lower)
 
 

time: 85.4 us -> 85.2 us (level)
  no operation moved by 1% of the time
where the time goes in v11:
time: 85.2 us; the launch traced here: 84.7 us
  blocking collectives  47.6 us (56%)
  starting transfers between devices  18.3 us (21%)
  Pallas kernels  10.3 us (12%)
  waiting for transfers between devices  6.22 us (7%)
    all_to_all x3, blocking collectives, to_all(): near = lax.all_to_all(sent, ('x', 'z', 'y'), 0, 0, tiled=True)  47.6 us
    pallas_call x11, Pallas kernels, call(): pl.pallas_call(kernel, out_shape=[(pltpu.HBM if hbm_out else jax.ShapeDty...  10.3 us
    ppermute x5, starting transfers between devices, other_core(): return lax.ppermute(values, 'core', [(0, 1), (1, 0)])  9.69 us
    all_to_all x1, starting transfers between devices, shards(): near = lax.all_to_all(sent, ('z', 'y'), 0, 0, tiled=True)  8.6 us
    all_to_all x1, waiting for transfers between devices, shards(): near = lax.all_to_all(sent, ('z', 'y'), 0, 0, tiled=True)  3.11 us
    ppermute x5, waiting for transfers between devices, other_core(): return lax.ppermute(values, 'core', [(0, 1), (1, 0)])  3.11 us
  transfers between devices with their start and end apart: 6, of which 5 were waited for; matrix products, arithmetic and copies ran while one was open for 0% of the time, Pallas kernels for 6%

profile of v11, /device:TPU:1, one launch (start us, length us, event | category | flops | bytes accessed | tf_op | source)
XLA Modules:
  0.0 84.7 jit_solution(1667962432826372669)
XLA Ops:
  0.6 0.8 multiply_convert_fusion
  1.4 0.8 broadcast_in_dim.2
  2.2 8.6 %all-to-all-start = ((bf16[16,96,128]{2,1,0:T(8,128)(2,1)}), bf16[16,96,128]{2,1,0:T(8,128)(2,1)S(1)}, u32[]{:S(2)}, u32[]{:S(2)}) async-start(bf16[16,96,128]{2,1,0:T(8,128)(2,1)} %broadcast_in_dim.2), calls=%async_computation | async-start | bytes 786432 | tf_op jit(solution)/shard_map/all_to_all | solution.py:416
  10.8 1.0 %collective-permute-start = (s32[1,24]{1,0:T(1,128)}, s32[1,24]{1,0:T(1,128)S(1)}, u32[]{:S(2)}, u32[]{:S(2)}) collective-permute-start(s32[1,24]{1,0:T(1,128)} %idx_hbm.1), channel_id=1, source_target_pairs={{0,16},{16,0},{1,17},{17,1},{2,18},{18,2},{3,19},{19,3},{4,20},{20... | collective-permute-start | bytes 296 | tf_op jit(solution)/shard_map/ppermute | solution.py:396
  11.9 4.1 %shard_map.77.upper = bf16[24,128,384]{2,1,0:T(8,128)(2,1)S(1)} custom-call(s32[2,24]{1,0:T(2,128)} %bitcast.21, bf16[24,128,128]{2,1,0:T(8,128)(2,1)} %bitcast.20, bf16[24,3,128,128]{3,2,1,0:T(8,128)(2,1)} %bitcast.19), custom_call_target="tpu_custom_call" | custom-call | tf_op jit(solution)/shard_map/pallas_call | solution.py:381
  16.0 0.9 %shard_map.78 = (f32[96,128]{1,0:T(8,128)S(1)}, f32[96,128]{1,0:T(8,128)S(1)}, s32[160,128]{1,0:T(8,128)S(1)}, f32[2,128]{1,0:T(2,128)S(1)}, bf16[128,1664]{1,0:T(8,128)(2,1)S(1)}) custom-call(s32[1,24]{1,0:T(1,128)S(1)} %collective-permute-done.other_idx, f32[96,128]{1,0:T(8,128)} %rhs_hbm.1, f32[96,128]{1,0:T(8,128)} %diag_hbm.1, s32[1,24]{1,0:T(1,128)} %idx_hbm.1), custom_call_target="tpu_custom_call" | custom-call | tf_op jit(solution)/shard_map/pallas_call | solution.py:381
  16.9 3.1 %all-to-all-done = bf16[16,96,128]{2,1,0:T(8,128)(2,1)S(1)} async-done(((bf16[16,96,128]{2,1,0:T(8,128)(2,1)}), bf16[16,96,128]{2,1,0:T(8,128)(2,1)S(1)}, u32[]{:S(2)}, u32[]{:S(2)}) %all-to-all-start) | async-done | bytes 393248 | tf_op jit(solution)/shard_map/all_to_all | solution.py:416
  20.2 1.9 %collective-permute-start.1 = (bf16[32,256]{1,0:T(8,128)(2,1)S(1)}, bf16[32,256]{1,0:T(8,128)(2,1)S(1)}, u32[]{:S(2)}, u32[]{:S(2)}) collective-permute-start(bf16[32,256]{1,0:T(8,128)(2,1)S(1)} %get-tuple-element.48), channel_id=1, source_target_pairs={{0,16},{16,0},{1,17},{17,1},{2,18},{18,2},{3,19},{19,3},{4,20},{20... | collective-permute-start | bytes 49160 | tf_op jit(solution)/shard_map/ppermute | solution.py:396
  22.2 0.4 shard_map.80.lower
  22.6 0.4 collective-permute-done.1.got
  23.0 0.8 shard_map.81
  23.8 16.9 %all_to_all.20 = bf16[64,13,2,128]{3,2,1,0:T(2,128)(2,1)S(1)} all-to-all(bf16[64,13,2,128]{3,2,1,0:T(2,128)(2,1)S(1)} %bitcast.18), channel_id=1, replica_groups=mesh['x'=4,'core'=2,'z'=4,'y'=4] {'x','z','y'}, dimensions={0} | all-to-all | bytes 851968 | tf_op jit(solution)/shard_map/all_to_all | solution.py:401
  40.7 0.6 shard_map.82
  41.4 2.2 %collective-permute-start.2 = (f32[128,128]{1,0:T(8,128)S(1)}, f32[128,128]{1,0:T(8,128)S(1)}, u32[]{:S(2)}, u32[]{:S(2)}) collective-permute-start(f32[128,128]{1,0:T(8,128)S(1)} %get-tuple-element.56), channel_id=1, source_target_pairs={{0,16},{16,0},{1,17},{17,1},{2,18},{18,2},{3,19},{19,3},{4,20},{20... | collective-permute-start | bytes 196616 | tf_op jit(solution)/shard_map/ppermute | solution.py:396
  43.6 0.9 %collective-permute-done.2.got = f32[128,128]{1,0:T(8,128)S(1)} collective-permute-done((f32[128,128]{1,0:T(8,128)S(1)}, f32[128,128]{1,0:T(8,128)S(1)}, u32[]{:S(2)}, u32[]{:S(2)}) %collective-permute-start.2) | collective-permute-done | bytes 65568 | tf_op jit(solution)/shard_map/ppermute | solution.py:396
  44.5 0.9 %shard_map.83 = (bf16[1664,128]{1,0:T(8,128)(2,1)S(1)}, f32[32,128]{1,0:T(8,128)S(1)}, f32[32,128]{1,0:T(8,128)S(1)}, f32[2,128]{1,0:T(2,128)S(1)}, f32[96,128]{...) custom-call(f32[128,128]{1,0:T(8,128)S(1)} %get-tuple-element.55.keep, ...), custom_call_target="tpu_custom_call" | custom-call | tf_op jit(solution)/shard_map/pallas_call | solution.py:381
  45.4 15.3 %all_to_all.21 = bf16[64,13,2,128]{3,2,1,0:T(2,128)(2,1)S(1)} all-to-all(bf16[64,13,2,128]{3,2,1,0:T(2,128)(2,1)S(1)} %bitcast.17), channel_id=1, replica_groups=mesh['x'=4,'core'=2,'z'=4,'y'=4] {'x','z','y'}, dimensions={0} | all-to-all | bytes 851968 | tf_op jit(solution)/shard_map/all_to_all | solution.py:401
  61.1 2.2 %collective-permute-start.3 = (f32[128,128]{1,0:T(8,128)S(1)}, f32[128,128]{1,0:T(8,128)S(1)}, u32[]{:S(2)}, u32[]{:S(2)}) collective-permute-start(f32[128,128]{1,0:T(8,128)S(1)} %get-tuple-element.62), channel_id=1, source_target_pairs={{0,16},{16,0},{1,17},{17,1},{2,18},{18,2},{3,19},{19,3},{4,20},{20... | collective-permute-start | bytes 196616 | tf_op jit(solution)/shard_map/ppermute | solution.py:396
  63.3 0.9 %collective-permute-done.3.got = f32[128,128]{1,0:T(8,128)S(1)} collective-permute-done((f32[128,128]{1,0:T(8,128)S(1)}, f32[128,128]{1,0:T(8,128)S(1)}, u32[]{:S(2)}, u32[]{:S(2)}) %collective-permute-start.3) | collective-permute-done | bytes 65568 | tf_op jit(solution)/shard_map/ppermute | solution.py:396
  64.2 0.9 %shard_map.85 = (bf16[1664,128]{1,0:T(8,128)(2,1)S(1)}, f32[2,128]{1,0:T(2,128)S(1)}, f32[96,128]{1,0:T(8,128)S(1)}, f32[96,128]{1,0:T(8,128)S(1)}, f32[96,128]{1,0:T(8,128)S(1)}, /*index=5*/f32[96,128]{1,0:T(8,128)S(1)}) custom-call(f32[128,128]{1,0:T(8,128)S(1)} %get-tuple-element.61.keep, f32[128,128]{1,0:T(8,128)S(1)} %collective-permute-done.3.got, ...), custom_call_target="tpu_custom_call" | custom-call | tf_op jit(solution)/shard_map/pallas_call | solution.py:381
  65.1 15.4 %all_to_all.22 = bf16[64,13,2,128]{3,2,1,0:T(2,128)(2,1)S(1)} all-to-all(bf16[64,13,2,128]{3,2,1,0:T(2,128)(2,1)S(1)} %bitcast.16), channel_id=1, replica_groups=mesh['x'=4,'core'=2,'z'=4,'y'=4] {'x','z','y'}, dimensions={0} | all-to-all | bytes 851968 | tf_op jit(solution)/shard_map/all_to_all | solution.py:401
  80.8 2.2 %collective-permute-start.4 = (f32[128,128]{1,0:T(8,128)S(1)}, f32[128,128]{1,0:T(8,128)S(1)}, u32[]{:S(2)}, u32[]{:S(2)}) collective-permute-start(f32[128,128]{1,0:T(8,128)S(1)} %get-tuple-element.72), channel_id=1, source_target_pairs={{0,16},{16,0},{1,17},{17,1},{2,18},{18,2},{3,19},{19,3},{4,20},{20... | collective-permute-start | bytes 196616 | tf_op jit(solution)/shard_map/ppermute | solution.py:396
  83.0 0.9 %collective-permute-done.4.got = f32[128,128]{1,0:T(8,128)S(1)} collective-permute-done((f32[128,128]{1,0:T(8,128)S(1)}, f32[128,128]{1,0:T(8,128)S(1)}, u32[]{:S(2)}, u32[]{:S(2)}) %collective-permute-start.4) | collective-permute-done | bytes 65568 | tf_op jit(solution)/shard_map/ppermute | solution.py:396
  83.9 0.8 shard_map.87
  (5 shorter events, 0.8 us)
Async XLA Ops:
  2.2 17.8 %all-to-all-start = ((bf16[16,96,128]{2,1,0:T(8,128)(2,1)}), bf16[16,96,128]{2,1,0:T(8,128)(2,1)S(1)}, u32[]{:S(2)}, u32[]{:S(2)}) async-start(bf16[16,96,128]{2,1,0:T(8,128)(2,1)} %broadcast_in_dim.2), calls=%async_computation | async-start | bytes 786432 | tf_op jit(solution)/shard_map/all_to_all | solution.py:416
  10.8 5.2 %collective-permute-start = (s32[1,24]{1,0:T(1,128)}, s32[1,24]{1,0:T(1,128)S(1)}, u32[]{:S(2)}, u32[]{:S(2)}) collective-permute-start(s32[1,24]{1,0:T(1,128)} %idx_hbm.1), channel_id=1, source_target_pairs={{0,16},{16,0},{1,17},{17,1},{2,18},{18,2},{3,19},{19,3},{4,20},{20... | collective-permute-start | bytes 296 | tf_op jit(solution)/shard_map/ppermute | solution.py:396
  20.2 2.8 %collective-permute-start.1 = (bf16[32,256]{1,0:T(8,128)(2,1)S(1)}, bf16[32,256]{1,0:T(8,128)(2,1)S(1)}, u32[]{:S(2)}, u32[]{:S(2)}) collective-permute-start(bf16[32,256]{1,0:T(8,128)(2,1)S(1)} %get-tuple-element.48), channel_id=1, source_target_pairs={{0,16},{16,0},{1,17},{17,1},{2,18},{18,2},{3,19},{19,3},{4,20},{20... | collective-permute-start | bytes 49160 | tf_op jit(solution)/shard_map/ppermute | solution.py:396
  41.4 3.1 %collective-permute-start.2 = (f32[128,128]{1,0:T(8,128)S(1)}, f32[128,128]{1,0:T(8,128)S(1)}, u32[]{:S(2)}, u32[]{:S(2)}) collective-permute-start(f32[128,128]{1,0:T(8,128)S(1)} %get-tuple-element.56), channel_id=1, source_target_pairs={{0,16},{16,0},{1,17},{17,1},{2,18},{18,2},{3,19},{19,3},{4,20},{20... | collective-permute-start | bytes 196616 | tf_op jit(solution)/shard_map/ppermute | solution.py:396
  61.1 3.1 %collective-permute-start.3 = (f32[128,128]{1,0:T(8,128)S(1)}, f32[128,128]{1,0:T(8,128)S(1)}, u32[]{:S(2)}, u32[]{:S(2)}) collective-permute-start(f32[128,128]{1,0:T(8,128)S(1)} %get-tuple-element.62), channel_id=1, source_target_pairs={{0,16},{16,0},{1,17},{17,1},{2,18},{18,2},{3,19},{19,3},{4,20},{20... | collective-permute-start | bytes 196616 | tf_op jit(solution)/shard_map/ppermute | solution.py:396
  80.8 3.1 %collective-permute-start.4 = (f32[128,128]{1,0:T(8,128)S(1)}, f32[128,128]{1,0:T(8,128)S(1)}, u32[]{:S(2)}, u32[]{:S(2)}) collective-permute-start(f32[128,128]{1,0:T(8,128)S(1)} %get-tuple-element.72), channel_id=1, source_target_pairs={{0,16},{16,0},{1,17},{17,1},{2,18},{18,2},{3,19},{19,3},{4,20},{20... | collective-permute-start | bytes 196616 | tf_op jit(solution)/shard_map/ppermute | solution.py:396

commit v12 on v11

--- a/solution.py
+++ b/solution.py
@@ -39,7 +39,7 @@
 
 
 def only_row(values, r):
-    rows = lax.broadcasted_iota(jnp.int32, (PAD, WIDTH), 0)
+    rows = lax.broadcasted_iota(jnp.int32, values.shape, 0)
     return jnp.where(rows == r, values, 0.0).astype(BF16)
 
 
@@ -47,11 +47,14 @@
     rows = lax.broadcasted_iota(jnp.int32, (PAD, WIDTH), 0)
     exact = y.astype(BF16).astype(F32)
     columns = jnp.concatenate([exact] * (WIDTH // PAD), axis=0).T
-    spread = jnp.zeros((PAD, UPPER * WIDTH), F32)
+    half = PAD // 2
+    spread = [jnp.zeros((half, UPPER * WIDTH), F32) for group in range(2)]
     below = [jnp.zeros((PAD, WIDTH), F32) for band in range(LOWER)]
     for r in range(0, ROWS, 2):
-        pair = jnp.concatenate([only_row(y, r), only_row(y, r + 1)], axis=1)
-        spread += dot_nn(pair, upper[r : r + 2].reshape(2 * WIDTH, UPPER * WIDTH))
+        group = r // half
+        some = y[group * half : (group + 1) * half, :]
+        pair = jnp.concatenate([only_row(some, r % half), only_row(some, r % half + 1)], axis=1)
+        spread[group] += dot_nn(pair, upper[r : r + 2].reshape(2 * WIDTH, UPPER * WIDTH))
         for d in (r, r + 1):
             for band in range(LOWER):
                 c = d + band - LOWER
@@ -59,6 +62,7 @@
                     block = lower[d, :, band * WIDTH : (band + 1) * WIDTH].astype(F32)
                     line = column_sum(block * columns[:, d : d + 1])
                     below[band] = jnp.where(rows == c, line, below[band])
+    spread = jnp.concatenate(spread, axis=0)
     lifted = spread[:, 0:WIDTH] + below[0] + below[1]
     for band in range(1, UPPER):
         lifted += pltpu.roll(spread[:, band * WIDTH : (band + 1) * WIDTH], band, 0)
@@ -304,6 +308,10 @@
     give_and_keep(dot_nn(hot[...], part[...]), keep, give)
 
 
+def last_sum(part, hot, half):
+    half[...] = dot_nn(hot[PAD // 2 : PAD + OWN, :], part[...])
+
+
 def advance(total, us, inv_s, ps, u, cost, q, d, x, r, per_gamma, per_alpha):
     gamma = jnp.sum(total[ROWS : ROWS + 1, :], axis=1, keepdims=True)
     delta = jnp.sum(total[ROWS + 1 : ROWS + 2, :], axis=1, keepdims=True)
@@ -362,8 +370,8 @@
     next_message(msg_out, u_s, inv * rn, rn, c, upper, lower)
 
 
-def last_kernel(keep, got, scal, d, q, x, r, cost, x_out, r_out):
-    total = keep[...] + got[...]
+def last_kernel(half, got, scal, d, q, x, r, cost, x_out, r_out):
+    total = jnp.concatenate([jnp.zeros((PAD // 2, WIDTH), F32), half[...] + got[...]], axis=0)
     c = cost[...]
     found = advance(
         total, None, None, None, r[...] / c, c, q[...], d[...], x[...], r[...],
@@ -454,8 +462,8 @@
         keep, other_core(give), us, ps, inv_s, sc, d, q, x, r, cost, upper, lower,
     )
     near = to_all(sent)
-    keep, give = call(message_sum, [sums, sums], near, hot)
-    return call(last_kernel, [own, own], keep, other_core(give), sc, d, q, x, r, cost)
+    half = call(last_sum, [((PAD // 2 + OWN, WIDTH), F32)], near, hot)[0]
+    return call(last_kernel, [own, own], half, other_core(half), sc, d, q, x, r, cost)
 
 
 def solution(mesh):

time: 85.2 us -> 85 us (level)
  no operation moved by 1% of the time
where the time goes in v12:
time: 85 us; the launch traced here: 84.5 us
  blocking collectives  47.6 us (56%)
  starting transfers between devices  18.3 us (22%)
  Pallas kernels  10.1 us (12%)
  waiting for transfers between devices  6.21 us (7%)
    all_to_all x3, blocking collectives, to_all(): near = lax.all_to_all(sent, ('x', 'z', 'y'), 0, 0, tiled=True)  47.6 us
    pallas_call x11, Pallas kernels, call(): pl.pallas_call(kernel, out_shape=[(pltpu.HBM if hbm_out else jax.ShapeDty...  10.1 us
    ppermute x5, starting transfers between devices, other_core(): return lax.ppermute(values, 'core', [(0, 1), (1, 0)])  9.7 us
    all_to_all x1, starting transfers between devices, shards(): near = lax.all_to_all(sent, ('z', 'y'), 0, 0, tiled=True)  8.6 us
    all_to_all x1, waiting for transfers between devices, shards(): near = lax.all_to_all(sent, ('z', 'y'), 0, 0, tiled=True)  3.12 us
    ppermute x5, waiting for transfers between devices, other_core(): return lax.ppermute(values, 'core', [(0, 1), (1, 0)])  3.1 us
  transfers between devices with their start and end apart: 6, of which 5 were waited for; matrix products, arithmetic and copies ran while one was open for 0% of the time, Pallas kernels for 6%

profile of v12, /device:TPU:1, one launch (start us, length us, event | category | flops | bytes accessed | tf_op | source)
XLA Modules:
  0.0 84.5 jit_solution(18247387634186763930)
XLA Ops:
  0.6 0.8 multiply_convert_fusion
  1.4 0.8 broadcast_in_dim.2
  2.2 8.6 %all-to-all-start = ((bf16[16,96,128]{2,1,0:T(8,128)(2,1)}), bf16[16,96,128]{2,1,0:T(8,128)(2,1)S(1)}, u32[]{:S(2)}, u32[]{:S(2)}) async-start(bf16[16,96,128]{2,1,0:T(8,128)(2,1)} %broadcast_in_dim.2), calls=%async_computation | async-start | bytes 786432 | tf_op jit(solution)/shard_map/all_to_all | solution.py:424
  10.8 1.0 %collective-permute-start = (s32[1,24]{1,0:T(1,128)}, s32[1,24]{1,0:T(1,128)S(1)}, u32[]{:S(2)}, u32[]{:S(2)}) collective-permute-start(s32[1,24]{1,0:T(1,128)} %idx_hbm.1), channel_id=1, source_target_pairs={{0,16},{16,0},{1,17},{17,1},{2,18},{18,2},{3,19},{19,3},{4,20},{20... | collective-permute-start | bytes 296 | tf_op jit(solution)/shard_map/ppermute | solution.py:404
  11.9 4.1 %shard_map.77.upper = bf16[24,128,384]{2,1,0:T(8,128)(2,1)S(1)} custom-call(s32[2,24]{1,0:T(2,128)} %bitcast.21, bf16[24,128,128]{2,1,0:T(8,128)(2,1)} %bitcast.20, bf16[24,3,128,128]{3,2,1,0:T(8,128)(2,1)} %bitcast.19), custom_call_target="tpu_custom_call" | custom-call | tf_op jit(solution)/shard_map/pallas_call | solution.py:389
  16.0 0.9 %shard_map.78 = (f32[96,128]{1,0:T(8,128)S(1)}, f32[96,128]{1,0:T(8,128)S(1)}, s32[160,128]{1,0:T(8,128)S(1)}, f32[2,128]{1,0:T(2,128)S(1)}, bf16[128,1664]{1,0:T(8,128)(2,1)S(1)}) custom-call(s32[1,24]{1,0:T(1,128)S(1)} %collective-permute-done.other_idx, f32[96,128]{1,0:T(8,128)} %rhs_hbm.1, f32[96,128]{1,0:T(8,128)} %diag_hbm.1, s32[1,24]{1,0:T(1,128)} %idx_hbm.1), custom_call_target="tpu_custom_call" | custom-call | tf_op jit(solution)/shard_map/pallas_call | solution.py:389
  16.9 3.1 %all-to-all-done = bf16[16,96,128]{2,1,0:T(8,128)(2,1)S(1)} async-done(((bf16[16,96,128]{2,1,0:T(8,128)(2,1)}), bf16[16,96,128]{2,1,0:T(8,128)(2,1)S(1)}, u32[]{:S(2)}, u32[]{:S(2)}) %all-to-all-start) | async-done | bytes 393248 | tf_op jit(solution)/shard_map/all_to_all | solution.py:424
  20.2 1.9 %collective-permute-start.1 = (bf16[32,256]{1,0:T(8,128)(2,1)S(1)}, bf16[32,256]{1,0:T(8,128)(2,1)S(1)}, u32[]{:S(2)}, u32[]{:S(2)}) collective-permute-start(bf16[32,256]{1,0:T(8,128)(2,1)S(1)} %get-tuple-element.46), channel_id=1, source_target_pairs={{0,16},{16,0},{1,17},{17,1},{2,18},{18,2},{3,19},{19,3},{4,20},{20... | collective-permute-start | bytes 49160 | tf_op jit(solution)/shard_map/ppermute | solution.py:404
  22.2 0.4 shard_map.80.lower
  22.6 0.4 collective-permute-done.1.got
  23.0 0.7 shard_map.81
  23.8 16.9 %all_to_all.20 = bf16[64,13,2,128]{3,2,1,0:T(2,128)(2,1)S(1)} all-to-all(bf16[64,13,2,128]{3,2,1,0:T(2,128)(2,1)S(1)} %bitcast.18), channel_id=1, replica_groups=mesh['x'=4,'core'=2,'z'=4,'y'=4] {'x','z','y'}, dimensions={0} | all-to-all | bytes 851968 | tf_op jit(solution)/shard_map/all_to_all | solution.py:409
  40.7 0.6 shard_map.82
  41.3 2.2 %collective-permute-start.2 = (f32[128,128]{1,0:T(8,128)S(1)}, f32[128,128]{1,0:T(8,128)S(1)}, u32[]{:S(2)}, u32[]{:S(2)}) collective-permute-start(f32[128,128]{1,0:T(8,128)S(1)} %get-tuple-element.54), channel_id=1, source_target_pairs={{0,16},{16,0},{1,17},{17,1},{2,18},{18,2},{3,19},{19,3},{4,20},{20... | collective-permute-start | bytes 196616 | tf_op jit(solution)/shard_map/ppermute | solution.py:404
  43.5 0.9 %collective-permute-done.2.got = f32[128,128]{1,0:T(8,128)S(1)} collective-permute-done((f32[128,128]{1,0:T(8,128)S(1)}, f32[128,128]{1,0:T(8,128)S(1)}, u32[]{:S(2)}, u32[]{:S(2)}) %collective-permute-start.2) | collective-permute-done | bytes 65568 | tf_op jit(solution)/shard_map/ppermute | solution.py:404
  44.4 0.9 %shard_map.83 = (bf16[1664,128]{1,0:T(8,128)(2,1)S(1)}, f32[32,128]{1,0:T(8,128)S(1)}, f32[32,128]{1,0:T(8,128)S(1)}, f32[2,128]{1,0:T(2,128)S(1)}, f32[96,128]{...) custom-call(f32[128,128]{1,0:T(8,128)S(1)} %get-tuple-element.53.keep, ...), custom_call_target="tpu_custom_call" | custom-call | tf_op jit(solution)/shard_map/pallas_call | solution.py:389
  45.3 15.3 %all_to_all.21 = bf16[64,13,2,128]{3,2,1,0:T(2,128)(2,1)S(1)} all-to-all(bf16[64,13,2,128]{3,2,1,0:T(2,128)(2,1)S(1)} %bitcast.17), channel_id=1, replica_groups=mesh['x'=4,'core'=2,'z'=4,'y'=4] {'x','z','y'}, dimensions={0} | all-to-all | bytes 851968 | tf_op jit(solution)/shard_map/all_to_all | solution.py:409
  61.0 2.2 %collective-permute-start.3 = (f32[128,128]{1,0:T(8,128)S(1)}, f32[128,128]{1,0:T(8,128)S(1)}, u32[]{:S(2)}, u32[]{:S(2)}) collective-permute-start(f32[128,128]{1,0:T(8,128)S(1)} %get-tuple-element.60), channel_id=1, source_target_pairs={{0,16},{16,0},{1,17},{17,1},{2,18},{18,2},{3,19},{19,3},{4,20},{20... | collective-permute-start | bytes 196616 | tf_op jit(solution)/shard_map/ppermute | solution.py:404
  63.2 0.9 %collective-permute-done.3.got = f32[128,128]{1,0:T(8,128)S(1)} collective-permute-done((f32[128,128]{1,0:T(8,128)S(1)}, f32[128,128]{1,0:T(8,128)S(1)}, u32[]{:S(2)}, u32[]{:S(2)}) %collective-permute-start.3) | collective-permute-done | bytes 65568 | tf_op jit(solution)/shard_map/ppermute | solution.py:404
  64.1 0.9 %shard_map.85 = (bf16[1664,128]{1,0:T(8,128)(2,1)S(1)}, f32[2,128]{1,0:T(2,128)S(1)}, f32[96,128]{1,0:T(8,128)S(1)}, f32[96,128]{1,0:T(8,128)S(1)}, f32[96,128]{1,0:T(8,128)S(1)}, /*index=5*/f32[96,128]{1,0:T(8,128)S(1)}) custom-call(f32[128,128]{1,0:T(8,128)S(1)} %get-tuple-element.59.keep, f32[128,128]{1,0:T(8,128)S(1)} %collective-permute-done.3.got, ...), custom_call_target="tpu_custom_call" | custom-call | tf_op jit(solution)/shard_map/pallas_call | solution.py:389
  65.0 15.3 %all_to_all.22 = bf16[64,13,2,128]{3,2,1,0:T(2,128)(2,1)S(1)} all-to-all(bf16[64,13,2,128]{3,2,1,0:T(2,128)(2,1)S(1)} %bitcast.16), channel_id=1, replica_groups=mesh['x'=4,'core'=2,'z'=4,'y'=4] {'x','z','y'}, dimensions={0} | all-to-all | bytes 851968 | tf_op jit(solution)/shard_map/all_to_all | solution.py:409
  80.6 2.2 %collective-permute-start.4 = (f32[112,128]{1,0:T(8,128)S(1)}, f32[112,128]{1,0:T(8,128)S(1)}, u32[]{:S(2)}, u32[]{:S(2)}) collective-permute-start(f32[112,128]{1,0:T(8,128)S(1)} %shard_map.86.half), channel_id=1, source_target_pairs={{0,16},{16,0},{1,17},{17,1},{2,18},{18,2},{3,19},{19,3},{4,20},{20... | collective-permute-start | bytes 172040 | tf_op jit(solution)/shard_map/ppermute | solution.py:404
  82.9 0.9 %collective-permute-done.4.got = f32[112,128]{1,0:T(8,128)S(1)} collective-permute-done((f32[112,128]{1,0:T(8,128)S(1)}, f32[112,128]{1,0:T(8,128)S(1)}, u32[]{:S(2)}, u32[]{:S(2)}) %collective-permute-start.4) | collective-permute-done | bytes 57376 | tf_op jit(solution)/shard_map/ppermute | solution.py:404
  83.8 0.8 shard_map.87
  (5 shorter events, 0.8 us)
Async XLA Ops:
  2.2 17.8 %all-to-all-start = ((bf16[16,96,128]{2,1,0:T(8,128)(2,1)}), bf16[16,96,128]{2,1,0:T(8,128)(2,1)S(1)}, u32[]{:S(2)}, u32[]{:S(2)}) async-start(bf16[16,96,128]{2,1,0:T(8,128)(2,1)} %broadcast_in_dim.2), calls=%async_computation | async-start | bytes 786432 | tf_op jit(solution)/shard_map/all_to_all | solution.py:424
  10.8 5.2 %collective-permute-start = (s32[1,24]{1,0:T(1,128)}, s32[1,24]{1,0:T(1,128)S(1)}, u32[]{:S(2)}, u32[]{:S(2)}) collective-permute-start(s32[1,24]{1,0:T(1,128)} %idx_hbm.1), channel_id=1, source_target_pairs={{0,16},{16,0},{1,17},{17,1},{2,18},{18,2},{3,19},{19,3},{4,20},{20... | collective-permute-start | bytes 296 | tf_op jit(solution)/shard_map/ppermute | solution.py:404
  20.2 2.8 %collective-permute-start.1 = (bf16[32,256]{1,0:T(8,128)(2,1)S(1)}, bf16[32,256]{1,0:T(8,128)(2,1)S(1)}, u32[]{:S(2)}, u32[]{:S(2)}) collective-permute-start(bf16[32,256]{1,0:T(8,128)(2,1)S(1)} %get-tuple-element.46), channel_id=1, source_target_pairs={{0,16},{16,0},{1,17},{17,1},{2,18},{18,2},{3,19},{19,3},{4,20},{20... | collective-permute-start | bytes 49160 | tf_op jit(solution)/shard_map/ppermute | solution.py:404
  41.3 3.1 %collective-permute-start.2 = (f32[128,128]{1,0:T(8,128)S(1)}, f32[128,128]{1,0:T(8,128)S(1)}, u32[]{:S(2)}, u32[]{:S(2)}) collective-permute-start(f32[128,128]{1,0:T(8,128)S(1)} %get-tuple-element.54), channel_id=1, source_target_pairs={{0,16},{16,0},{1,17},{17,1},{2,18},{18,2},{3,19},{19,3},{4,20},{20... | collective-permute-start | bytes 196616 | tf_op jit(solution)/shard_map/ppermute | solution.py:404
  61.0 3.1 %collective-permute-start.3 = (f32[128,128]{1,0:T(8,128)S(1)}, f32[128,128]{1,0:T(8,128)S(1)}, u32[]{:S(2)}, u32[]{:S(2)}) collective-permute-start(f32[128,128]{1,0:T(8,128)S(1)} %get-tuple-element.60), channel_id=1, source_target_pairs={{0,16},{16,0},{1,17},{17,1},{2,18},{18,2},{3,19},{19,3},{4,20},{20... | collective-permute-start | bytes 196616 | tf_op jit(solution)/shard_map/ppermute | solution.py:404
  80.6 3.1 %collective-permute-start.4 = (f32[112,128]{1,0:T(8,128)S(1)}, f32[112,128]{1,0:T(8,128)S(1)}, u32[]{:S(2)}, u32[]{:S(2)}) collective-permute-start(f32[112,128]{1,0:T(8,128)S(1)} %shard_map.86.half), channel_id=1, source_target_pairs={{0,16},{16,0},{1,17},{17,1},{2,18},{18,2},{3,19},{19,3},{4,20},{20... | collective-permute-start | bytes 172040 | tf_op jit(solution)/shard_map/ppermute | solution.py:404

commit v13 on v12

--- a/solution.py
+++ b/solution.py
@@ -117,7 +117,8 @@
 
 def here():
     vec = lax.axis_index("z") * 4 + lax.axis_index("y")
-    return lax.axis_index("core"), lax.axis_index("x") * PLANE + vec, vec
+    chip = lax.axis_index("x") * PLANE + lax.axis_index("y") * 4 + lax.axis_index("z")
+    return lax.axis_index("core"), chip, vec
 
 
 def copy_parts(source, target, sems, first, parts):
@@ -355,7 +356,7 @@
 
 def third_kernel(
     keep, got, us, ps, inv_s, scal, d, q, x, r, cost, upper, lower,
-    msg_out, scal_out, d_out, q_out, x_out, r_out,
+    msg_out, scal_out, d_out, q_out, x_out, r_out, u_out,
 ):
     total = keep[...] + got[...]
     c = cost[...]
@@ -367,14 +368,16 @@
     d_out[...], q_out[...], x_out[...], r_out[...] = dn, qn, xn, rn
     scal_out[0:1, :] = jnp.broadcast_to(1.0 / gamma, (1, WIDTH))
     scal_out[1:2, :] = jnp.broadcast_to(1.0 / alpha, (1, WIDTH))
-    next_message(msg_out, u_s, inv * rn, rn, c, upper, lower)
-
-
-def last_kernel(half, got, scal, d, q, x, r, cost, x_out, r_out):
+    un = inv * rn
+    u_out[...] = un
+    next_message(msg_out, u_s, un, rn, c, upper, lower)
+
+
+def last_kernel(half, got, scal, d, q, x, r, u, cost, x_out, r_out):
     total = jnp.concatenate([jnp.zeros((PAD // 2, WIDTH), F32), half[...] + got[...]], axis=0)
     c = cost[...]
     found = advance(
-        total, None, None, None, r[...] / c, c, q[...], d[...], x[...], r[...],
+        total, None, None, None, u[...], c, q[...], d[...], x[...], r[...],
         scal[0:1, 0:1], scal[1:2, 0:1],
     )
     x_out[...], r_out[...] = found[6], found[7]
@@ -406,7 +409,7 @@
 
 def to_all(sent):
     sent = sent.reshape(CHIPS, SENT // 2, 2, WIDTH)
-    near = lax.all_to_all(sent, ("x", "z", "y"), 0, 0, tiled=True)
+    near = lax.all_to_all(sent, ("x", "y", "z"), 0, 0, tiled=True)
     return near.reshape(CHIPS * SENT, WIDTH)
 
 
@@ -457,13 +460,13 @@
     )
     near = to_all(sent)
     keep, give = call(message_sum, [sums, sums], near, hot)
-    sent, sc, d, q, x, r = call(
-        third_kernel, [msg, scal, own, own, own, own],
+    sent, sc, d, q, x, r, u = call(
+        third_kernel, [msg, scal, own, own, own, own, own],
         keep, other_core(give), us, ps, inv_s, sc, d, q, x, r, cost, upper, lower,
     )
     near = to_all(sent)
     half = call(last_sum, [((PAD // 2 + OWN, WIDTH), F32)], near, hot)[0]
-    return call(last_kernel, [own, own], half, other_core(half), sc, d, q, x, r, cost)
+    return call(last_kernel, [own, own], half, other_core(half), sc, d, q, x, r, u, cost)
 
 
 def solution(mesh):

time: 85 us -> 85 us (level)
  no operation moved by 1% of the time
where the time goes in v13:
time: 85 us; the launch traced here: 84.5 us
  blocking collectives  48 us (56%)
  starting transfers between devices  17.9 us (21%)
  Pallas kernels  10.1 us (12%)
  waiting for transfers between devices  6.2 us (7%)
    all_to_all x3, blocking collectives, to_all(): near = lax.all_to_all(sent, ('x', 'y', 'z'), 0, 0, tiled=True)  48 us
    pallas_call x11, Pallas kernels, call(): pl.pallas_call(kernel, out_shape=[(pltpu.HBM if hbm_out else jax.ShapeDty...  10.1 us
    ppermute x5, starting transfers between devices, other_core(): return lax.ppermute(values, 'core', [(0, 1), (1, 0)])  9.3 us
    all_to_all x1, starting transfers between devices, shards(): near = lax.all_to_all(sent, ('z', 'y'), 0, 0, tiled=True)  8.6 us
    all_to_all x1, waiting for transfers between devices, shards(): near = lax.all_to_all(sent, ('z', 'y'), 0, 0, tiled=True)  3.11 us
    ppermute x5, waiting for transfers between devices, other_core(): return lax.ppermute(values, 'core', [(0, 1), (1, 0)])  3.1 us
  transfers between devices with their start and end apart: 6, of which 5 were waited for; matrix products, arithmetic and copies ran while one was open for 0% of the time, Pallas kernels for 6%

profile of v13, /device:TPU:1, one launch (start us, length us, event | category | flops | bytes accessed | tf_op | source)
XLA Modules:
  0.0 84.5 jit_solution(17218757885701506302)
XLA Ops:
  0.6 0.8 multiply_convert_fusion
  1.4 0.8 broadcast_in_dim.2
  2.2 8.6 %all-to-all-start = ((bf16[16,96,128]{2,1,0:T(8,128)(2,1)}), bf16[16,96,128]{2,1,0:T(8,128)(2,1)S(1)}, u32[]{:S(2)}, u32[]{:S(2)}) async-start(bf16[16,96,128]{2,1,0:T(8,128)(2,1)} %broadcast_in_dim.2), calls=%async_computation | async-start | bytes 786432 | tf_op jit(solution)/shard_map/all_to_all | solution.py:427
  10.8 1.0 %collective-permute-start = (s32[1,24]{1,0:T(1,128)}, s32[1,24]{1,0:T(1,128)S(1)}, u32[]{:S(2)}, u32[]{:S(2)}) collective-permute-start(s32[1,24]{1,0:T(1,128)} %idx_hbm.1), channel_id=1, source_target_pairs={{0,16},{16,0},{1,17},{17,1},{2,18},{18,2},{3,19},{19,3},{4,20},{20... | collective-permute-start | bytes 296 | tf_op jit(solution)/shard_map/ppermute | solution.py:407
  11.9 4.1 %shard_map.77.upper = bf16[24,128,384]{2,1,0:T(8,128)(2,1)S(1)} custom-call(s32[2,24]{1,0:T(2,128)} %bitcast.21, bf16[24,128,128]{2,1,0:T(8,128)(2,1)} %bitcast.20, bf16[24,3,128,128]{3,2,1,0:T(8,128)(2,1)} %bitcast.19), custom_call_target="tpu_custom_call" | custom-call | tf_op jit(solution)/shard_map/pallas_call | solution.py:392
  16.0 0.9 %shard_map.78 = (f32[96,128]{1,0:T(8,128)S(1)}, f32[96,128]{1,0:T(8,128)S(1)}, s32[160,128]{1,0:T(8,128)S(1)}, f32[2,128]{1,0:T(2,128)S(1)}, bf16[128,1664]{1,0:T(8,128)(2,1)S(1)}) custom-call(s32[1,24]{1,0:T(1,128)S(1)} %collective-permute-done.other_idx, f32[96,128]{1,0:T(8,128)} %rhs_hbm.1, f32[96,128]{1,0:T(8,128)} %diag_hbm.1, s32[1,24]{1,0:T(1,128)} %idx_hbm.1), custom_call_target="tpu_custom_call" | custom-call | tf_op jit(solution)/shard_map/pallas_call | solution.py:392
  16.9 3.1 %all-to-all-done = bf16[16,96,128]{2,1,0:T(8,128)(2,1)S(1)} async-done(((bf16[16,96,128]{2,1,0:T(8,128)(2,1)}), bf16[16,96,128]{2,1,0:T(8,128)(2,1)S(1)}, u32[]{:S(2)}, u32[]{:S(2)}) %all-to-all-start) | async-done | bytes 393248 | tf_op jit(solution)/shard_map/all_to_all | solution.py:427
  20.2 1.9 %collective-permute-start.1 = (bf16[32,256]{1,0:T(8,128)(2,1)S(1)}, bf16[32,256]{1,0:T(8,128)(2,1)S(1)}, u32[]{:S(2)}, u32[]{:S(2)}) collective-permute-start(bf16[32,256]{1,0:T(8,128)(2,1)S(1)} %get-tuple-element.47), channel_id=1, source_target_pairs={{0,16},{16,0},{1,17},{17,1},{2,18},{18,2},{3,19},{19,3},{4,20},{20... | collective-permute-start | bytes 49160 | tf_op jit(solution)/shard_map/ppermute | solution.py:407
  22.2 0.4 shard_map.80.lower
  22.6 0.4 collective-permute-done.1.got
  23.0 0.7 shard_map.81
  23.8 17.0 %all_to_all.20 = bf16[64,13,2,128]{3,2,1,0:T(2,128)(2,1)S(1)} all-to-all(bf16[64,13,2,128]{3,2,1,0:T(2,128)(2,1)S(1)} %bitcast.18), channel_id=1, replica_groups=mesh['x'=4,'core'=2,'z'=4,'y'=4] {'x','y','z'}, dimensions={0} | all-to-all | bytes 851968 | tf_op jit(solution)/shard_map/all_to_all | solution.py:412
  40.8 0.6 shard_map.82
  41.4 2.1 %collective-permute-start.2 = (f32[128,128]{1,0:T(8,128)S(1)}, f32[128,128]{1,0:T(8,128)S(1)}, u32[]{:S(2)}, u32[]{:S(2)}) collective-permute-start(f32[128,128]{1,0:T(8,128)S(1)} %get-tuple-element.55), channel_id=1, source_target_pairs={{0,16},{16,0},{1,17},{17,1},{2,18},{18,2},{3,19},{19,3},{4,20},{20... | collective-permute-start | bytes 196616 | tf_op jit(solution)/shard_map/ppermute | solution.py:407
  43.5 0.9 %collective-permute-done.2.got = f32[128,128]{1,0:T(8,128)S(1)} collective-permute-done((f32[128,128]{1,0:T(8,128)S(1)}, f32[128,128]{1,0:T(8,128)S(1)}, u32[]{:S(2)}, u32[]{:S(2)}) %collective-permute-start.2) | collective-permute-done | bytes 65568 | tf_op jit(solution)/shard_map/ppermute | solution.py:407
  44.4 0.9 %shard_map.83 = (bf16[1664,128]{1,0:T(8,128)(2,1)S(1)}, f32[32,128]{1,0:T(8,128)S(1)}, f32[32,128]{1,0:T(8,128)S(1)}, f32[2,128]{1,0:T(2,128)S(1)}, f32[96,128]{...) custom-call(f32[128,128]{1,0:T(8,128)S(1)} %get-tuple-element.54.keep, ...), custom_call_target="tpu_custom_call" | custom-call | tf_op jit(solution)/shard_map/pallas_call | solution.py:392
  45.3 15.5 %all_to_all.21 = bf16[64,13,2,128]{3,2,1,0:T(2,128)(2,1)S(1)} all-to-all(bf16[64,13,2,128]{3,2,1,0:T(2,128)(2,1)S(1)} %bitcast.17), channel_id=1, replica_groups=mesh['x'=4,'core'=2,'z'=4,'y'=4] {'x','y','z'}, dimensions={0} | all-to-all | bytes 851968 | tf_op jit(solution)/shard_map/all_to_all | solution.py:412
  61.1 2.1 %collective-permute-start.3 = (f32[128,128]{1,0:T(8,128)S(1)}, f32[128,128]{1,0:T(8,128)S(1)}, u32[]{:S(2)}, u32[]{:S(2)}) collective-permute-start(f32[128,128]{1,0:T(8,128)S(1)} %get-tuple-element.61), channel_id=1, source_target_pairs={{0,16},{16,0},{1,17},{17,1},{2,18},{18,2},{3,19},{19,3},{4,20},{20... | collective-permute-start | bytes 196616 | tf_op jit(solution)/shard_map/ppermute | solution.py:407
  63.2 0.9 %collective-permute-done.3.got = f32[128,128]{1,0:T(8,128)S(1)} collective-permute-done((f32[128,128]{1,0:T(8,128)S(1)}, f32[128,128]{1,0:T(8,128)S(1)}, u32[]{:S(2)}, u32[]{:S(2)}) %collective-permute-start.3) | collective-permute-done | bytes 65568 | tf_op jit(solution)/shard_map/ppermute | solution.py:407
  64.1 0.9 %shard_map.85 = (bf16[1664,128]{1,0:T(8,128)(2,1)S(1)}, f32[2,128]{1,0:T(2,128)S(1)}, f32[96,128]{1,0:T(8,128)S(1)}, f32[96,128]{1,0:T(8,128)S(1)}, f32[96,128]{...) custom-call(f32[128,128]{1,0:T(8,128)S(1)} %get-tuple-element.60.keep, ...), custom_call_target="tpu_custom_call" | custom-call | tf_op jit(solution)/shard_map/pallas_call | solution.py:392
  65.0 15.5 %all_to_all.22 = bf16[64,13,2,128]{3,2,1,0:T(2,128)(2,1)S(1)} all-to-all(bf16[64,13,2,128]{3,2,1,0:T(2,128)(2,1)S(1)} %bitcast.16), channel_id=1, replica_groups=mesh['x'=4,'core'=2,'z'=4,'y'=4] {'x','y','z'}, dimensions={0} | all-to-all | bytes 851968 | tf_op jit(solution)/shard_map/all_to_all | solution.py:412
  80.8 2.1 %collective-permute-start.4 = (f32[112,128]{1,0:T(8,128)S(1)}, f32[112,128]{1,0:T(8,128)S(1)}, u32[]{:S(2)}, u32[]{:S(2)}) collective-permute-start(f32[112,128]{1,0:T(8,128)S(1)} %shard_map.86.half), channel_id=1, source_target_pairs={{0,16},{16,0},{1,17},{17,1},{2,18},{18,2},{3,19},{19,3},{4,20},{20... | collective-permute-start | bytes 172040 | tf_op jit(solution)/shard_map/ppermute | solution.py:407
  82.9 0.9 %collective-permute-done.4.got = f32[112,128]{1,0:T(8,128)S(1)} collective-permute-done((f32[112,128]{1,0:T(8,128)S(1)}, f32[112,128]{1,0:T(8,128)S(1)}, u32[]{:S(2)}, u32[]{:S(2)}) %collective-permute-start.4) | collective-permute-done | bytes 57376 | tf_op jit(solution)/shard_map/ppermute | solution.py:407
  83.8 0.8 shard_map.87
  (5 shorter events, 0.8 us)
Async XLA Ops:
  2.2 17.8 %all-to-all-start = ((bf16[16,96,128]{2,1,0:T(8,128)(2,1)}), bf16[16,96,128]{2,1,0:T(8,128)(2,1)S(1)}, u32[]{:S(2)}, u32[]{:S(2)}) async-start(bf16[16,96,128]{2,1,0:T(8,128)(2,1)} %broadcast_in_dim.2), calls=%async_computation | async-start | bytes 786432 | tf_op jit(solution)/shard_map/all_to_all | solution.py:427
  10.8 5.2 %collective-permute-start = (s32[1,24]{1,0:T(1,128)}, s32[1,24]{1,0:T(1,128)S(1)}, u32[]{:S(2)}, u32[]{:S(2)}) collective-permute-start(s32[1,24]{1,0:T(1,128)} %idx_hbm.1), channel_id=1, source_target_pairs={{0,16},{16,0},{1,17},{17,1},{2,18},{18,2},{3,19},{19,3},{4,20},{20... | collective-permute-start | bytes 296 | tf_op jit(solution)/shard_map/ppermute | solution.py:407
  20.2 2.8 %collective-permute-start.1 = (bf16[32,256]{1,0:T(8,128)(2,1)S(1)}, bf16[32,256]{1,0:T(8,128)(2,1)S(1)}, u32[]{:S(2)}, u32[]{:S(2)}) collective-permute-start(bf16[32,256]{1,0:T(8,128)(2,1)S(1)} %get-tuple-element.47), channel_id=1, source_target_pairs={{0,16},{16,0},{1,17},{17,1},{2,18},{18,2},{3,19},{19,3},{4,20},{20... | collective-permute-start | bytes 49160 | tf_op jit(solution)/shard_map/ppermute | solution.py:407
  41.4 3.0 %collective-permute-start.2 = (f32[128,128]{1,0:T(8,128)S(1)}, f32[128,128]{1,0:T(8,128)S(1)}, u32[]{:S(2)}, u32[]{:S(2)}) collective-permute-start(f32[128,128]{1,0:T(8,128)S(1)} %get-tuple-element.55), channel_id=1, source_target_pairs={{0,16},{16,0},{1,17},{17,1},{2,18},{18,2},{3,19},{19,3},{4,20},{20... | collective-permute-start | bytes 196616 | tf_op jit(solution)/shard_map/ppermute | solution.py:407
  61.1 3.0 %collective-permute-start.3 = (f32[128,128]{1,0:T(8,128)S(1)}, f32[128,128]{1,0:T(8,128)S(1)}, u32[]{:S(2)}, u32[]{:S(2)}) collective-permute-start(f32[128,128]{1,0:T(8,128)S(1)} %get-tuple-element.61), channel_id=1, source_target_pairs={{0,16},{16,0},{1,17},{17,1},{2,18},{18,2},{3,19},{19,3},{4,20},{20... | collective-permute-start | bytes 196616 | tf_op jit(solution)/shard_map/ppermute | solution.py:407
  80.8 3.0 %collective-permute-start.4 = (f32[112,128]{1,0:T(8,128)S(1)}, f32[112,128]{1,0:T(8,128)S(1)}, u32[]{:S(2)}, u32[]{:S(2)}) collective-permute-start(f32[112,128]{1,0:T(8,128)S(1)} %shard_map.86.half), channel_id=1, source_target_pairs={{0,16},{16,0},{1,17},{17,1},{2,18},{18,2},{3,19},{19,3},{4,20},{20... | collective-permute-start | bytes 172040 | tf_op jit(solution)/shard_map/ppermute | solution.py:407

commit v14 on v13

--- a/solution.py
+++ b/solution.py
@@ -203,7 +203,7 @@
 
 
 def index_kernel(
-    other_idx, rhs_hbm, diag_hbm, idx_hbm, rhs, diag, targets, labels, selector, idx, sems
+    other_idx, rhs_hbm, diag_hbm, idx_hbm, rhs, diag, inv, targets, labels, selector, idx, sems
 ):
     _, chip, vec = here()
     index = pltpu.make_async_copy(idx_hbm, idx, sems.at[2])
@@ -231,6 +231,7 @@
         labels[line : line + 1, :] = column_sum(jnp.where(mine, values, 0).astype(F32))
     for copy in copies:
         copy.wait()
+    inv[...] = 1.0 / diag[...]
 
 
 def fetch_kernel(near, targets, keep, give):
@@ -256,14 +257,14 @@
                 lower[d + band, :, at : at + WIDTH] = block.T
 
 
-def first_kernel(keep, got, labels, own, cost, upper, lower, msg_out, us_out, inv_out):
+def first_kernel(keep, got, labels, own, inv, upper, lower, msg_out, us_out, inv_out):
     chip = here()[1]
     total = keep[...] + got[...].astype(F32)
     us = total[:, 0:WIDTH]
     us_out[...], inv_out[...] = us, total[:, WIDTH:]
     lifted = scenario_lift(us, upper, lower)
     r = own[...]
-    ru = r * (r * (1.0 / cost[...]))
+    ru = r * (r * inv[...])
     lane = lax.broadcasted_iota(jnp.int32, (1, WIDTH), 1)
     turned = (lane - SENT * chip) & (WIDTH - 1)
     parts = []
@@ -337,12 +338,12 @@
 
 
 def second_kernel(
-    keep, got, us, inv_s, own, cost, upper, lower,
+    keep, got, us, inv_s, own, cost, inverse, upper, lower,
     msg_out, us_out, ps_out, scal_out, d_out, q_out, x_out, r_out,
 ):
     total = keep[...] + got[...]
     d = cost[...]
-    inv = 1.0 / d
+    inv = inverse[...]
     r = own[...]
     gamma, alpha, u_s, p_s, dn, qn, xn, rn = advance(
         total, us[...], inv_s[...], None, inv * r, d, None, None, None, r, None, None
@@ -355,12 +356,12 @@
 
 
 def third_kernel(
-    keep, got, us, ps, inv_s, scal, d, q, x, r, cost, upper, lower,
+    keep, got, us, ps, inv_s, scal, d, q, x, r, cost, inverse, upper, lower,
     msg_out, scal_out, d_out, q_out, x_out, r_out, u_out,
 ):
     total = keep[...] + got[...]
     c = cost[...]
-    inv = 1.0 / c
+    inv = inverse[...]
     gamma, alpha, u_s, p_s, dn, qn, xn, rn = advance(
         total, us[...], inv_s[...], ps[...], inv * r[...], c, q[...], d[...], x[...], r[...],
         scal[0:1, 0:1], scal[1:2, 0:1],
@@ -437,32 +438,32 @@
             (triple, BF16), (wide, BF16),
         ],
     )[0]
-    r, cost, targets, labels, selector = call(
-        index_kernel, [own, own, aims, scal, selectors],
+    r, cost, inv, targets, labels, selector = call(
+        index_kernel, [own, own, own, aims, scal, selectors],
         other_idx, weights=in_hbm(rhs, diag, couple_idx),
         scratch=[((1, ROWS), jnp.int32)], sems=3,
     )
-    near, upper, r, cost, targets, labels, selector = lax.optimization_barrier(
-        (near, upper, r, cost, targets, labels, selector)
+    near, upper, r, cost, inv, targets, labels, selector = lax.optimization_barrier(
+        (near, upper, r, cost, inv, targets, labels, selector)
     )
     pair = (PAD, 2 * WIDTH)
     keep, give = call(fetch_kernel, [(pair, F32), (pair, BF16)], near, targets)
     lower = call(lower_kernel, [below], upper)[0]
     sent, us, inv_s = call(
-        first_kernel, [msg, scen, scen], keep, other_core(give), labels, r, cost, upper, lower
+        first_kernel, [msg, scen, scen], keep, other_core(give), labels, r, inv, upper, lower
     )
 
     near = to_all(sent)
     hot, keep, give = call(label_sum, [hots, sums, sums], near, targets, selector)
     sent, us, ps, sc, d, q, x, r = call(
         second_kernel, [msg, scen, scen, scal, own, own, own, own],
-        keep, other_core(give), us, inv_s, r, cost, upper, lower,
+        keep, other_core(give), us, inv_s, r, cost, inv, upper, lower,
     )
     near = to_all(sent)
     keep, give = call(message_sum, [sums, sums], near, hot)
     sent, sc, d, q, x, r, u = call(
         third_kernel, [msg, scal, own, own, own, own, own],
-        keep, other_core(give), us, ps, inv_s, sc, d, q, x, r, cost, upper, lower,
+        keep, other_core(give), us, ps, inv_s, sc, d, q, x, r, cost, inv, upper, lower,
     )
     near = to_all(sent)
     half = call(last_sum, [((PAD // 2 + OWN, WIDTH), F32)], near, hot)[0]

time: 85 us -> 85 us (level)
  no operation moved by 1% of the time
where the time goes in v14:
time: 85 us; the launch traced here: 84.5 us
  blocking collectives  48 us (56%)
  starting transfers between devices  17.9 us (21%)
  Pallas kernels  10.1 us (12%)
  waiting for transfers between devices  6.19 us (7%)
    all_to_all x3, blocking collectives, to_all(): near = lax.all_to_all(sent, ('x', 'y', 'z'), 0, 0, tiled=True)  48 us
    pallas_call x11, Pallas kernels, call(): pl.pallas_call(kernel, out_shape=[(pltpu.HBM if hbm_out else jax.ShapeDty...  10.1 us
    ppermute x5, starting transfers between devices, other_core(): return lax.ppermute(values, 'core', [(0, 1), (1, 0)])  9.3 us
    all_to_all x1, starting transfers between devices, shards(): near = lax.all_to_all(sent, ('z', 'y'), 0, 0, tiled=True)  8.6 us
    ppermute x5, waiting for transfers between devices, other_core(): return lax.ppermute(values, 'core', [(0, 1), (1, 0)])  3.1 us
    all_to_all x1, waiting for transfers between devices, shards(): near = lax.all_to_all(sent, ('z', 'y'), 0, 0, tiled=True)  3.09 us
  transfers between devices with their start and end apart: 6, of which 5 were waited for; matrix products, arithmetic and copies ran while one was open for 0% of the time, Pallas kernels for 6%

profile of v14, /device:TPU:1, one launch (start us, length us, event | category | flops | bytes accessed | tf_op | source)
XLA Modules:
  0.0 84.5 jit_solution(13281138361458206207)
XLA Ops:
  0.6 0.8 multiply_convert_fusion
  1.4 0.8 broadcast_in_dim.2
  2.2 8.6 %all-to-all-start = ((bf16[16,96,128]{2,1,0:T(8,128)(2,1)}), bf16[16,96,128]{2,1,0:T(8,128)(2,1)S(1)}, u32[]{:S(2)}, u32[]{:S(2)}) async-start(bf16[16,96,128]{2,1,0:T(8,128)(2,1)} %broadcast_in_dim.2), calls=%async_computation | async-start | bytes 786432 | tf_op jit(solution)/shard_map/all_to_all | solution.py:428
  10.8 1.0 %collective-permute-start = (s32[1,24]{1,0:T(1,128)}, s32[1,24]{1,0:T(1,128)S(1)}, u32[]{:S(2)}, u32[]{:S(2)}) collective-permute-start(s32[1,24]{1,0:T(1,128)} %idx_hbm.1), channel_id=1, source_target_pairs={{0,16},{16,0},{1,17},{17,1},{2,18},{18,2},{3,19},{19,3},{4,20},{20... | collective-permute-start | bytes 296 | tf_op jit(solution)/shard_map/ppermute | solution.py:408
  11.9 4.1 %shard_map.77.upper = bf16[24,128,384]{2,1,0:T(8,128)(2,1)S(1)} custom-call(s32[2,24]{1,0:T(2,128)} %bitcast.21, bf16[24,128,128]{2,1,0:T(8,128)(2,1)} %bitcast.20, bf16[24,3,128,128]{3,2,1,0:T(8,128)(2,1)} %bitcast.19), custom_call_target="tpu_custom_call" | custom-call | tf_op jit(solution)/shard_map/pallas_call | solution.py:393
  16.0 0.9 %shard_map.78 = (f32[96,128]{1,0:T(8,128)S(1)}, f32[96,128]{1,0:T(8,128)S(1)}, f32[96,128]{1,0:T(8,128)S(1)}, s32[160,128]{1,0:T(8,128)S(1)}, f32[2,128]{1,0:T(2,128)S(1)}, /*index=5*/bf16[128,1664]{1,0:T(8,128)(2,1)S(1)}) custom-call(s32[1,24]{1,0:T(1,128)S(1)} %collective-permute-done.other_idx, f32[96,128]{1,0:T(8,128)} %rhs_hbm.1, f32[96,128]{1,0:T(8,128)} %diag_hbm.1, ...), custom_call_target="tpu_custom_call" | custom-call | tf_op jit(solution)/shard_map/pallas_call | solution.py:393
  16.9 3.1 %all-to-all-done = bf16[16,96,128]{2,1,0:T(8,128)(2,1)S(1)} async-done(((bf16[16,96,128]{2,1,0:T(8,128)(2,1)}), bf16[16,96,128]{2,1,0:T(8,128)(2,1)S(1)}, u32[]{:S(2)}, u32[]{:S(2)}) %all-to-all-start) | async-done | bytes 393248 | tf_op jit(solution)/shard_map/all_to_all | solution.py:428
  20.2 1.9 %collective-permute-start.1 = (bf16[32,256]{1,0:T(8,128)(2,1)S(1)}, bf16[32,256]{1,0:T(8,128)(2,1)S(1)}, u32[]{:S(2)}, u32[]{:S(2)}) collective-permute-start(bf16[32,256]{1,0:T(8,128)(2,1)S(1)} %get-tuple-element.50), channel_id=1, source_target_pairs={{0,16},{16,0},{1,17},{17,1},{2,18},{18,2},{3,19},{19,3},{4,20},{20... | collective-permute-start | bytes 49160 | tf_op jit(solution)/shard_map/ppermute | solution.py:408
  22.2 0.4 shard_map.80.lower
  22.6 0.4 collective-permute-done.1.got
  23.0 0.7 shard_map.81
  23.8 17.0 %all_to_all.20 = bf16[64,13,2,128]{3,2,1,0:T(2,128)(2,1)S(1)} all-to-all(bf16[64,13,2,128]{3,2,1,0:T(2,128)(2,1)S(1)} %bitcast.18), channel_id=1, replica_groups=mesh['x'=4,'core'=2,'z'=4,'y'=4] {'x','y','z'}, dimensions={0} | all-to-all | bytes 851968 | tf_op jit(solution)/shard_map/all_to_all | solution.py:413
  40.8 0.6 shard_map.82
  41.4 2.1 %collective-permute-start.2 = (f32[128,128]{1,0:T(8,128)S(1)}, f32[128,128]{1,0:T(8,128)S(1)}, u32[]{:S(2)}, u32[]{:S(2)}) collective-permute-start(f32[128,128]{1,0:T(8,128)S(1)} %get-tuple-element.58), channel_id=1, source_target_pairs={{0,16},{16,0},{1,17},{17,1},{2,18},{18,2},{3,19},{19,3},{4,20},{20... | collective-permute-start | bytes 196616 | tf_op jit(solution)/shard_map/ppermute | solution.py:408
  43.5 0.9 %collective-permute-done.2.got = f32[128,128]{1,0:T(8,128)S(1)} collective-permute-done((f32[128,128]{1,0:T(8,128)S(1)}, f32[128,128]{1,0:T(8,128)S(1)}, u32[]{:S(2)}, u32[]{:S(2)}) %collective-permute-start.2) | collective-permute-done | bytes 65568 | tf_op jit(solution)/shard_map/ppermute | solution.py:408
  44.4 0.9 %shard_map.83 = (bf16[1664,128]{1,0:T(8,128)(2,1)S(1)}, f32[32,128]{1,0:T(8,128)S(1)}, f32[32,128]{1,0:T(8,128)S(1)}, f32[2,128]{1,0:T(2,128)S(1)}, f32[96,128]{...) custom-call(f32[128,128]{1,0:T(8,128)S(1)} %get-tuple-element.57.keep, ...), custom_call_target="tpu_custom_call" | custom-call | tf_op jit(solution)/shard_map/pallas_call | solution.py:393
  45.3 15.5 %all_to_all.21 = bf16[64,13,2,128]{3,2,1,0:T(2,128)(2,1)S(1)} all-to-all(bf16[64,13,2,128]{3,2,1,0:T(2,128)(2,1)S(1)} %bitcast.17), channel_id=1, replica_groups=mesh['x'=4,'core'=2,'z'=4,'y'=4] {'x','y','z'}, dimensions={0} | all-to-all | bytes 851968 | tf_op jit(solution)/shard_map/all_to_all | solution.py:413
  61.1 2.1 %collective-permute-start.3 = (f32[128,128]{1,0:T(8,128)S(1)}, f32[128,128]{1,0:T(8,128)S(1)}, u32[]{:S(2)}, u32[]{:S(2)}) collective-permute-start(f32[128,128]{1,0:T(8,128)S(1)} %get-tuple-element.65), channel_id=1, source_target_pairs={{0,16},{16,0},{1,17},{17,1},{2,18},{18,2},{3,19},{19,3},{4,20},{20... | collective-permute-start | bytes 196616 | tf_op jit(solution)/shard_map/ppermute | solution.py:408
  63.2 0.9 %collective-permute-done.3.got = f32[128,128]{1,0:T(8,128)S(1)} collective-permute-done((f32[128,128]{1,0:T(8,128)S(1)}, f32[128,128]{1,0:T(8,128)S(1)}, u32[]{:S(2)}, u32[]{:S(2)}) %collective-permute-start.3) | collective-permute-done | bytes 65568 | tf_op jit(solution)/shard_map/ppermute | solution.py:408
  64.1 0.9 %shard_map.85 = (bf16[1664,128]{1,0:T(8,128)(2,1)S(1)}, f32[2,128]{1,0:T(2,128)S(1)}, f32[96,128]{1,0:T(8,128)S(1)}, f32[96,128]{1,0:T(8,128)S(1)}, f32[96,128]{...) custom-call(f32[128,128]{1,0:T(8,128)S(1)} %get-tuple-element.64.keep, ...), custom_call_target="tpu_custom_call" | custom-call | tf_op jit(solution)/shard_map/pallas_call | solution.py:393
  65.0 15.5 %all_to_all.22 = bf16[64,13,2,128]{3,2,1,0:T(2,128)(2,1)S(1)} all-to-all(bf16[64,13,2,128]{3,2,1,0:T(2,128)(2,1)S(1)} %bitcast.16), channel_id=1, replica_groups=mesh['x'=4,'core'=2,'z'=4,'y'=4] {'x','y','z'}, dimensions={0} | all-to-all | bytes 851968 | tf_op jit(solution)/shard_map/all_to_all | solution.py:413
  80.8 2.1 %collective-permute-start.4 = (f32[112,128]{1,0:T(8,128)S(1)}, f32[112,128]{1,0:T(8,128)S(1)}, u32[]{:S(2)}, u32[]{:S(2)}) collective-permute-start(f32[112,128]{1,0:T(8,128)S(1)} %shard_map.86.half), channel_id=1, source_target_pairs={{0,16},{16,0},{1,17},{17,1},{2,18},{18,2},{3,19},{19,3},{4,20},{20... | collective-permute-start | bytes 172040 | tf_op jit(solution)/shard_map/ppermute | solution.py:408
  82.9 0.9 %collective-permute-done.4.got = f32[112,128]{1,0:T(8,128)S(1)} collective-permute-done((f32[112,128]{1,0:T(8,128)S(1)}, f32[112,128]{1,0:T(8,128)S(1)}, u32[]{:S(2)}, u32[]{:S(2)}) %collective-permute-start.4) | collective-permute-done | bytes 57376 | tf_op jit(solution)/shard_map/ppermute | solution.py:408
  83.8 0.8 shard_map.87
  (5 shorter events, 0.8 us)
Async XLA Ops:
  2.2 17.8 %all-to-all-start = ((bf16[16,96,128]{2,1,0:T(8,128)(2,1)}), bf16[16,96,128]{2,1,0:T(8,128)(2,1)S(1)}, u32[]{:S(2)}, u32[]{:S(2)}) async-start(bf16[16,96,128]{2,1,0:T(8,128)(2,1)} %broadcast_in_dim.2), calls=%async_computation | async-start | bytes 786432 | tf_op jit(solution)/shard_map/all_to_all | solution.py:428
  10.8 5.2 %collective-permute-start = (s32[1,24]{1,0:T(1,128)}, s32[1,24]{1,0:T(1,128)S(1)}, u32[]{:S(2)}, u32[]{:S(2)}) collective-permute-start(s32[1,24]{1,0:T(1,128)} %idx_hbm.1), channel_id=1, source_target_pairs={{0,16},{16,0},{1,17},{17,1},{2,18},{18,2},{3,19},{19,3},{4,20},{20... | collective-permute-start | bytes 296 | tf_op jit(solution)/shard_map/ppermute | solution.py:408
  20.2 2.8 %collective-permute-start.1 = (bf16[32,256]{1,0:T(8,128)(2,1)S(1)}, bf16[32,256]{1,0:T(8,128)(2,1)S(1)}, u32[]{:S(2)}, u32[]{:S(2)}) collective-permute-start(bf16[32,256]{1,0:T(8,128)(2,1)S(1)} %get-tuple-element.50), channel_id=1, source_target_pairs={{0,16},{16,0},{1,17},{17,1},{2,18},{18,2},{3,19},{19,3},{4,20},{20... | collective-permute-start | bytes 49160 | tf_op jit(solution)/shard_map/ppermute | solution.py:408
  41.4 3.0 %collective-permute-start.2 = (f32[128,128]{1,0:T(8,128)S(1)}, f32[128,128]{1,0:T(8,128)S(1)}, u32[]{:S(2)}, u32[]{:S(2)}) collective-permute-start(f32[128,128]{1,0:T(8,128)S(1)} %get-tuple-element.58), channel_id=1, source_target_pairs={{0,16},{16,0},{1,17},{17,1},{2,18},{18,2},{3,19},{19,3},{4,20},{20... | collective-permute-start | bytes 196616 | tf_op jit(solution)/shard_map/ppermute | solution.py:408
  61.1 3.0 %collective-permute-start.3 = (f32[128,128]{1,0:T(8,128)S(1)}, f32[128,128]{1,0:T(8,128)S(1)}, u32[]{:S(2)}, u32[]{:S(2)}) collective-permute-start(f32[128,128]{1,0:T(8,128)S(1)} %get-tuple-element.65), channel_id=1, source_target_pairs={{0,16},{16,0},{1,17},{17,1},{2,18},{18,2},{3,19},{19,3},{4,20},{20... | collective-permute-start | bytes 196616 | tf_op jit(solution)/shard_map/ppermute | solution.py:408
  80.8 3.0 %collective-permute-start.4 = (f32[112,128]{1,0:T(8,128)S(1)}, f32[112,128]{1,0:T(8,128)S(1)}, u32[]{:S(2)}, u32[]{:S(2)}) collective-permute-start(f32[112,128]{1,0:T(8,128)S(1)} %shard_map.86.half), channel_id=1, source_target_pairs={{0,16},{16,0},{1,17},{17,1},{2,18},{18,2},{3,19},{19,3},{4,20},{20... | collective-permute-start | bytes 172040 | tf_op jit(solution)/shard_map/ppermute | solution.py:408

commit v15 on v13

--- a/solution.py
+++ b/solution.py
@@ -47,8 +47,8 @@
     rows = lax.broadcasted_iota(jnp.int32, (PAD, WIDTH), 0)
     exact = y.astype(BF16).astype(F32)
     columns = jnp.concatenate([exact] * (WIDTH // PAD), axis=0).T
-    half = PAD // 2
-    spread = [jnp.zeros((half, UPPER * WIDTH), F32) for group in range(2)]
+    half = PAD // 4
+    spread = [jnp.zeros((half, UPPER * WIDTH), F32) for group in range(4)]
     below = [jnp.zeros((PAD, WIDTH), F32) for band in range(LOWER)]
     for r in range(0, ROWS, 2):
         group = r // half

time: 85 us -> 85 us (level)
  no operation moved by 1% of the time
where the time goes in v15:
time: 85 us; the launch traced here: 84.5 us
  blocking collectives  48 us (56%)
  starting transfers between devices  17.9 us (21%)
  Pallas kernels  10.1 us (12%)
  waiting for transfers between devices  6.2 us (7%)
    all_to_all x3, blocking collectives, to_all(): near = lax.all_to_all(sent, ('x', 'y', 'z'), 0, 0, tiled=True)  48 us
    pallas_call x11, Pallas kernels, call(): pl.pallas_call(kernel, out_shape=[(pltpu.HBM if hbm_out else jax.ShapeDty...  10.1 us
    ppermute x5, starting transfers between devices, other_core(): return lax.ppermute(values, 'core', [(0, 1), (1, 0)])  9.29 us
    all_to_all x1, starting transfers between devices, shards(): near = lax.all_to_all(sent, ('z', 'y'), 0, 0, tiled=True)  8.6 us
    all_to_all x1, waiting for transfers between devices, shards(): near = lax.all_to_all(sent, ('z', 'y'), 0, 0, tiled=True)  3.11 us
    ppermute x5, waiting for transfers between devices, other_core(): return lax.ppermute(values, 'core', [(0, 1), (1, 0)])  3.1 us
  transfers between devices with their start and end apart: 6, of which 5 were waited for; matrix products, arithmetic and copies ran while one was open for 0% of the time, Pallas kernels for 6%

profile of v15, /device:TPU:1, one launch (start us, length us, event | category | flops | bytes accessed | tf_op | source)
XLA Modules:
  0.0 84.5 jit_solution(10281641044860069329)
XLA Ops:
  0.6 0.8 multiply_convert_fusion
  1.4 0.8 broadcast_in_dim.2
  2.2 8.6 %all-to-all-start = ((bf16[16,96,128]{2,1,0:T(8,128)(2,1)}), bf16[16,96,128]{2,1,0:T(8,128)(2,1)S(1)}, u32[]{:S(2)}, u32[]{:S(2)}) async-start(bf16[16,96,128]{2,1,0:T(8,128)(2,1)} %broadcast_in_dim.2), calls=%async_computation | async-start | bytes 786432 | tf_op jit(solution)/shard_map/all_to_all | solution.py:427
  10.8 1.0 %collective-permute-start = (s32[1,24]{1,0:T(1,128)}, s32[1,24]{1,0:T(1,128)S(1)}, u32[]{:S(2)}, u32[]{:S(2)}) collective-permute-start(s32[1,24]{1,0:T(1,128)} %idx_hbm.1), channel_id=1, source_target_pairs={{0,16},{16,0},{1,17},{17,1},{2,18},{18,2},{3,19},{19,3},{4,20},{20... | collective-permute-start | bytes 296 | tf_op jit(solution)/shard_map/ppermute | solution.py:407
  11.9 4.1 %shard_map.77.upper = bf16[24,128,384]{2,1,0:T(8,128)(2,1)S(1)} custom-call(s32[2,24]{1,0:T(2,128)} %bitcast.21, bf16[24,128,128]{2,1,0:T(8,128)(2,1)} %bitcast.20, bf16[24,3,128,128]{3,2,1,0:T(8,128)(2,1)} %bitcast.19), custom_call_target="tpu_custom_call" | custom-call | tf_op jit(solution)/shard_map/pallas_call | solution.py:392
  16.0 0.9 %shard_map.78 = (f32[96,128]{1,0:T(8,128)S(1)}, f32[96,128]{1,0:T(8,128)S(1)}, s32[160,128]{1,0:T(8,128)S(1)}, f32[2,128]{1,0:T(2,128)S(1)}, bf16[128,1664]{1,0:T(8,128)(2,1)S(1)}) custom-call(s32[1,24]{1,0:T(1,128)S(1)} %collective-permute-done.other_idx, f32[96,128]{1,0:T(8,128)} %rhs_hbm.1, f32[96,128]{1,0:T(8,128)} %diag_hbm.1, s32[1,24]{1,0:T(1,128)} %idx_hbm.1), custom_call_target="tpu_custom_call" | custom-call | tf_op jit(solution)/shard_map/pallas_call | solution.py:392
  16.9 3.1 %all-to-all-done = bf16[16,96,128]{2,1,0:T(8,128)(2,1)S(1)} async-done(((bf16[16,96,128]{2,1,0:T(8,128)(2,1)}), bf16[16,96,128]{2,1,0:T(8,128)(2,1)S(1)}, u32[]{:S(2)}, u32[]{:S(2)}) %all-to-all-start) | async-done | bytes 393248 | tf_op jit(solution)/shard_map/all_to_all | solution.py:427
  20.2 1.9 %collective-permute-start.1 = (bf16[32,256]{1,0:T(8,128)(2,1)S(1)}, bf16[32,256]{1,0:T(8,128)(2,1)S(1)}, u32[]{:S(2)}, u32[]{:S(2)}) collective-permute-start(bf16[32,256]{1,0:T(8,128)(2,1)S(1)} %get-tuple-element.47), channel_id=1, source_target_pairs={{0,16},{16,0},{1,17},{17,1},{2,18},{18,2},{3,19},{19,3},{4,20},{20... | collective-permute-start | bytes 49160 | tf_op jit(solution)/shard_map/ppermute | solution.py:407
  22.2 0.4 shard_map.80.lower
  22.6 0.4 collective-permute-done.1.got
  23.0 0.8 shard_map.81
  23.8 17.0 %all_to_all.20 = bf16[64,13,2,128]{3,2,1,0:T(2,128)(2,1)S(1)} all-to-all(bf16[64,13,2,128]{3,2,1,0:T(2,128)(2,1)S(1)} %bitcast.18), channel_id=1, replica_groups=mesh['x'=4,'core'=2,'z'=4,'y'=4] {'x','y','z'}, dimensions={0} | all-to-all | bytes 851968 | tf_op jit(solution)/shard_map/all_to_all | solution.py:412
  40.8 0.6 shard_map.82
  41.5 2.1 %collective-permute-start.2 = (f32[128,128]{1,0:T(8,128)S(1)}, f32[128,128]{1,0:T(8,128)S(1)}, u32[]{:S(2)}, u32[]{:S(2)}) collective-permute-start(f32[128,128]{1,0:T(8,128)S(1)} %get-tuple-element.55), channel_id=1, source_target_pairs={{0,16},{16,0},{1,17},{17,1},{2,18},{18,2},{3,19},{19,3},{4,20},{20... | collective-permute-start | bytes 196616 | tf_op jit(solution)/shard_map/ppermute | solution.py:407
  43.6 0.9 %collective-permute-done.2.got = f32[128,128]{1,0:T(8,128)S(1)} collective-permute-done((f32[128,128]{1,0:T(8,128)S(1)}, f32[128,128]{1,0:T(8,128)S(1)}, u32[]{:S(2)}, u32[]{:S(2)}) %collective-permute-start.2) | collective-permute-done | bytes 65568 | tf_op jit(solution)/shard_map/ppermute | solution.py:407
  44.5 0.9 %shard_map.83 = (bf16[1664,128]{1,0:T(8,128)(2,1)S(1)}, f32[32,128]{1,0:T(8,128)S(1)}, f32[32,128]{1,0:T(8,128)S(1)}, f32[2,128]{1,0:T(2,128)S(1)}, f32[96,128]{...) custom-call(f32[128,128]{1,0:T(8,128)S(1)} %get-tuple-element.54.keep, ...), custom_call_target="tpu_custom_call" | custom-call | tf_op jit(solution)/shard_map/pallas_call | solution.py:392
  45.3 15.5 %all_to_all.21 = bf16[64,13,2,128]{3,2,1,0:T(2,128)(2,1)S(1)} all-to-all(bf16[64,13,2,128]{3,2,1,0:T(2,128)(2,1)S(1)} %bitcast.17), channel_id=1, replica_groups=mesh['x'=4,'core'=2,'z'=4,'y'=4] {'x','y','z'}, dimensions={0} | all-to-all | bytes 851968 | tf_op jit(solution)/shard_map/all_to_all | solution.py:412
  61.1 2.1 %collective-permute-start.3 = (f32[128,128]{1,0:T(8,128)S(1)}, f32[128,128]{1,0:T(8,128)S(1)}, u32[]{:S(2)}, u32[]{:S(2)}) collective-permute-start(f32[128,128]{1,0:T(8,128)S(1)} %get-tuple-element.61), channel_id=1, source_target_pairs={{0,16},{16,0},{1,17},{17,1},{2,18},{18,2},{3,19},{19,3},{4,20},{20... | collective-permute-start | bytes 196616 | tf_op jit(solution)/shard_map/ppermute | solution.py:407
  63.2 0.9 %collective-permute-done.3.got = f32[128,128]{1,0:T(8,128)S(1)} collective-permute-done((f32[128,128]{1,0:T(8,128)S(1)}, f32[128,128]{1,0:T(8,128)S(1)}, u32[]{:S(2)}, u32[]{:S(2)}) %collective-permute-start.3) | collective-permute-done | bytes 65568 | tf_op jit(solution)/shard_map/ppermute | solution.py:407
  64.1 0.9 %shard_map.85 = (bf16[1664,128]{1,0:T(8,128)(2,1)S(1)}, f32[2,128]{1,0:T(2,128)S(1)}, f32[96,128]{1,0:T(8,128)S(1)}, f32[96,128]{1,0:T(8,128)S(1)}, f32[96,128]{...) custom-call(f32[128,128]{1,0:T(8,128)S(1)} %get-tuple-element.60.keep, ...), custom_call_target="tpu_custom_call" | custom-call | tf_op jit(solution)/shard_map/pallas_call | solution.py:392
  65.0 15.5 %all_to_all.22 = bf16[64,13,2,128]{3,2,1,0:T(2,128)(2,1)S(1)} all-to-all(bf16[64,13,2,128]{3,2,1,0:T(2,128)(2,1)S(1)} %bitcast.16), channel_id=1, replica_groups=mesh['x'=4,'core'=2,'z'=4,'y'=4] {'x','y','z'}, dimensions={0} | all-to-all | bytes 851968 | tf_op jit(solution)/shard_map/all_to_all | solution.py:412
  80.8 2.1 %collective-permute-start.4 = (f32[112,128]{1,0:T(8,128)S(1)}, f32[112,128]{1,0:T(8,128)S(1)}, u32[]{:S(2)}, u32[]{:S(2)}) collective-permute-start(f32[112,128]{1,0:T(8,128)S(1)} %shard_map.86.half), channel_id=1, source_target_pairs={{0,16},{16,0},{1,17},{17,1},{2,18},{18,2},{3,19},{19,3},{4,20},{20... | collective-permute-start | bytes 172040 | tf_op jit(solution)/shard_map/ppermute | solution.py:407
  82.9 0.9 %collective-permute-done.4.got = f32[112,128]{1,0:T(8,128)S(1)} collective-permute-done((f32[112,128]{1,0:T(8,128)S(1)}, f32[112,128]{1,0:T(8,128)S(1)}, u32[]{:S(2)}, u32[]{:S(2)}) %collective-permute-start.4) | collective-permute-done | bytes 57376 | tf_op jit(solution)/shard_map/ppermute | solution.py:407
  83.8 0.8 shard_map.87
  (5 shorter events, 0.8 us)
Async XLA Ops:
  2.2 17.8 %all-to-all-start = ((bf16[16,96,128]{2,1,0:T(8,128)(2,1)}), bf16[16,96,128]{2,1,0:T(8,128)(2,1)S(1)}, u32[]{:S(2)}, u32[]{:S(2)}) async-start(bf16[16,96,128]{2,1,0:T(8,128)(2,1)} %broadcast_in_dim.2), calls=%async_computation | async-start | bytes 786432 | tf_op jit(solution)/shard_map/all_to_all | solution.py:427
  10.8 5.2 %collective-permute-start = (s32[1,24]{1,0:T(1,128)}, s32[1,24]{1,0:T(1,128)S(1)}, u32[]{:S(2)}, u32[]{:S(2)}) collective-permute-start(s32[1,24]{1,0:T(1,128)} %idx_hbm.1), channel_id=1, source_target_pairs={{0,16},{16,0},{1,17},{17,1},{2,18},{18,2},{3,19},{19,3},{4,20},{20... | collective-permute-start | bytes 296 | tf_op jit(solution)/shard_map/ppermute | solution.py:407
  20.2 2.8 %collective-permute-start.1 = (bf16[32,256]{1,0:T(8,128)(2,1)S(1)}, bf16[32,256]{1,0:T(8,128)(2,1)S(1)}, u32[]{:S(2)}, u32[]{:S(2)}) collective-permute-start(bf16[32,256]{1,0:T(8,128)(2,1)S(1)} %get-tuple-element.47), channel_id=1, source_target_pairs={{0,16},{16,0},{1,17},{17,1},{2,18},{18,2},{3,19},{19,3},{4,20},{20... | collective-permute-start | bytes 49160 | tf_op jit(solution)/shard_map/ppermute | solution.py:407
  41.5 3.0 %collective-permute-start.2 = (f32[128,128]{1,0:T(8,128)S(1)}, f32[128,128]{1,0:T(8,128)S(1)}, u32[]{:S(2)}, u32[]{:S(2)}) collective-permute-start(f32[128,128]{1,0:T(8,128)S(1)} %get-tuple-element.55), channel_id=1, source_target_pairs={{0,16},{16,0},{1,17},{17,1},{2,18},{18,2},{3,19},{19,3},{4,20},{20... | collective-permute-start | bytes 196616 | tf_op jit(solution)/shard_map/ppermute | solution.py:407
  61.1 3.0 %collective-permute-start.3 = (f32[128,128]{1,0:T(8,128)S(1)}, f32[128,128]{1,0:T(8,128)S(1)}, u32[]{:S(2)}, u32[]{:S(2)}) collective-permute-start(f32[128,128]{1,0:T(8,128)S(1)} %get-tuple-element.61), channel_id=1, source_target_pairs={{0,16},{16,0},{1,17},{17,1},{2,18},{18,2},{3,19},{19,3},{4,20},{20... | collective-permute-start | bytes 196616 | tf_op jit(solution)/shard_map/ppermute | solution.py:407
  80.8 3.0 %collective-permute-start.4 = (f32[112,128]{1,0:T(8,128)S(1)}, f32[112,128]{1,0:T(8,128)S(1)}, u32[]{:S(2)}, u32[]{:S(2)}) collective-permute-start(f32[112,128]{1,0:T(8,128)S(1)} %shard_map.86.half), channel_id=1, source_target_pairs={{0,16},{16,0},{1,17},{17,1},{2,18},{18,2},{3,19},{19,3},{4,20},{20... | collective-permute-start | bytes 172040 | tf_op jit(solution)/shard_map/ppermute | solution.py:407
